TPU v7x, 512 devices: a whole 4x4x16 slice. The times are simulated.
512 devices in a mesh: rep: 8 (over x, core), grp: 8 (over y, z_hi), sub: 8 (over z_lo).
Axes of the slice: x: 4, y: 4, z: 16 (z_hi: 2, z_lo: 8; z = z_hi * 8 + z_lo), core: 2. Of those that a mesh axis runs over, the one named last changes fastest.
Arguments:
- table_rows: bfloat16 [48, 2048, 128], P('grp', 'sub'), may hold values from -3 to 3
- bag_rows: int32 [8192, 48, 8], P('rep', 'grp'), may hold values from 0 to 2047
- bag_lens: int32 [8192, 48], P('rep', 'grp'), may hold values from 1 to 8, 192 in all within a row
- labels: float32 [8192], P(('rep', 'grp', 'sub')), may hold values from 0 to 1
- proj: bfloat16 [2, 48, 8], replicated, may hold values from -0.875 to 0.875
- mlp_in: bfloat16 [2, 384, 384], replicated, may hold values from -0.3125 to 0.3125
- mlp_out: bfloat16 [2, 384, 1536], replicated, may hold values from -0.3125 to 0.3125
- compress: bfloat16 [2, 36, 48], replicated, may hold values from -0.875 to 0.875
- gain_fm: float32 [2, 384], replicated, may hold values from 0.25 to 1.75
- gain_out: float32 [2, 128], replicated, may hold values from 0.25 to 1.75
- head: bfloat16 [48, 128], replicated, may hold values from -0.078125 to 0.078125
Outputs:
- example_loss: float32 [8192], P(('rep', 'grp', 'sub'))
- row_grads: float32 [48, 2048, 128], P('grp', 'sub')
Inputs may be any that keep to these rules, and one draw needn't show every extreme that they name: `bag_lens`: the bag sizes of one example over its 48 tables sum to 192.
All inputs are finite; a program needn't handle non-finite values. No bound on the sum of `bag_lens` on one device may be relied on, other than what follows from the above.
Results may differ from a plain program's by a relative error of at most 0.022.
Values may be sent and summed in bfloat16 or wider, within the bound.
No kernel may reach another device: no remote copies, remote signals or barrier semaphores. Data moves between devices by JAX's collectives and lax.ppermute only.
A program may use at most 64 MiB of HBM per device.

v0:
```python
import jax
import jax.numpy as jnp
from jax import lax
from jax.sharding import PartitionSpec as P


def layer_norm(values, gain):
    center = jnp.mean(values, axis=-1, keepdims=True)
    spread = jnp.mean(jnp.square(values - center), axis=-1, keepdims=True)
    return (values - center) * lax.rsqrt(spread + 1e-05) * gain


def wukong_layer(features, proj, mlp_in, mlp_out, compress, gain_fm, gain_out):
    batch, fields, width = features.shape
    wide = features.astype(jnp.float32)
    summary = jnp.einsum(
        "bne,nk->bke", wide, proj.astype(jnp.float32), precision=lax.Precision.HIGHEST
    ).astype(jnp.bfloat16)
    pairwise = jnp.einsum(
        "bne,bke->bnk", wide, summary.astype(jnp.float32), precision=lax.Precision.HIGHEST
    )
    normed = layer_norm(pairwise.reshape(batch, -1), gain_fm).astype(jnp.bfloat16)
    hidden = jax.nn.silu(jnp.dot(normed, mlp_in, preferred_element_type=jnp.float32)).astype(
        jnp.bfloat16
    )
    machine = jnp.dot(hidden, mlp_out, preferred_element_type=jnp.float32).reshape(batch, -1, width)
    linear = jnp.einsum(
        "ln,bne->ble", compress.astype(jnp.float32), wide, precision=lax.Precision.HIGHEST
    )
    total = jnp.concatenate([machine, linear], axis=1) + wide
    return layer_norm(total, gain_out).astype(jnp.bfloat16)


def example_losses(features, labels, proj, mlp_in, mlp_out, compress, gain_fm, gain_out, head):
    for layer in range(proj.shape[0]):
        features = wukong_layer(
            features,
            proj[layer],
            mlp_in[layer],
            mlp_out[layer],
            compress[layer],
            gain_fm[layer],
            gain_out[layer],
        )
    logit = jnp.sum(features.astype(jnp.float32) * head.astype(jnp.float32), axis=(1, 2))
    return jax.nn.softplus(logit) - labels * logit


def slot_counts(bag_rows, bag_lens, lowest, rows_dev):
    ex_rep, tab_dev, bag_size = bag_rows.shape
    row_ids = jnp.arange(rows_dev, dtype=jnp.int32)
    slot_ids = jnp.arange(bag_size, dtype=jnp.int32)
    local_rows = jnp.transpose(bag_rows, (1, 0, 2)) - lowest
    live = jnp.transpose(bag_lens)[:, :, None] > slot_ids[None, None, :]
    match = (local_rows[:, :, :, None] == row_ids[None, None, None, :]) & live[:, :, :, None]
    return jnp.sum(match.astype(jnp.bfloat16), axis=2, dtype=jnp.bfloat16)


def per_device(
    table_rows, bag_rows, bag_lens, labels, proj, mlp_in, mlp_out, compress, gain_fm, gain_out, head
):
    tab_dev, rows_dev, width = table_rows.shape
    ex_rep, _, bag_size = bag_rows.shape
    groups = lax.axis_size("grp")
    shards = lax.axis_size("sub")
    ex_dev = ex_rep // (groups * shards)
    lowest = lax.axis_index("sub") * rows_dev
    counts = slot_counts(bag_rows, bag_lens, lowest, rows_dev)
    partial_value = jnp.einsum(
        "ter,trd->etd", counts, table_rows, preferred_element_type=jnp.float32
    ).astype(jnp.bfloat16)
    moved = lax.all_to_all(
        partial_value.reshape(ex_rep, 1, tab_dev, width),
        ("grp", "sub"),
        split_axis=0,
        concat_axis=1,
        tiled=True,
    )
    summed = jnp.sum(
        moved.reshape(ex_dev, groups, shards, tab_dev, width).astype(jnp.float32), axis=2
    )
    features = summed.reshape(ex_dev, groups * tab_dev, width).astype(jnp.bfloat16)

    def forward(values):
        return example_losses(
            values, labels, proj, mlp_in, mlp_out, compress, gain_fm, gain_out, head
        )

    losses, pull_back = jax.vjp(forward, features)
    feature_grads = pull_back(jnp.ones_like(losses))[0]
    spread_out = jnp.broadcast_to(
        feature_grads.reshape(ex_dev, groups, 1, tab_dev, width),
        (ex_dev, groups, shards, tab_dev, width),
    )
    returned = lax.all_to_all(
        spread_out.reshape(ex_dev, groups * shards, tab_dev, width),
        ("grp", "sub"),
        split_axis=1,
        concat_axis=0,
        tiled=True,
    )
    local_grads = returned.reshape(ex_rep, tab_dev, width)
    accum = jnp.einsum("ter,etd->trd", counts, local_grads, preferred_element_type=jnp.float32)
    row_grads = lax.psum(accum.astype(jnp.bfloat16), "rep").astype(jnp.float32)
    return (losses, row_grads)


def solution(mesh):
    return jax.shard_map(
        per_device,
        mesh=mesh,
        in_specs=(
            P("grp", "sub", None),
            P("rep", "grp", None),
            P("rep", "grp"),
            P(("rep", "grp", "sub")),
            P(),
            P(),
            P(),
            P(),
            P(),
            P(),
            P(),
        ),
        out_specs=(P(("rep", "grp", "sub")), P("grp", "sub", None)),
        check_vma=False,
    )
```

profile of v0, /device:TPU:1, one launch (start us, length us, event | category | flops | bytes accessed | tf_op | source)
XLA Modules:
  0.0 361.7 jit_solution(9066653383764333586)
XLA Ops:
  7.2 1.7 subtract_bitcast_fusion
  8.9 1.9 copy.115
  10.7 1.4 iota_compare_fusion.1
  12.1 2.5 copy.116
  14.6 37.8 %fusion.2 = bf16[6,1024,256]{2,1,0:T(8,128)(2,1)S(1)} fusion(s32[6,1024,8]{2,1,0:T(8,128)S(1)} %copy.115, pred[6,1024,8]{2,1,0:T(8,128)(4,1)} %copy.116), kind=kLoop, calls=%fused_computation.3 | loop fusion | flops 48758784 | bytes 3391488 | tf_op jit(solution)/shard_map/reduce_sum | solution.py:56
  52.4 1.0 fusion.3
  53.4 0.7 copy-done.1
  54.1 2.5 copy.117
  56.5 19.4 %all-to-all-start = ((bf16[1024,1,6,128]{3,2,1,0:T(8,128)(2,1)}), bf16[1024,1,6,128]{3,2,1,0:T(8,128)(2,1)S(1)}, u32[]{:S(2)}, u32[]{:S(2)}) async-start(bf16[1024,1,6,128]{3,2,1,0:T(8,128)(2,1)} %copy.117), calls=%async_computation | async-start | bytes 4194304 | tf_op jit(solution)/shard_map/all_to_all | solution.py:72
  76.4 3.2 slice_bitcast_fusion
  79.6 2.4 copy.124
  82.2 2.4 copy.139
  84.7 86.0 %all-to-all-done = bf16[1024,1,6,128]{3,2,1,0:T(8,128)(2,1)S(1)} async-done(((bf16[1024,1,6,128]{3,2,1,0:T(8,128)(2,1)}), bf16[1024,1,6,128]{3,2,1,0:T(8,128)(2,1)S(1)}, u32[]{:S(2)}, u32[]{:S(2)}) %all-to-all-start) | async-done | bytes 1572896 | tf_op jit(solution)/shard_map/all_to_all | solution.py:72
  170.7 0.5 reduce.39
  172.4 1.1 fusion.46
  173.5 1.7 fusion.93
  176.9 0.5 fusion.118
  178.1 1.1 fusion.43
  181.4 0.5 exponential_add_fusion
  182.0 0.5 fusion.41
  183.2 0.8 add_add_fusion.1
  184.4 2.2 multiply_reduce_fusion.15
  187.3 0.5 fusion.16
  188.1 0.8 multiply_reduce_fusion.7
  189.7 0.5 add_add_fusion
  190.7 2.1 multiply_reduce_fusion.14
  194.0 0.5 fusion.12
  194.9 81.1 %all_to_all.24 = bf16[16,64,6,128]{3,0,2,1:T(8,128)(2,1)S(1)} all-to-all(bf16[16,64,6,128]{3,0,2,1:T(8,128)(2,1)S(1)} %bitcast.196), channel_id=1, replica_groups=mesh['rep'=8,'grp'=8,'sub'=8] {'grp','sub'}, dimensions={1} | all-to-all | bytes 3145728 | tf_op jit(solution)/shard_map/all_to_all | solution.py:95
  276.2 1.6 copy-done.2
  277.8 1.9 convolution_convert_fusion.1
  279.8 73.1 %all-reduce.2.cloned.1.call-done = bf16[6,256,128]{2,1,0:T(8,128)(2,1)} async-done(((bf16[6,256,128]{2,1,0:T(8,128)(2,1)}), bf16[6,256,128]{2,1,0:T(8,128)(2,1)}) %all-reduce.2.cloned.1.call-update) | async-done | bytes 393232 | tf_op jit(solution)/shard_map/psum | solution.py:104
  352.9 1.9 convert_element_type.362
  (115 shorter events, 11.1 us)
Async XLA Ops:
  7.2 45.2 %copy-start = (bf16[6,256,128]{2,1,0:T(8,128)(2,1)S(1)}, bf16[6,256,128]{2,1,0:T(8,128)(2,1)}, u32[]{:S(2)}) copy-start(bf16[6,256,128]{2,1,0:T(8,128)(2,1)} %param.11) | copy-start | bytes 1179652
  52.4 1.7 copy-start.1
  56.5 19.7 %copy-start.8 = (f32[2,384]{1,0:T(2,128)S(1)}, f32[2,384]{1,0:T(2,128)}, u32[]{:S(2)}) copy-start(f32[2,384]{1,0:T(2,128)} %param.19) | copy-start | bytes 9220
  56.5 114.2 %all-to-all-start = ((bf16[1024,1,6,128]{3,2,1,0:T(8,128)(2,1)}), bf16[1024,1,6,128]{3,2,1,0:T(8,128)(2,1)S(1)}, u32[]{:S(2)}, u32[]{:S(2)}) async-start(bf16[1024,1,6,128]{3,2,1,0:T(8,128)(2,1)} %copy.117), calls=%async_computation | async-start | bytes 4194304 | tf_op jit(solution)/shard_map/all_to_all | solution.py:72
  75.9 276.9 %all-reduce.2.cloned.1.call-start = ((), (), s32[]{:S(2)}) async-start(), calls=%async_computation.2 | async-start | bytes 786432 | tf_op jit(solution)/shard_map/psum | solution.py:104
  79.6 5.0 %copy-start.6 = (bf16[48,128]{1,0:T(8,128)(2,1)S(1)}, bf16[48,128]{1,0:T(8,128)(2,1)}, u32[]{:S(2)}) copy-start(bf16[48,128]{1,0:T(8,128)(2,1)} %param.21) | copy-start | bytes 36868
  79.6 5.0 %copy-start.9 = (f32[2,128]{1,0:T(2,128)S(1)}, f32[2,128]{1,0:T(2,128)}, u32[]{:S(2)}) copy-start(f32[2,128]{1,0:T(2,128)} %param.20) | copy-start | bytes 3076
  79.6 5.1 %copy-start.5 = (bf16[2,36,48]{2,0,1:T(2,128)(2,1)S(1)}, bf16[2,36,48]{2,0,1:T(2,128)(2,1)}, u32[]{:S(2)}) copy-start(bf16[2,36,48]{2,0,1:T(2,128)(2,1)} %param.18) | copy-start | bytes 20740
  82.2 89.1 %copy-start.7 = (bf16[2,48,8]{1,2,0:T(8,128)(2,1)S(1)}, bf16[2,48,8]{1,2,0:T(8,128)(2,1)}, u32[]{:S(2)}) copy-start(bf16[2,48,8]{1,2,0:T(8,128)(2,1)} %param.15) | copy-start | bytes 4612
  176.1 3.2 copy-start.3
  179.3 2.2 copy-start.10
  188.1 2.6 copy-start.4
  275.9 1.9 copy-start.2
Sparse Core Ops, SparseCore 0:
  279.9 72.9 all-reduce.1
where the time goes:
time: 363 us; the launch traced here: 362 us
  waiting for transfers between devices  159 us (44%)
  blocking collectives  81.1 us (22%)
  other arithmetic  50.3 us (14%)
  local copies, waits for them, and re-layouts  20.5 us (6%)
  starting transfers between devices  19.6 us (5%)
  matrix products  16.4 us (5%)
  between operations  14.6 us (4%)
    all_to_all x1, waiting for transfers between devices, per_device(): lax.all_to_all(partial_value.reshape(ex_rep, 1, tab_dev, width), ('grp',...  86 us
    all_to_all x1, blocking collectives, per_device(): lax.all_to_all(spread_out.reshape(ex_dev, groups * shards, tab_dev, width...  81.1 us
    psum x1, waiting for transfers between devices, per_device(): row_grads = lax.psum(accum.astype(jnp.bfloat16), 'rep').astype(jnp.float32)  73.1 us
    reduce_sum x1, other arithmetic, slot_counts(): return jnp.sum(match.astype(jnp.bfloat16), axis=2, dtype=jnp.bfloat16)  37.8 us
    all_to_all x1, starting transfers between devices, per_device(): lax.all_to_all(partial_value.reshape(ex_rep, 1, tab_dev, width), ('grp',...  19.4 us
    dot_general x5, local copies, waits for them, and re-layouts, wukong_layer(): jnp.dot(hidden, mlp_out, preferred_element_type=jnp.float32)  8.2 us
  transfers between devices with their start and end apart: 2, of which 2 were waited for; matrix products, arithmetic and copies ran while one was open for 2% of the time, Pallas kernels for 0%

commit v1 on v0

v1 whole, which is shorter than its diff:
```python
import functools

import jax
import jax.numpy as jnp
from jax import lax
from jax.experimental import pallas as pl
from jax.experimental.pallas import tpu as pltpu
from jax.sharding import Mesh
from jax.sharding import PartitionSpec as P

REP = ("x", "core")
GRP = ("y", "zhi")
DEAD = 4095


def layer_norm(values, gain):
    center = jnp.mean(values, axis=-1, keepdims=True)
    spread = jnp.mean(jnp.square(values - center), axis=-1, keepdims=True)
    return (values - center) * lax.rsqrt(spread + 1e-05) * gain


def wukong_layer(features, proj, mlp_in, mlp_out, compress, gain_fm, gain_out):
    batch, fields, width = features.shape
    wide = features.astype(jnp.float32)
    summary = jnp.einsum(
        "bne,nk->bke", wide, proj.astype(jnp.float32), precision=lax.Precision.HIGHEST
    ).astype(jnp.bfloat16)
    pairwise = jnp.einsum(
        "bne,bke->bnk", wide, summary.astype(jnp.float32), precision=lax.Precision.HIGHEST
    )
    normed = layer_norm(pairwise.reshape(batch, -1), gain_fm).astype(jnp.bfloat16)
    hidden = jax.nn.silu(jnp.dot(normed, mlp_in, preferred_element_type=jnp.float32)).astype(
        jnp.bfloat16
    )
    machine = jnp.dot(hidden, mlp_out, preferred_element_type=jnp.float32).reshape(batch, -1, width)
    linear = jnp.einsum(
        "ln,bne->ble", compress.astype(jnp.float32), wide, precision=lax.Precision.HIGHEST
    )
    total = jnp.concatenate([machine, linear], axis=1) + wide
    return layer_norm(total, gain_out).astype(jnp.bfloat16)


def example_losses(features, labels, proj, mlp_in, mlp_out, compress, gain_fm, gain_out, head):
    for layer in range(proj.shape[0]):
        features = wukong_layer(
            features,
            proj[layer],
            mlp_in[layer],
            mlp_out[layer],
            compress[layer],
            gain_fm[layer],
            gain_out[layer],
        )
    logit = jnp.sum(features.astype(jnp.float32) * head.astype(jnp.float32), axis=(1, 2))
    return jax.nn.softplus(logit) - labels * logit


def pick_kernel(sub_ref, rows_ref, lens_ref, out_ref):
    tables, bag, _ = rows_ref.shape
    slots = lax.broadcasted_iota(jnp.int32, (bag, 128), 0)
    lanes = lax.broadcasted_iota(jnp.int32, (bag, 128), 1)
    sub = sub_ref[0]
    for table in range(tables):
        kept = jnp.zeros((bag, 128), jnp.int32)
        for run in range(8):
            cut = slice(run * 128, run * 128 + 128)
            coded = jnp.where(
                slots < lens_ref[table : table + 1, cut], rows_ref[table, :, cut], DEAD
            )
            moved = pltpu.roll(coded, (run * 16 - sub * 16) & 127, 1)
            kept = jnp.where(lanes // 16 == run, moved, kept)
        out_ref[pl.ds(table * bag, bag), :] = kept


def pool_kernel(rep_ref, bags_ref, tab_ref, pools_ref, counts_ref, idx_ref):
    reps, coded_rows, _ = bags_ref.shape
    shards, tables, rows, width = tab_ref.shape
    local = shards * rows
    rep = rep_ref[0]
    for src in range(reps):
        coded = bags_ref[src]
        mine = ((coded >> 5) & 7) == rep
        spot = ((coded >> 8) << 5) | (coded & 31)
        idx_ref[:, src * 128 : src * 128 + 128] = jnp.where(mine, spot, 1024).astype(jnp.float32)
    ids = [
        (lax.broadcasted_iota(jnp.int32, (16, 128), 0) + 16 * i).astype(jnp.float32).astype(jnp.bfloat16)
        for i in range(local // 16)
    ]
    one = jnp.ones((16, 128), jnp.bfloat16)
    zero = jnp.zeros((16, 128), jnp.bfloat16)

    def per_table(table, carry):
        for src in range(reps):
            cut = slice(src * 128, src * 128 + 128)
            slots = idx_ref[pl.ds(pl.multiple_of(table * 8, 8), 8), cut]
            keys = [
                jnp.broadcast_to(slots[b : b + 1], (16, 128)).astype(jnp.bfloat16) for b in range(8)
            ]
            for i in range(local // 16):
                hits = [jnp.where(keys[b] == ids[i], one, zero) for b in range(8)]
                while len(hits) > 1:
                    hits = [hits[k] + hits[k + 1] for k in range(0, len(hits), 2)]
                counts_ref[table, i * 16 : i * 16 + 16, cut] = hits[0]
        part = lax.dot_general(
            counts_ref[table],
            tab_ref[:, table].reshape(local, width),
            (((0,), (0,)), ((), ())),
            preferred_element_type=jnp.float32,
        )
        pools_ref[:, table] = part.astype(jnp.bfloat16).reshape(32, 32, width)
        return carry

    lax.fori_loop(0, tables, per_table, 0)


def grads_kernel(counts_ref, moved_ref, out_ref):
    tables, local, examples = counts_ref.shape
    shards, _, rows, width = out_ref.shape

    def per_table(table, carry):
        grads = moved_ref[:, table].reshape(examples, width)
        acc = jnp.dot(counts_ref[table], grads, preferred_element_type=jnp.float32)
        out_ref[:, table] = acc.astype(jnp.bfloat16).reshape(shards, rows, width)
        return carry

    lax.fori_loop(0, tables, per_table, 0)


def swap(values, axes):
    return lax.all_to_all(values, axes, split_axis=0, concat_axis=0, tiled=True)


def per_device(
    table_rows, bag_rows, bag_lens, labels, proj, mlp_in, mlp_out, compress, gain_fm, gain_out, head
):
    tables, rows_dev, width = table_rows.shape
    vmem = pl.BlockSpec(memory_space=pltpu.VMEM)
    smem = pl.BlockSpec(memory_space=pltpu.SMEM)
    params = pltpu.CompilerParams(vmem_limit_bytes=48 * 1024 * 1024)
    sub = lax.axis_index("sub")
    rep = lax.axis_index(REP)
    reps, subs, ys, zs = 8, 8, 4, 2
    part_rows = rows_dev // reps

    coded = pl.pallas_call(
        pick_kernel,
        out_shape=jax.ShapeDtypeStruct((tables * 8, 128), jnp.int32),
        in_specs=[smem, vmem, vmem],
        out_specs=vmem,
        compiler_params=params,
    )(sub.reshape(1), jnp.transpose(bag_rows, (1, 2, 0)), jnp.transpose(bag_lens))
    bags = swap(jnp.broadcast_to(coded, (reps, tables * 8, 128)), REP)

    part = lax.dynamic_slice_in_dim(table_rows, rep * part_rows, part_rows, axis=1)
    gathered = swap(jnp.broadcast_to(part, (subs, tables, part_rows, width)), "sub")

    pools, counts = pl.pallas_call(
        pool_kernel,
        out_shape=(
            jax.ShapeDtypeStruct((reps * ys, tables, 32, width), jnp.bfloat16),
            jax.ShapeDtypeStruct((tables, rows_dev, 1024), jnp.bfloat16),
        ),
        in_specs=[smem, vmem, vmem],
        out_specs=(vmem, vmem),
        scratch_shapes=[pltpu.VMEM((tables * 8, 1024), jnp.float32)],
        compiler_params=params,
    )(rep.reshape(1), bags, gathered)

    moved = swap(pools, REP + ("y",))
    summed = jnp.sum(
        moved.reshape(reps, ys, tables, zs, 16, width).astype(jnp.float32), axis=0
    ).astype(jnp.bfloat16)
    near = swap(jnp.transpose(summed, (2, 0, 1, 3, 4)), "zhi")
    features = jnp.transpose(near, (3, 1, 0, 2, 4)).reshape(16, ys * zs * tables, width)

    def forward(values):
        return example_losses(
            values, labels, proj, mlp_in, mlp_out, compress, gain_fm, gain_out, head
        )

    losses, pull_back = jax.vjp(forward, features)
    feature_grads = pull_back(jnp.ones_like(losses))[0]

    back = jnp.transpose(feature_grads.reshape(16, ys, zs, tables, width), (2, 1, 3, 0, 4))
    back = swap(back, "zhi")
    back = jnp.transpose(back, (1, 2, 0, 3, 4)).reshape(ys, tables, 32, width)
    returned = swap(
        jnp.broadcast_to(back, (reps, ys, tables, 32, width)).reshape(
            reps * ys, tables, 32, width
        ),
        REP + ("y",),
    )
    partial = pl.pallas_call(
        grads_kernel,
        out_shape=jax.ShapeDtypeStruct((subs, tables, part_rows, width), jnp.bfloat16),
        in_specs=[vmem, vmem],
        out_specs=vmem,
        compiler_params=params,
    )(counts, returned)
    pieces = swap(partial, "sub")
    own = jnp.sum(pieces.astype(jnp.float32), axis=0).astype(jnp.bfloat16)
    spread = swap(jnp.broadcast_to(own, (reps, tables, part_rows, width)), REP)
    row_grads = jnp.transpose(spread, (1, 0, 2, 3)).reshape(tables, rows_dev, width)
    return (losses, row_grads.astype(jnp.float32))


def solution(mesh):
    view = Mesh(mesh.devices.reshape(4, 2, 4, 2, 8), ("x", "core", "y", "zhi", "sub"))
    return jax.shard_map(
        per_device,
        mesh=view,
        in_specs=(
            P(GRP, "sub", None),
            P(REP, GRP, None),
            P(REP, GRP),
            P(REP + GRP + ("sub",)),
            P(),
            P(),
            P(),
            P(),
            P(),
            P(),
            P(),
        ),
        out_specs=(P(REP + GRP + ("sub",)), P(GRP, "sub", None)),
        check_vma=False,
    )
```

time: 363 us -> 310 us (0.85)
  waiting for transfers between devices: 159 us -> 25.3 us
  local copies, waits for them, and re-layouts: 20.5 us -> 68.7 us
  blocking collectives: 81.1 us -> 115 us
  other arithmetic: 50.3 us -> 36 us
  between operations: 14.6 us -> 1.28 us
  matrix products: 16.4 us -> 25.1 us
  starting transfers between devices: 19.6 us -> 27.7 us
  Pallas kernels: 0 us -> 6.85 us
    psum x1 -> x0, waiting for transfers between devices: 73.1 us -> none  [per_device(): row_grads = lax.psum(accum.astype(jnp.bfloat16), 'rep').astype(jnp.float32)]
    all_to_all x1 -> x3, waiting for transfers between devices: 86 us -> 25.3 us  [swap(): return lax.all_to_all(values, axes, split_axis=0, concat_axis=0, tiled=True)]
    reduce_sum x1 -> x2, other arithmetic: 37.8 us -> 2.42 us  [the longest x1 2.36 us: per_device(): jnp.sum(moved.reshape(reps, ys, tables, zs, 16, width).astype(jnp.float32...]
    all_to_all x1 -> x5, blocking collectives: 81.1 us -> 115 us  [swap(): return lax.all_to_all(values, axes, split_axis=0, concat_axis=0, tiled=True)]
    unnamed x22 -> x112, local copies, waits for them, and re-layouts: 2.32 us -> 12.1 us
    all_to_all x1 -> x3, starting transfers between devices: 19.4 us -> 27.7 us  [swap(): return lax.all_to_all(values, axes, split_axis=0, concat_axis=0, tiled=True)]
    pallas_call x0 -> x3, Pallas kernels: none -> 6.85 us  [the longest x1 5.02 us: per_device(): pl.pallas_call(pool_kernel, out_shape=(jax.ShapeDtypeStruct((reps * ys, t...]
    reshape x4, local copies, waits for them, and re-layouts: 0.41 us -> 6.59 us  [wukong_layer(): pairwise.reshape(batch, -1)]
  transfers between devices with their start and end apart: 2 -> 3, of which waited for: 2 -> 3; matrix products, arithmetic and copies ran while one was open for 2% -> 5% of each run, Pallas kernels for 0% -> 0%
where the time goes in v1:
time: 310 us; the launch traced here: 306 us
  blocking collectives  115 us (37%)
  local copies, waits for them, and re-layouts  68.7 us (22%)
  other arithmetic  36 us (12%)
  starting transfers between devices  27.7 us (9%)
  waiting for transfers between devices  25.3 us (8%)
  matrix products  25.1 us (8%)
  Pallas kernels  6.85 us (2%)
    all_to_all x5, blocking collectives, swap(): return lax.all_to_all(values, axes, split_axis=0, concat_axis=0, tiled=True)  115 us
    all_to_all x3, starting transfers between devices, swap(): return lax.all_to_all(values, axes, split_axis=0, concat_axis=0, tiled=True)  27.7 us
    all_to_all x3, waiting for transfers between devices, swap(): return lax.all_to_all(values, axes, split_axis=0, concat_axis=0, tiled=True)  25.3 us
    unnamed x112, local copies, waits for them, and re-layouts  12.1 us
    dot_general x4, matrix products, wukong_layer(): jnp.dot(normed, mlp_in, preferred_element_type=jnp.float32)  9.16 us
    dot_general x5, local copies, waits for them, and re-layouts, wukong_layer(): jnp.dot(hidden, mlp_out, preferred_element_type=jnp.float32)  8.07 us
    dot_general x6, matrix products, wukong_layer(): jnp.einsum('bne,bke->bnk', wide, summary.astype(jnp.float32), precision=l...  7.84 us
    reduce_sum x8, other arithmetic, layer_norm(): spread = jnp.mean(jnp.square(values - center), axis=-1, keepdims=True)  7.52 us
  transfers between devices with their start and end apart: 3, of which 3 were waited for; matrix products, arithmetic and copies ran while one was open for 5% of the time, Pallas kernels for 0%

profile of v1, /device:TPU:1, one launch (start us, length us, event | category | flops | bytes accessed | tf_op | source)
XLA Modules:
  0.0 306.5 jit_solution(1689735223648233096)
XLA Ops:
  3.2 10.2 %all-to-all-start = ((s32[8,48,128]{2,1,0:T(8,128)}), s32[8,48,128]{2,1,0:T(8,128)S(1)}, u32[]{:S(2)}, u32[]{:S(2)}) async-start(s32[8,48,128]{2,1,0:T(8,128)} %broadcast_in_dim.20), calls=%async_computation | async-start | bytes 393216 | tf_op jit(solution)/shard_map/all_to_all | solution.py:130
  13.4 5.9 %all-to-all-done.bags_ref = s32[8,48,128]{2,1,0:T(8,128)S(1)} async-done(((s32[8,48,128]{2,1,0:T(8,128)}), s32[8,48,128]{2,1,0:T(8,128)S(1)}, u32[]{:S(2)}, u32[]{:S(2)}) %all-to-all-start) | async-done | bytes 196640 | tf_op jit(solution)/shard_map/all_to_all | solution.py:130
  19.3 26.9 %all_to_all.40.tab_ref = bf16[8,6,32,128]{3,2,1,0:T(8,128)(2,1)S(1)} all-to-all(bf16[8,6,32,128]{3,2,1,0:T(8,128)(2,1)S(1)} %broadcast_in_dim.21), channel_id=1, replica_groups=mesh['x'=4,'core'=2,'y'=4,'zhi'=2,'sub'=8] {'sub'}, dimensions={0} | all-to-all | bytes 786432 | tf_op jit(solution)/shard_map/all_to_all | solution.py:130
  47.2 5.0 %shard_map.123 = (bf16[32,6,32,128]{3,2,1,0:T(8,128)(2,1)S(1)}, bf16[6,256,1024]{2,1,0:T(8,128)(2,1)S(1)}) custom-call(s32[1]{0:T(128)} %bitcast.rep_ref, s32[8,48,128]{2,1,0:T(8,128)S(1)} %copy-done.3, bf16[8,6,32,128]{3,2,1,0:T(8,128)(2,1)S(1)} %all_to_all.40.tab_ref), custom_call_target="tpu_custom_call" | custom-call | tf_op jit(solution)/shard_map/pallas_call | solution.py:157
  53.4 10.3 %all-to-all-start.2 = ((bf16[32,6,32,128]{3,2,1,0:T(8,128)(2,1)}), bf16[32,6,32,128]{3,2,1,0:T(8,128)(2,1)}, u32[]{:S(2)}, u32[]{:S(2)}) async-start(bf16[32,6,32,128]{3,2,1,0:T(8,128)(2,1)} %copy-done.1), calls=%async_computation.2 | async-start | bytes 3145728 | tf_op jit(solution)/shard_map/all_to_all | solution.py:130
  67.0 3.2 %slice_bitcast_fusion = (bf16[1536,384]{0,1:T(8,128)(2,1)}, bf16[1536,384]{0,1:T(8,128)(2,1)}) fusion(bf16[2,384,1536]{2,1,0:T(8,128)(2,1)} %param.17), kind=kLoop, calls=%fused_computation.36 | loop fusion | bytes 4718592 | tf_op jit(solution)/shard_map/jvp()/dot_general | solution.py:35
  70.2 2.4 copy.109
  74.7 2.4 copy.120
  77.0 8.1 %all-to-all-done.2 = bf16[32,6,32,128]{3,2,1,0:T(8,128)(2,1)} async-done(((bf16[32,6,32,128]{3,2,1,0:T(8,128)(2,1)}), bf16[32,6,32,128]{3,2,1,0:T(8,128)(2,1)}, u32[]{:S(2)}, u32[]{:S(2)}) %all-to-all-start.2) | async-done | bytes 1572896 | tf_op jit(solution)/shard_map/all_to_all | solution.py:130
  85.2 2.4 reduce_sum.249
  87.5 1.6 copy.103
  89.1 7.3 %all-to-all-start.3 = ((bf16[2,4,6,16,128]{4,3,2,1,0:T(8,128)(2,1)}), bf16[2,4,6,16,128]{4,3,2,1,0:T(8,128)(2,1)}, u32[]{:S(2)}, u32[]{:S(2)}) async-start(bf16[2,4,6,16,128]{4,3,2,1,0:T(8,128)(2,1)} %copy.103), calls=%async_computation.3 | async-start | bytes 393216 | tf_op jit(solution)/shard_map/all_to_all | solution.py:130
  98.5 11.3 %all-to-all-done.3 = bf16[2,4,6,16,128]{4,3,2,1,0:T(8,128)(2,1)} async-done(((bf16[2,4,6,16,128]{4,3,2,1,0:T(8,128)(2,1)}), bf16[2,4,6,16,128]{4,3,2,1,0:T(8,128)(2,1)}, u32[]{:S(2)}, u32[]{:S(2)}) %all-to-all-start.3) | async-done | bytes 196640 | tf_op jit(solution)/shard_map/all_to_all | solution.py:130
  116.9 1.7 fusion.85
  139.7 1.7 fusion.83
  149.7 1.6 copy.130
  164.3 1.6 add_add_fusion.1
  167.7 1.6 copy.138
  169.4 1.6 copy.131
  171.0 3.4 %multiply_reduce_fusion.15 = (f32[16]{0:T(128)}, f32[16]{0:T(128)}, f32[16,384]{1,0:T(8,128)}) fusion(f32[16]{0:T(128)} %copy-done.50, f32[16,384]{1,0:T(8,128)} %copy.131, f32[16]{0:T(128)} %copy-done.42, f32[384]{0:T(512)} %copy-done.44, bf16[2,384,384]{2,1,0:T(8,128)(2,1)} %param.16, f32[16,384]{1,0:T(8,128)} %copy-done.29, ...), kind=kOutput, calls=%fused_computation.118 | convolution fusion | flops 23703520 | bytes 1617024 | tf_op jit(solution)/shard_map/transpose(jvp())/dot_general | solution.py:32
  179.9 1.7 copy.133
  183.7 3.2 %multiply_reduce_fusion.7 = (f32[16,48]{1,0:T(8,128)}, f32[16,48]{1,0:T(8,128)}, f32[16,48,128]{2,1,0:T(8,128)}) fusion(f32[16,48]{1,0:T(8,128)S(1)} %rsqrt.49, f32[16,48]{1,0:T(8,128)S(1)} %copy.115, f32[16,48,128]{2,1,0:T(8,128)} %copy-done.15, bf16[16,48,128]{2,0,1:T(8,128)(2,1)} %bitcast.212, f32[128]{0:T(128)} %get-tuple-element.26, ...), kind=kOutput, calls=%fused_computation.62 | convolution fusion | flops 10615296 | bytes 1839616 | tf_op jit(solution)/shard_map/transpose(jvp(bne,bke->bnk))/dot_general | solution.py:28
  196.1 1.7 add_add_fusion
  199.5 1.6 copy.139
  201.2 3.3 %multiply_reduce_fusion.14 = (f32[16]{0:T(128)}, f32[16]{0:T(128)}, f32[16,384]{1,0:T(8,128)}) fusion(f32[16]{0:T(128)} %copy-done.48, f32[16,384]{1,0:T(8,128)} %copy.139, f32[16]{0:T(128)} %copy-done.40, f32[384]{0:T(512)} %copy-done.43, bf16[2,384,384]{2,1,0:T(8,128)(2,1)} %param.16, f32[16,384]{1,0:T(8,128)} %copy-done.28, ...), kind=kOutput, calls=%fused_computation.117 | convolution fusion | flops 23703520 | bytes 1617024 | tf_op jit(solution)/shard_map/transpose(jvp())/dot_general | solution.py:32
  209.9 1.7 copy.141
  213.1 1.6 fusion.8
  214.7 16.0 %all_to_all.41 = bf16[2,4,6,16,128]{4,3,2,1,0:T(8,128)(2,1)S(1)} all-to-all(bf16[2,4,6,16,128]{4,3,2,1,0:T(8,128)(2,1)S(1)} %copy.145), channel_id=1, replica_groups=mesh['x'=4,'core'=2,'y'=4,'zhi'=2,'sub'=8] {'zhi'}, dimensions={0} | all-to-all | bytes 393216 | tf_op jit(solution)/shard_map/all_to_all | solution.py:130
  231.1 29.5 %all_to_all.42.moved_ref = bf16[32,6,32,128]{3,2,1,0:T(8,128)(2,1)S(1)} all-to-all(bf16[32,6,32,128]{3,2,1,0:T(8,128)(2,1)S(1)} %bitcast.217), channel_id=1, replica_groups=mesh['x'=4,'core'=2,'y'=4,'zhi'=2,'sub'=8] {'x','core','y'}, dimensions={0} | all-to-all | bytes 3145728 | tf_op jit(solution)/shard_map/all_to_all | solution.py:130
  260.5 1.7 shard_map.124
  262.3 27.3 %all_to_all.43 = bf16[8,6,32,128]{3,2,1,0:T(8,128)(2,1)S(1)} all-to-all(bf16[8,6,32,128]{3,2,1,0:T(8,128)(2,1)S(1)} %shard_map.124), channel_id=1, replica_groups=mesh['x'=4,'core'=2,'y'=4,'zhi'=2,'sub'=8] {'sub'}, dimensions={0} | all-to-all | bytes 786432 | tf_op jit(solution)/shard_map/all_to_all | solution.py:130
  289.7 15.8 %all_to_all.44 = bf16[8,6,32,128]{3,2,1,0:T(8,128)(2,1)S(1)} all-to-all(bf16[8,6,32,128]{3,2,1,0:T(8,128)(2,1)S(1)} %broadcast_in_dim.51), channel_id=1, replica_groups=mesh['x'=4,'core'=2,'y'=4,'zhi'=2,'sub'=8] {'x','core'}, dimensions={0} | all-to-all | bytes 786432 | tf_op jit(solution)/shard_map/all_to_all | solution.py:130
  (215 shorter events, 90.0 us)
Async XLA Ops:
  0.6 12.7 %copy-start = (bf16[6,256,128]{2,1,0:T(8,128)(2,1)S(1)}, bf16[6,256,128]{2,1,0:T(8,128)(2,1)}, u32[]{:S(2)}) copy-start(bf16[6,256,128]{2,1,0:T(8,128)(2,1)} %param.11) | copy-start | bytes 1179652
  3.2 16.1 %all-to-all-start = ((s32[8,48,128]{2,1,0:T(8,128)}), s32[8,48,128]{2,1,0:T(8,128)S(1)}, u32[]{:S(2)}, u32[]{:S(2)}) async-start(s32[8,48,128]{2,1,0:T(8,128)} %broadcast_in_dim.20), calls=%async_computation | async-start | bytes 393216 | tf_op jit(solution)/shard_map/all_to_all | solution.py:130
  19.3 27.0 %copy-start.2 = (s32[8,48,128]{2,1,0:T(8,128)}, s32[8,48,128]{2,1,0:T(8,128)S(1)}, u32[]{:S(2)}) copy-start(s32[8,48,128]{2,1,0:T(8,128)S(1)} %all-to-all-done.bags_ref) | copy-start | bytes 589828
  53.3 10.3 %copy-start.35 = (bf16[48,128]{1,0:T(8,128)(2,1)S(1)}, bf16[48,128]{1,0:T(8,128)(2,1)}, u32[]{:S(2)}) copy-start(bf16[48,128]{1,0:T(8,128)(2,1)} %param.21) | copy-start | bytes 36868
  53.3 11.5 %copy-start.47 = (f32[2,384]{1,0:T(2,128)S(1)}, f32[2,384]{1,0:T(2,128)}, u32[]{:S(2)}) copy-start(f32[2,384]{1,0:T(2,128)} %param.19) | copy-start | bytes 9220
  53.4 31.8 %all-to-all-start.2 = ((bf16[32,6,32,128]{3,2,1,0:T(8,128)(2,1)}), bf16[32,6,32,128]{3,2,1,0:T(8,128)(2,1)}, u32[]{:S(2)}, u32[]{:S(2)}) async-start(bf16[32,6,32,128]{3,2,1,0:T(8,128)(2,1)} %copy-done.1), calls=%async_computation.2 | async-start | bytes 3145728 | tf_op jit(solution)/shard_map/all_to_all | solution.py:130
  64.9 7.7 %copy-start.44 = (f32[384]{0:T(512)}, f32[384]{0:T(512)S(1)}, u32[]{:S(2)}) copy-start(f32[384]{0:T(512)S(1)} %get-tuple-element.12) | copy-start | bytes 4612
  85.2 11.3 %copy-start.51 = (f32[2,128]{1,0:T(2,128)S(1)}, f32[2,128]{1,0:T(2,128)}, u32[]{:S(2)}) copy-start(f32[2,128]{1,0:T(2,128)} %param.20) | copy-start | bytes 3076
  85.2 25.6 %copy-start.45 = (bf16[2,48,8]{1,2,0:T(8,128)(2,1)S(1)}, bf16[2,48,8]{1,2,0:T(8,128)(2,1)}, u32[]{:S(2)}) copy-start(bf16[2,48,8]{1,2,0:T(8,128)(2,1)} %param.15) | copy-start | bytes 4612
  89.1 20.7 %all-to-all-start.3 = ((bf16[2,4,6,16,128]{4,3,2,1,0:T(8,128)(2,1)}), bf16[2,4,6,16,128]{4,3,2,1,0:T(8,128)(2,1)}, u32[]{:S(2)}, u32[]{:S(2)}) async-start(bf16[2,4,6,16,128]{4,3,2,1,0:T(8,128)(2,1)} %copy.103), calls=%async_computation.3 | async-start | bytes 393216 | tf_op jit(solution)/shard_map/all_to_all | solution.py:130
  115.6 3.0 copy-start.11
  115.6 3.0 copy-start.30
  116.9 2.7 copy-start.28
  118.6 3.0 copy-start.18
  119.6 2.0 copy-start.15
  129.9 3.0 copy-start.12
  129.9 3.0 copy-start.14
  129.9 3.0 copy-start.19
  129.9 6.4 %copy-start.37 = (f32[48,8]{0,1:T(8,128)S(1)}, f32[48,8]{0,1:T(8,128)}, u32[]{:S(2)}) copy-start(f32[48,8]{0,1:T(8,128)} %copy.118) | copy-start | bytes 4612
  132.9 1.9 copy-start.27
  138.5 3.0 copy-start.9
  138.5 3.0 copy-start.32
  139.7 2.0 copy-start.29
  141.9 2.1 copy-start.6
  141.9 1.6 copy-start.55
  142.1 1.9 copy-start.22
  161.8 4.8 %copy-start.33 = (bf16[1,36,48]{2,0,1:T(2,128)(2,1)S(1)}, bf16[1,36,48]{2,0,1:T(2,128)(2,1)}, u32[]{:S(2)}) copy-start(bf16[1,36,48]{2,0,1:T(2,128)(2,1)} %get-tuple-element.20) | copy-start | bytes 10372
  195.3 3.1 %copy-start.31 = (bf16[1,36,48]{2,0,1:T(2,128)(2,1)S(1)}, bf16[1,36,48]{2,0,1:T(2,128)(2,1)}, u32[]{:S(2)}) copy-start(bf16[1,36,48]{2,0,1:T(2,128)(2,1)} %get-tuple-element.21) | copy-start | bytes 10372
  198.4 6.1 %copy-start.53 = (f32[16]{0:T(128)S(1)}, f32[16]{0:T(128)}, u32[]{:S(2)}) copy-start(f32[16]{0:T(128)} %copy-done.52) | copy-start | bytes 196
  198.4 6.8 %copy-start.41 = (f32[16]{0:T(128)S(1)}, f32[16]{0:T(128)}, u32[]{:S(2)}) copy-start(f32[16]{0:T(128)} %copy-done.40) | copy-start | bytes 196
  199.5 7.4 %copy-start.49 = (f32[16]{0:T(128)S(1)}, f32[16]{0:T(128)}, u32[]{:S(2)}) copy-start(f32[16]{0:T(128)} %copy-done.48) | copy-start | bytes 196
  201.2 11.6 %copy-start.46 = (bf16[2,48,8]{1,2,0:T(8,128)(2,1)S(1)}, bf16[2,48,8]{1,2,0:T(8,128)(2,1)}, u32[]{:S(2)}) copy-start(bf16[2,48,8]{1,2,0:T(8,128)(2,1)} %param.15) | copy-start | bytes 4612
  (27 other events, 20.8 us)

commit v2 on v1

v2 whole, which is shorter than its diff:
```python
import jax
import jax.numpy as jnp
from jax import lax
from jax.experimental import pallas as pl
from jax.experimental.pallas import tpu as pltpu
from jax.sharding import Mesh
from jax.sharding import PartitionSpec as P

REP = ("x", "core")
GRP = ("y", "zhi")
DEAD = 4095
FIELDS, BATCH, WIDTH, RANK, NF = 48, 16, 128, 8, 12
VMEM_LIMIT = 48 * 1024 * 1024


def pick_kernel(sub_ref, rows_ref, lens_ref, out_ref):
    tables, bag, _ = rows_ref.shape
    slots = lax.broadcasted_iota(jnp.int32, (bag, 128), 0)
    lanes = lax.broadcasted_iota(jnp.int32, (bag, 128), 1)
    sub = sub_ref[0]
    for table in range(tables):
        kept = jnp.zeros((bag, 128), jnp.int32)
        for run in range(8):
            cut = slice(run * 128, run * 128 + 128)
            coded = jnp.where(
                slots < lens_ref[table : table + 1, cut], rows_ref[table, :, cut], DEAD
            )
            moved = pltpu.roll(coded, (run * 16 - sub * 16) & 127, 1)
            kept = jnp.where(lanes // 16 == run, moved, kept)
        out_ref[pl.ds(table * bag, bag), :] = kept


def dot(a, b, dims):
    return lax.dot_general(a, b, (dims, ((), ())), preferred_element_type=jnp.float32)


def slide(values, shift):
    halves = []
    for half in range(2):
        part = values[half * 8 : half * 8 + 8]
        base = (shift + half * 64) % WIDTH
        if base + 7 * RANK >= WIDTH:
            part, base = pltpu.roll(part, base, 1), 0
        halves.append(pltpu.roll(part, base, 1, stride=RANK, stride_axis=0))
    return jnp.concatenate(halves, axis=0)


def dense_kernel(
    near_ref, labels_ref, mix_ref, mlp_in_ref, mlp_out_ref, gain_fm_ref, gain_out_ref, head_ref,
    loss_ref, back_ref,
    x_ref, t_ref, xhat_ref, rstd_ref, xb_ref, d_ref,
):
    f32, bf16 = jnp.float32, jnp.bfloat16
    zs, ys, tables = near_ref.shape[:3]
    layers = mix_ref.shape[0]
    block = tables * BATCH
    rows = FIELDS * BATCH
    chunk = 128
    lane = lax.broadcasted_iota(jnp.int32, (BATCH, WIDTH), 1) // RANK

    for y in range(ys):
        for z in range(zs):
            at = (y * zs + z) * block
            xb_ref[0, at : at + block] = near_ref[z, y].reshape(block, WIDTH)
    x_ref[...] = xb_ref[0].astype(f32)

    def example(ref, e):
        return ref[pl.ds(e, FIELDS, stride=BATCH), :]

    saved = []
    for layer in range(layers):
        across = jnp.concatenate([example(x_ref, e).astype(bf16) for e in range(BATCH)], axis=1)
        mixed = dot(mix_ref[layer], across, ((1,), (0,)))
        for e in range(BATCH):
            t_ref[pl.ds(e, FIELDS, stride=BATCH), :] = mixed[:, e * WIDTH : (e + 1) * WIDTH]
        pieces = [mixed[:RANK, e * WIDTH : (e + 1) * WIDTH] for e in range(BATCH)]
        summary = jnp.concatenate(pieces, axis=0).astype(bf16)
        mirrored = jnp.concatenate(pieces[::-1], axis=0).astype(bf16)
        pairs = dot(xb_ref[layer], mirrored, ((1,), (1,)))
        flat = []
        for q in range(FIELDS // BATCH):
            acc = jnp.zeros((BATCH, WIDTH), f32)
            for j in range(BATCH):
                at = (q * BATCH + j) * BATCH
                moved = slide(pairs[at : at + BATCH], (j + 1) * RANK)
                acc = jnp.where(lane == j, moved, acc)
            flat.append(acc)
        flat = jnp.concatenate(flat, axis=1)
        center = jnp.mean(flat, axis=1, keepdims=True)
        flat = flat - center
        rstd_fm = lax.rsqrt(jnp.mean(flat * flat, axis=1, keepdims=True) + 1e-05)
        nhat = flat * rstd_fm
        normed = (nhat * gain_fm_ref[layer : layer + 1]).astype(bf16)
        z = dot(normed, mlp_in_ref[layer], ((1,), (0,)))
        gate = jax.nn.sigmoid(z)
        hidden = (z * gate).astype(bf16)
        machine = dot(hidden, mlp_out_ref[layer], ((1,), (0,)))
        for n in range(NF):
            t_ref[n * BATCH : (n + 1) * BATCH] = machine[:, n * WIDTH : (n + 1) * WIDTH]
        gain = gain_out_ref[layer : layer + 1]
        for at in range(0, rows, chunk):
            cut = slice(at, at + chunk)
            total = t_ref[cut] + x_ref[cut]
            total = total - jnp.mean(total, axis=1, keepdims=True)
            rstd = lax.rsqrt(jnp.mean(total * total, axis=1, keepdims=True) + 1e-05)
            xhat = total * rstd
            xhat_ref[layer, cut] = xhat
            rstd_ref[layer, cut] = rstd
            out = (xhat * gain).astype(bf16)
            xb_ref[layer + 1, cut] = out
            x_ref[cut] = out.astype(f32)
        saved.append((summary, nhat, rstd_fm, z, gate))

    acc = jnp.zeros((BATCH, WIDTH), f32)
    head = head_ref[...].astype(f32)
    for t in range(FIELDS):
        acc = acc + x_ref[t * BATCH : (t + 1) * BATCH] * head[t : t + 1]
    logit = jnp.sum(acc, axis=1, keepdims=True)
    labels = labels_ref[...]
    loss_ref[...] = jnp.maximum(logit, 0.0) + jnp.log1p(jnp.exp(-jnp.abs(logit))) - labels * logit
    dlogit = jnp.broadcast_to(jax.nn.sigmoid(logit) - labels, (BATCH, WIDTH))
    for t in range(FIELDS):
        x_ref[t * BATCH : (t + 1) * BATCH] = (dlogit * head[t : t + 1]).astype(bf16).astype(f32)

    low = lax.broadcasted_iota(jnp.int32, (RANK, WIDTH), 0) >= NF - RANK
    for layer in reversed(range(layers)):
        summary, nhat, rstd_fm, z, gate = saved[layer]
        gain = gain_out_ref[layer : layer + 1]
        for at in range(0, rows, chunk):
            cut = slice(at, at + chunk)
            xhat = xhat_ref[layer, cut]
            dxhat = x_ref[cut] * gain
            mean_d = jnp.mean(dxhat, axis=1, keepdims=True)
            mean_p = jnp.mean(dxhat * xhat, axis=1, keepdims=True)
            t_ref[cut] = rstd_ref[layer, cut] * (dxhat - mean_d - xhat * mean_p)
        dmachine = jnp.concatenate(
            [t_ref[n * BATCH : (n + 1) * BATCH].astype(bf16) for n in range(NF)], axis=1
        )
        dhidden = dot(dmachine, mlp_out_ref[layer], ((1,), (1,))).astype(bf16).astype(f32)
        dz = (dhidden * gate * (1.0 + z * (1.0 - gate))).astype(bf16)
        dnormed = dot(dz, mlp_in_ref[layer], ((1,), (1,))).astype(bf16).astype(f32)
        dnhat = dnormed * gain_fm_ref[layer : layer + 1]
        mean_d = jnp.mean(dnhat, axis=1, keepdims=True)
        mean_p = jnp.mean(dnhat * nhat, axis=1, keepdims=True)
        dflat = rstd_fm * (dnhat - mean_d - nhat * mean_p)
        for q in range(FIELDS // BATCH):
            part = dflat[:, q * WIDTH : (q + 1) * WIDTH]
            for j in range(BATCH):
                at = (q * BATCH + j) * BATCH
                only = jnp.where(lane == j, part, 0.0)
                d_ref[at : at + BATCH] = slide(only, -j * RANK).astype(bf16)
        dpairs = d_ref[...]
        dsummary = dot(dpairs, xb_ref[layer], ((0,), (0,)))
        parts = []
        for e in range(BATCH):
            straight = example(t_ref, e)
            parts.append(
                jnp.concatenate(
                    [
                        dsummary[e * RANK : (e + 1) * RANK],
                        jnp.where(low, straight[RANK : 2 * RANK], 0.0),
                        straight[2 * RANK :],
                    ],
                    axis=0,
                ).astype(bf16)
            )
        dacross = dot(mix_ref[layer], jnp.concatenate(parts, axis=1), ((0,), (0,)))
        for e in range(BATCH):
            x_ref[pl.ds(e, FIELDS, stride=BATCH), :] = dacross[:, e * WIDTH : (e + 1) * WIDTH]
        for at in range(0, rows, chunk):
            cut = slice(at, at + chunk)
            dx = x_ref[cut] + t_ref[cut] + dot(d_ref[cut], summary, ((1,), (0,)))
            x_ref[cut] = dx.astype(bf16).astype(f32)

    for y in range(ys):
        for z in range(zs):
            at = (y * zs + z) * block
            back_ref[z, y] = x_ref[at : at + block].astype(bf16).reshape(tables, BATCH, WIDTH)


def mix_of(proj, compress):
    layers = proj.shape[0]
    gap = jnp.zeros((layers, NF - RANK, FIELDS), proj.dtype)
    return jnp.concatenate([jnp.transpose(proj, (0, 2, 1)), gap, compress], axis=1)


def counts_kernel(where_ref, b0_ref, b1_ref, b2_ref, b3_ref, counts_ref, idx_ref):
    tables, local, examples = counts_ref.shape
    column, core = where_ref[0], where_ref[1]
    for src, bags_ref in enumerate((b0_ref, b1_ref, b2_ref, b3_ref)):
        coded = bags_ref[...]
        mine = ((coded >> 6) & 3) == column
        side = ((coded >> 5) & 1) ^ core
        spot = (side << 8) | ((coded >> 8) << 5) | (coded & 31)
        spot = jnp.where(mine & (coded < DEAD), spot, -1)
        at = pl.multiple_of(((column + src) & 3) * 128, 128)
        idx_ref[:, pl.ds(at, 128)] = spot.astype(jnp.float32)
    steps = local // 32
    ids = [
        (lax.broadcasted_iota(jnp.int32, (16, 128), 0) + 16 * i)
        .astype(jnp.float32)
        .astype(jnp.bfloat16)
        for i in range(256 // 16)
    ]
    one = jnp.ones((16, 128), jnp.bfloat16)
    zero = jnp.zeros((16, 128), jnp.bfloat16)

    def per_table(table, carry):
        for run in range(examples // 128):
            cut = slice(run * 128, run * 128 + 128)
            slots = idx_ref[pl.ds(pl.multiple_of(table * 8, 8), 8), cut]
            for half in range(2):
                keys = [
                    jnp.broadcast_to(slots[b : b + 1] - 256.0 * half, (16, 128)).astype(jnp.bfloat16)
                    for b in range(8)
                ]
                for i in range(steps):
                    hits = [jnp.where(keys[b] == ids[i], one, zero) for b in range(8)]
                    while len(hits) > 1:
                        hits = [hits[k] + hits[k + 1] for k in range(0, len(hits), 2)]
                    at = half * 256 + i * 16
                    counts_ref[table, at : at + 16, cut] = hits[0]
        return carry

    lax.fori_loop(0, tables, per_table, 0)


def pool_kernel(counts_ref, mine_ref, other_ref, pools_ref):
    tables, local, examples = counts_ref.shape
    width = mine_ref.shape[-1]

    def per_table(table, carry):
        rows = jnp.concatenate(
            [ref[:, table].reshape(local // 2, width) for ref in (mine_ref, other_ref)], axis=0
        )
        part = dot(counts_ref[table], rows, ((0,), (0,)))
        pools_ref[:, table] = part.astype(jnp.bfloat16).reshape(examples // 32, 32, width)
        return carry

    lax.fori_loop(0, tables, per_table, 0)


def merge_kernel(moved_ref, out_ref):
    columns, ys, tables = moved_ref.shape[:3]

    def per_table(table, carry):
        for y in range(ys):
            total = moved_ref[0, y, table].astype(jnp.float32)
            for column in range(1, columns):
                total = total + moved_ref[column, y, table].astype(jnp.float32)
            total = total.astype(jnp.bfloat16)
            out_ref[0, y, table] = total[:BATCH]
            out_ref[1, y, table] = total[BATCH:]
        return carry

    lax.fori_loop(0, tables, per_table, 0)


def grads_kernel(counts_ref, moved_ref, mine_ref, other_ref):
    tables, local, examples = counts_ref.shape
    shards, _, rows, width = mine_ref.shape

    def per_table(table, carry):
        grads = moved_ref[:, table].reshape(examples, width)
        acc = dot(counts_ref[table], grads, ((1,), (0,))).astype(jnp.bfloat16)
        mine_ref[:, table] = acc[: local // 2].reshape(shards, rows, width)
        other_ref[:, table] = acc[local // 2 :].reshape(shards, rows, width)
        return carry

    lax.fori_loop(0, tables, per_table, 0)


def add_kernel(left_ref, right_ref, out_ref):
    for shard in range(out_ref.shape[0]):
        total = left_ref[shard].astype(jnp.float32) + right_ref[shard].astype(jnp.float32)
        out_ref[shard] = total.astype(jnp.bfloat16)


def swap(values, axes):
    return lax.all_to_all(values, axes, split_axis=0, concat_axis=0, tiled=True)


def call(kernel, out_shape, ins, args, scratch=()):
    vmem = pl.BlockSpec(memory_space=pltpu.VMEM)
    smem = pl.BlockSpec(memory_space=pltpu.SMEM)
    many = isinstance(out_shape, tuple)
    return pl.pallas_call(
        kernel,
        out_shape=out_shape,
        in_specs=[smem if kind == "s" else vmem for kind in ins],
        out_specs=(vmem,) * len(out_shape) if many else vmem,
        scratch_shapes=list(scratch),
        compiler_params=pltpu.CompilerParams(vmem_limit_bytes=VMEM_LIMIT),
    )(*args)


def per_device(
    table_rows, bag_rows, bag_lens, labels, proj, mlp_in, mlp_out, compress, gain_fm, gain_out, head
):
    f32, bf16 = jnp.float32, jnp.bfloat16
    shape = jax.ShapeDtypeStruct
    tables, rows_dev, width = table_rows.shape
    layers = proj.shape[0]
    sub = lax.axis_index("sub")
    rep = lax.axis_index(REP)
    column, core = lax.axis_index("x"), lax.axis_index("core")
    columns, cores, subs, ys, zs = 4, 2, 8, 4, 2
    reps = columns * cores
    part_rows = rows_dev // reps
    examples = columns * ys * zs * BATCH
    across = [(0, 1), (1, 0)]

    coded = call(
        pick_kernel,
        shape((tables * 8, 128), jnp.int32),
        "svv",
        (sub.reshape(1), jnp.transpose(bag_rows, (1, 2, 0)), jnp.transpose(bag_lens)),
    )
    bags = [coded] + [
        lax.ppermute(coded, "x", [((i + hop) % columns, i) for i in range(columns)])
        for hop in range(1, columns)
    ]
    part = lax.dynamic_slice_in_dim(table_rows, rep * part_rows, part_rows, axis=1)
    gathered = swap(jnp.broadcast_to(part, (subs, tables, part_rows, width)), "sub")
    counts = call(
        counts_kernel,
        shape((tables, 2 * rows_dev, examples), bf16),
        "svvvv",
        (jnp.stack([column, core]), *bags),
        [pltpu.VMEM((tables * 8, examples), f32)],
    )
    other = lax.ppermute(gathered, "core", across)
    pools = call(
        pool_kernel,
        shape((columns * ys, tables, zs * BATCH, width), bf16),
        "vvv",
        (counts, gathered, other),
    )
    moved = swap(pools, ("x", "y"))
    merged = call(
        merge_kernel,
        shape((zs, ys, tables, BATCH, width), bf16),
        "v",
        (moved.reshape(columns, ys, tables, zs * BATCH, width),),
    )
    near = swap(merged, "zhi")

    rows = FIELDS * BATCH
    losses, back = call(
        dense_kernel,
        (shape((BATCH, 1), f32), shape(near.shape, bf16)),
        "v" * 8,
        (
            near,
            labels.reshape(BATCH, 1),
            mix_of(proj, compress),
            mlp_in,
            mlp_out,
            gain_fm,
            gain_out,
            head,
        ),
        [
            pltpu.VMEM((rows, WIDTH), f32),
            pltpu.VMEM((rows, WIDTH), f32),
            pltpu.VMEM((layers, rows, WIDTH), f32),
            pltpu.VMEM((layers, rows, 1), f32),
            pltpu.VMEM((layers + 1, rows, WIDTH), bf16),
            pltpu.VMEM((rows, WIDTH), bf16),
        ],
    )

    back = jnp.transpose(swap(back, "zhi"), (1, 2, 0, 3, 4)).reshape(1, ys, tables, -1, width)
    back = jnp.broadcast_to(back, (columns, *back.shape[1:]))
    returned = swap(back.reshape(columns * ys, tables, -1, width), ("x", "y"))
    piece = shape((subs, tables, part_rows, width), bf16)
    mine, other = call(grads_kernel, (piece, piece), "vv", (counts, returned))
    other = lax.ppermute(other, "core", across)
    pieces = swap(call(add_kernel, piece, "vv", (mine, other)), "sub")
    own = jnp.sum(pieces.astype(f32), axis=0).astype(bf16)
    spread = swap(jnp.broadcast_to(own, (reps, tables, part_rows, width)), REP)
    row_grads = jnp.transpose(spread, (1, 0, 2, 3)).reshape(tables, rows_dev, width)
    return (losses.reshape(BATCH), row_grads.astype(f32))


def solution(mesh):
    view = Mesh(mesh.devices.reshape(4, 2, 4, 2, 8), ("x", "core", "y", "zhi", "sub"))
    return jax.shard_map(
        per_device,
        mesh=view,
        in_specs=(
            P(GRP, "sub", None),
            P(REP, GRP, None),
            P(REP, GRP),
            P(REP + GRP + ("sub",)),
            P(),
            P(),
            P(),
            P(),
            P(),
            P(),
            P(),
        ),
        out_specs=(P(REP + GRP + ("sub",)), P(GRP, "sub", None)),
        check_vma=False,
    )
```

time: 310 us -> 200 us (0.65)
  local copies, waits for them, and re-layouts: 68.7 us -> 10.8 us
  other arithmetic: 36 us -> 2.4 us
  matrix products: 25.1 us -> 0 us
  Pallas kernels: 6.85 us -> 15.7 us
  starting transfers between devices: 27.7 us -> 35 us
  blocking collectives: 115 us -> 109 us
    dot_general x20 -> x0, matrix products: 25.1 us -> none  [the longest x4 9.16 us: wukong_layer(): jnp.dot(normed, mlp_in, preferred_element_type=jnp.float32)]
    ppermute x0 -> x5, starting transfers between devices: none -> 21.3 us  [the longest x3 9.33 us: per_device(): lax.ppermute(coded, 'x', [((i + hop) % columns, i) for i in range(columns)])]
    all_to_all x3 -> x2, starting transfers between devices: 27.7 us -> 13.7 us  [swap(): return lax.all_to_all(values, axes, split_axis=0, concat_axis=0, tiled=True)]
    reduce_sum x15 -> x1, other arithmetic: 13.6 us -> 0.06 us  [per_device(): own = jnp.sum(pieces.astype(f32), axis=0).astype(bf16)]
    dot_general x7 -> x0, local copies, waits for them, and re-layouts: 11.3 us -> none  [the longest x5 8.07 us: wukong_layer(): jnp.dot(hidden, mlp_out, preferred_element_type=jnp.float32)]
    pallas_call x3 -> x7, Pallas kernels: 6.85 us -> 15.7 us  [call(): pl.pallas_call(kernel, out_shape=out_shape, in_specs=[smem if kind == 's'...]
    add_any x5 -> x0, other arithmetic: 6.73 us -> none  [the longest x4 6.19 us: layer_norm(): center = jnp.mean(values, axis=-1, keepdims=True)]
    all_to_all x5, blocking collectives: 115 us -> 109 us  [swap(): return lax.all_to_all(values, axes, split_axis=0, concat_axis=0, tiled=True)]
  transfers between devices with their start and end apart: 3 -> 7, of which waited for: 3 -> 5; matrix products, arithmetic and copies ran while one was open for 5% -> 1% of each run, Pallas kernels for 0% -> 2%
where the time goes in v2:
time: 200 us; the launch traced here: 199 us
  blocking collectives  109 us (54%)
  starting transfers between devices  35 us (18%)
  waiting for transfers between devices  25 us (12%)
  Pallas kernels  15.7 us (8%)
  local copies, waits for them, and re-layouts  10.8 us (5%)
  other arithmetic  2.4 us (1%)
    all_to_all x5, blocking collectives, swap(): return lax.all_to_all(values, axes, split_axis=0, concat_axis=0, tiled=True)  109 us
    all_to_all x2, waiting for transfers between devices, swap(): return lax.all_to_all(values, axes, split_axis=0, concat_axis=0, tiled=True)  20.5 us
    pallas_call x7, Pallas kernels, call(): pl.pallas_call(kernel, out_shape=out_shape, in_specs=[smem if kind == 's'...  15.7 us
    all_to_all x2, starting transfers between devices, swap(): return lax.all_to_all(values, axes, split_axis=0, concat_axis=0, tiled=True)  13.7 us
    unnamed x25, local copies, waits for them, and re-layouts  9.61 us
    ppermute x3, starting transfers between devices, per_device(): lax.ppermute(coded, 'x', [((i + hop) % columns, i) for i in range(columns)])  9.33 us
    ppermute x1, starting transfers between devices, per_device(): other = lax.ppermute(gathered, 'core', across)  6.76 us
    ppermute x1, starting transfers between devices, per_device(): other = lax.ppermute(other, 'core', across)  5.23 us
  transfers between devices with their start and end apart: 7, of which 5 were waited for; matrix products, arithmetic and copies ran while one was open for 1% of the time, Pallas kernels for 2%

profile of v2, /device:TPU:1, one launch (start us, length us, event | category | flops | bytes accessed | tf_op | source)
XLA Modules:
  0.0 198.5 jit_solution(9858925405231343022)
XLA Ops:
  0.7 1.0 copy-done
  1.7 32.2 %all_to_all.35.mine_ref = bf16[8,6,32,128]{3,2,1,0:T(8,128)(2,1)} all-to-all(bf16[8,6,32,128]{3,2,1,0:T(8,128)(2,1)S(1)} %broadcast_in_dim.16), channel_id=1, replica_groups=mesh['x'=4,'core'=2,'y'=4,'zhi'=2,'sub'=8] {'sub'}, dimensions={0} | all-to-all | bytes 786432 | tf_op jit(solution)/shard_map/all_to_all | solution.py:280
  33.9 6.8 %collective-permute-start.3 = (bf16[8,6,32,128]{3,2,1,0:T(8,128)(2,1)}, bf16[8,6,32,128]{3,2,1,0:T(8,128)(2,1)}, u32[]{:S(2)}, u32[]{:S(2)}) collective-permute-start(bf16[8,6,32,128]{3,2,1,0:T(8,128)(2,1)} %all_to_all.35.mine_ref), channel_id=1, source_target_pairs={{0,64},{64,0},{1,65},{65,1},{2,66},{66,2},{3,67},{67,3},{4,68},{68... | collective-permute-start | bytes 1179656 | tf_op jit(solution)/shard_map/ppermute | solution.py:332
  40.7 0.9 copy-done.4
  41.6 0.8 copy-done.6
  42.5 4.4 %collective-permute-start = (s32[48,128]{1,0:T(8,128)S(1)}, s32[48,128]{1,0:T(8,128)S(1)}, u32[]{:S(2)}, u32[]{:S(2)}) collective-permute-start(s32[48,128]{1,0:T(8,128)S(1)} %shard_map.122.b0_ref), channel_id=1, source_target_pairs={{128,0},{256,128},{384,256},{0,384},{129,1},{257,129},{385,257},{1... | collective-permute-start | bytes 73736 | tf_op jit(solution)/shard_map/ppermute | solution.py:320
  46.9 2.4 %collective-permute-start.1 = (s32[48,128]{1,0:T(8,128)S(1)}, s32[48,128]{1,0:T(8,128)S(1)}, u32[]{:S(2)}, u32[]{:S(2)}) collective-permute-start(s32[48,128]{1,0:T(8,128)S(1)} %shard_map.122.b0_ref), channel_id=1, source_target_pairs={{256,0},{384,128},{0,256},{128,384},{257,1},{385,129},{1,257},{129... | collective-permute-start | bytes 73736 | tf_op jit(solution)/shard_map/ppermute | solution.py:320
  49.3 2.5 %collective-permute-start.2 = (s32[48,128]{1,0:T(8,128)S(1)}, s32[48,128]{1,0:T(8,128)S(1)}, u32[]{:S(2)}, u32[]{:S(2)}) collective-permute-start(s32[48,128]{1,0:T(8,128)S(1)} %shard_map.122.b0_ref), channel_id=1, source_target_pairs={{384,0},{0,128},{128,256},{256,384},{385,1},{1,129},{129,257},{257... | collective-permute-start | bytes 73736 | tf_op jit(solution)/shard_map/ppermute | solution.py:320
  51.9 1.0 collective-permute-done.1.b2_ref
  52.9 2.1 %collective-permute-done.2.b3_ref = s32[48,128]{1,0:T(8,128)S(1)} collective-permute-done((s32[48,128]{1,0:T(8,128)S(1)}, s32[48,128]{1,0:T(8,128)S(1)}, u32[]{:S(2)}, u32[]{:S(2)}) %collective-permute-start.2) | collective-permute-done | bytes 24608 | tf_op jit(solution)/shard_map/ppermute | solution.py:320
  55.1 3.3 %shard_map.123.counts_ref = bf16[6,512,512]{2,1,0:T(8,128)(2,1)S(1)} custom-call(s32[2]{0:T(128)S(1)} %pad_add_fusion.where_ref, s32[48,128]{1,0:T(8,128)S(1)} %shard_map.122.b0_ref, s32[48,128]{1,0:T(8,128)S(1)} %collective-permute-done.b1_ref, s32[48,128]{1,0:T(8,128)S(1)} %collective-permute-done.1.b2_ref, s32[48,128]{1,0:T(8,128)S(1)} %collective-permute-done.2.b3_ref), custom_call_target="tpu_custom_call" | custom-call | tf_op jit(solution)/shard_map/pallas_call | solution.py:287
  58.4 3.2 %shard_map.124 = bf16[16,6,32,128]{3,2,1,0:T(8,128)(2,1)S(1)} custom-call(bf16[6,512,512]{2,1,0:T(8,128)(2,1)S(1)} %shard_map.123.counts_ref, bf16[8,6,32,128]{3,2,1,0:T(8,128)(2,1)} %all_to_all.35.mine_ref, bf16[8,6,32,128]{3,2,1,0:T(8,128)(2,1)} %collective-permute-done.3.other_ref), custom_call_target="tpu_custom_call" | custom-call | tf_op jit(solution)/shard_map/pallas_call | solution.py:287
  61.6 16.8 %all_to_all.36 = bf16[16,6,32,128]{3,2,1,0:T(8,128)(2,1)S(1)} all-to-all(bf16[16,6,32,128]{3,2,1,0:T(8,128)(2,1)S(1)} %shard_map.124), channel_id=1, replica_groups=mesh['x'=4,'core'=2,'y'=4,'zhi'=2,'sub'=8] {'x','y'}, dimensions={0} | all-to-all | bytes 1572864 | tf_op jit(solution)/shard_map/all_to_all | solution.py:280
  79.2 7.3 %all-to-all-start.2 = ((bf16[2,4,6,16,128]{4,3,2,1,0:T(8,128)(2,1)}), bf16[2,4,6,16,128]{4,3,2,1,0:T(8,128)(2,1)}, u32[]{:S(2)}, u32[]{:S(2)}) async-start(bf16[2,4,6,16,128]{4,3,2,1,0:T(8,128)(2,1)} %copy-done.2), calls=%async_computation.2 | async-start | bytes 393216 | tf_op jit(solution)/shard_map/all_to_all | solution.py:280
  86.6 0.7 copy.21
  88.1 13.0 %all-to-all-done.2.near_ref = bf16[2,4,6,16,128]{4,3,2,1,0:T(8,128)(2,1)} async-done(((bf16[2,4,6,16,128]{4,3,2,1,0:T(8,128)(2,1)}), bf16[2,4,6,16,128]{4,3,2,1,0:T(8,128)(2,1)}, u32[]{:S(2)}, u32[]{:S(2)}) %all-to-all-start.2) | async-done | bytes 196640 | tf_op jit(solution)/shard_map/all_to_all | solution.py:280
  101.1 1.7 copy-done.1
  102.8 1.1 copy-done.3
  103.8 0.7 copy-done.5
  104.6 0.7 copy-done.7
  105.3 0.7 copy-done.8
  106.6 7.1 %shard_map.126 = (f32[16,1]{1,0:T(8,128)S(1)}, bf16[2,4,6,16,128]{4,3,2,1,0:T(8,128)(2,1)S(1)}) custom-call(bf16[2,4,6,16,128]{4,3,2,1,0:T(8,128)(2,1)} %all-to-all-done.2.near_ref, f32[16,1]{1,0:T(8,128)S(1)} %copy.22.labels_ref, bf16[2,48,48]{2,1,0:T(8,128)(2,1)S(1)} %copy-done.5, bf16[2,384,384]{2,1,0:T(8,128)(2,1)S(1)} %copy-done.3, ...), custom_call_target="tpu_custom_call" | custom-call | tf_op jit(solution)/shard_map/pallas_call | solution.py:287
  113.8 17.0 %all_to_all.37 = bf16[2,4,6,16,128]{4,3,2,1,0:T(8,128)(2,1)S(1)} all-to-all(bf16[2,4,6,16,128]{4,3,2,1,0:T(8,128)(2,1)S(1)} %get-tuple-element.7), channel_id=1, replica_groups=mesh['x'=4,'core'=2,'y'=4,'zhi'=2,'sub'=8] {'zhi'}, dimensions={0} | all-to-all | bytes 393216 | tf_op jit(solution)/shard_map/all_to_all | solution.py:280
  130.9 15.1 %all_to_all.38.moved_ref = bf16[16,6,32,128]{3,2,1,0:T(8,128)(2,1)S(1)} all-to-all(bf16[16,6,32,128]{3,2,1,0:T(8,128)(2,1)S(1)} %bitcast.17), channel_id=1, replica_groups=mesh['x'=4,'core'=2,'y'=4,'zhi'=2,'sub'=8] {'x','y'}, dimensions={0} | all-to-all | bytes 1572864 | tf_op jit(solution)/shard_map/all_to_all | solution.py:280
  146.0 1.8 shard_map.127
  147.8 5.2 %collective-permute-start.4 = (bf16[8,6,32,128]{3,2,1,0:T(8,128)(2,1)S(1)}, bf16[8,6,32,128]{3,2,1,0:T(8,128)(2,1)S(1)}, u32[]{:S(2)}, u32[]{:S(2)}) collective-permute-start(bf16[8,6,32,128]{3,2,1,0:T(8,128)(2,1)S(1)} %get-tuple-element.9), channel_id=1, source_target_pairs={{0,64},{64,0},{1,65},{65,1},{2,66},{66,2},{3,67},{67,3},{4,68},{68... | collective-permute-start | bytes 1179656 | tf_op jit(solution)/shard_map/ppermute | solution.py:378
  153.0 1.3 collective-permute-done.4.right_ref
  154.4 27.8 %all_to_all.39 = bf16[8,6,32,128]{3,2,1,0:T(8,128)(2,1)S(1)} all-to-all(bf16[8,6,32,128]{3,2,1,0:T(8,128)(2,1)S(1)} %shard_map.128), channel_id=1, replica_groups=mesh['x'=4,'core'=2,'y'=4,'zhi'=2,'sub'=8] {'sub'}, dimensions={0} | all-to-all | bytes 786432 | tf_op jit(solution)/shard_map/all_to_all | solution.py:280
  182.3 0.8 broadcast_in_dim.20
  183.1 6.4 %all-to-all-start.6 = ((bf16[8,6,32,128]{3,2,1,0:T(8,128)(2,1)}), bf16[8,6,32,128]{3,2,1,0:T(8,128)(2,1)S(1)}, u32[]{:S(2)}, u32[]{:S(2)}) async-start(bf16[8,6,32,128]{3,2,1,0:T(8,128)(2,1)} %broadcast_in_dim.20), calls=%async_computation.6 | async-start | bytes 786432 | tf_op jit(solution)/shard_map/all_to_all | solution.py:280
  190.1 7.5 %all-to-all-done.6 = bf16[8,6,32,128]{3,2,1,0:T(8,128)(2,1)S(1)} async-done(((bf16[8,6,32,128]{3,2,1,0:T(8,128)(2,1)}), bf16[8,6,32,128]{3,2,1,0:T(8,128)(2,1)S(1)}, u32[]{:S(2)}, u32[]{:S(2)}) %all-to-all-start.6) | async-done | bytes 393248 | tf_op jit(solution)/shard_map/all_to_all | solution.py:280
  197.6 1.0 copy_convert_fusion
  (32 shorter events, 3.5 us)
Async XLA Ops:
  0.6 1.0 copy-start
  33.9 24.5 %collective-permute-start.3 = (bf16[8,6,32,128]{3,2,1,0:T(8,128)(2,1)}, bf16[8,6,32,128]{3,2,1,0:T(8,128)(2,1)}, u32[]{:S(2)}, u32[]{:S(2)}) collective-permute-start(bf16[8,6,32,128]{3,2,1,0:T(8,128)(2,1)} %all_to_all.35.mine_ref), channel_id=1, source_target_pairs={{0,64},{64,0},{1,65},{65,1},{2,66},{66,2},{3,67},{67,3},{4,68},{68... | collective-permute-start | bytes 1179656 | tf_op jit(solution)/shard_map/ppermute | solution.py:332
  40.7 0.9 copy-start.4
  41.6 0.8 copy-start.6
  42.5 9.4 %collective-permute-start = (s32[48,128]{1,0:T(8,128)S(1)}, s32[48,128]{1,0:T(8,128)S(1)}, u32[]{:S(2)}, u32[]{:S(2)}) collective-permute-start(s32[48,128]{1,0:T(8,128)S(1)} %shard_map.122.b0_ref), channel_id=1, source_target_pairs={{128,0},{256,128},{384,256},{0,384},{129,1},{257,129},{385,257},{1... | collective-permute-start | bytes 73736 | tf_op jit(solution)/shard_map/ppermute | solution.py:320
  46.9 6.1 %collective-permute-start.1 = (s32[48,128]{1,0:T(8,128)S(1)}, s32[48,128]{1,0:T(8,128)S(1)}, u32[]{:S(2)}, u32[]{:S(2)}) collective-permute-start(s32[48,128]{1,0:T(8,128)S(1)} %shard_map.122.b0_ref), channel_id=1, source_target_pairs={{256,0},{384,128},{0,256},{128,384},{257,1},{385,129},{1,257},{129... | collective-permute-start | bytes 73736 | tf_op jit(solution)/shard_map/ppermute | solution.py:320
  49.3 5.8 %collective-permute-start.2 = (s32[48,128]{1,0:T(8,128)S(1)}, s32[48,128]{1,0:T(8,128)S(1)}, u32[]{:S(2)}, u32[]{:S(2)}) collective-permute-start(s32[48,128]{1,0:T(8,128)S(1)} %shard_map.122.b0_ref), channel_id=1, source_target_pairs={{384,0},{0,128},{128,256},{256,384},{385,1},{1,129},{129,257},{257... | collective-permute-start | bytes 73736 | tf_op jit(solution)/shard_map/ppermute | solution.py:320
  58.3 28.1 %copy-start.11 = (f32[16]{0:T(128)S(1)}, f32[16]{0:T(128)}, u32[]{:S(2)}) copy-start(f32[16]{0:T(128)} %param.14) | copy-start | bytes 196
  58.4 29.0 %copy-start.10 = (bf16[2,48,8]{1,2,0:T(8,128)(2,1)S(1)}, bf16[2,48,8]{1,2,0:T(8,128)(2,1)}, u32[]{:S(2)}) copy-start(bf16[2,48,8]{1,2,0:T(8,128)(2,1)} %param.15) | copy-start | bytes 4612
  78.5 0.7 copy-start.2
  79.2 21.9 %all-to-all-start.2 = ((bf16[2,4,6,16,128]{4,3,2,1,0:T(8,128)(2,1)}), bf16[2,4,6,16,128]{4,3,2,1,0:T(8,128)(2,1)}, u32[]{:S(2)}, u32[]{:S(2)}) async-start(bf16[2,4,6,16,128]{4,3,2,1,0:T(8,128)(2,1)} %copy-done.2), calls=%async_computation.2 | async-start | bytes 393216 | tf_op jit(solution)/shard_map/all_to_all | solution.py:280
  101.1 1.7 copy-start.1
  102.8 1.1 copy-start.3
  103.8 0.7 copy-start.5
  104.6 0.7 copy-start.7
  105.3 0.7 copy-start.8
  106.0 0.7 copy-start.9
  147.8 6.6 %collective-permute-start.4 = (bf16[8,6,32,128]{3,2,1,0:T(8,128)(2,1)S(1)}, bf16[8,6,32,128]{3,2,1,0:T(8,128)(2,1)S(1)}, u32[]{:S(2)}, u32[]{:S(2)}) collective-permute-start(bf16[8,6,32,128]{3,2,1,0:T(8,128)(2,1)S(1)} %get-tuple-element.9), channel_id=1, source_target_pairs={{0,64},{64,0},{1,65},{65,1},{2,66},{66,2},{3,67},{67,3},{4,68},{68... | collective-permute-start | bytes 1179656 | tf_op jit(solution)/shard_map/ppermute | solution.py:378
  183.1 14.5 %all-to-all-start.6 = ((bf16[8,6,32,128]{3,2,1,0:T(8,128)(2,1)}), bf16[8,6,32,128]{3,2,1,0:T(8,128)(2,1)S(1)}, u32[]{:S(2)}, u32[]{:S(2)}) async-start(bf16[8,6,32,128]{3,2,1,0:T(8,128)(2,1)} %broadcast_in_dim.20), calls=%async_computation.6 | async-start | bytes 786432 | tf_op jit(solution)/shard_map/all_to_all | solution.py:280

commit v3 on v2

--- a/solution.py
+++ b/solution.py
@@ -8,6 +8,7 @@
 
 REP = ("x", "core")
 GRP = ("y", "zhi")
+SUB = ("sub",)
 DEAD = 4095
 FIELDS, BATCH, WIDTH, RANK, NF = 48, 16, 128, 8, 12
 VMEM_LIMIT = 48 * 1024 * 1024
@@ -46,22 +47,33 @@
 
 
 def dense_kernel(
-    near_ref, labels_ref, mix_ref, mlp_in_ref, mlp_out_ref, gain_fm_ref, gain_out_ref, head_ref,
+    near_ref, labels_ref, mix_hbm, mlp_in_hbm, mlp_out_hbm, gain_fm_hbm, gain_out_hbm, head_hbm,
     loss_ref, back_ref,
     x_ref, t_ref, xhat_ref, rstd_ref, xb_ref, d_ref,
+    mix_ref, mlp_in_ref, mlp_out_ref, gain_fm_ref, gain_out_ref, head_ref, fetch_sems,
 ):
     f32, bf16 = jnp.float32, jnp.bfloat16
-    zs, ys, tables = near_ref.shape[:3]
     layers = mix_ref.shape[0]
-    block = tables * BATCH
     rows = FIELDS * BATCH
     chunk = 128
     lane = lax.broadcasted_iota(jnp.int32, (BATCH, WIDTH), 1) // RANK
-
-    for y in range(ys):
-        for z in range(zs):
-            at = (y * zs + z) * block
-            xb_ref[0, at : at + block] = near_ref[z, y].reshape(block, WIDTH)
+    fetches = [
+        pltpu.make_async_copy(source, target, fetch_sems.at[i])
+        for i, (source, target) in enumerate(
+            (
+                (mix_hbm, mix_ref),
+                (gain_fm_hbm, gain_fm_ref),
+                (mlp_in_hbm, mlp_in_ref),
+                (mlp_out_hbm, mlp_out_ref),
+                (gain_out_hbm, gain_out_ref),
+                (head_hbm, head_ref),
+            )
+        )
+    ]
+    for fetch in fetches:
+        fetch.start()
+
+    xb_ref[0] = near_ref[...].reshape(rows, WIDTH)
     x_ref[...] = xb_ref[0].astype(f32)
 
     def example(ref, e):
@@ -70,6 +82,8 @@
     saved = []
     for layer in range(layers):
         across = jnp.concatenate([example(x_ref, e).astype(bf16) for e in range(BATCH)], axis=1)
+        if layer == 0:
+            fetches[0].wait()
         mixed = dot(mix_ref[layer], across, ((1,), (0,)))
         for e in range(BATCH):
             t_ref[pl.ds(e, FIELDS, stride=BATCH), :] = mixed[:, e * WIDTH : (e + 1) * WIDTH]
@@ -90,10 +104,16 @@
         flat = flat - center
         rstd_fm = lax.rsqrt(jnp.mean(flat * flat, axis=1, keepdims=True) + 1e-05)
         nhat = flat * rstd_fm
+        if layer == 0:
+            fetches[1].wait()
+            fetches[2].wait()
         normed = (nhat * gain_fm_ref[layer : layer + 1]).astype(bf16)
         z = dot(normed, mlp_in_ref[layer], ((1,), (0,)))
         gate = jax.nn.sigmoid(z)
         hidden = (z * gate).astype(bf16)
+        if layer == 0:
+            fetches[3].wait()
+            fetches[4].wait()
         machine = dot(hidden, mlp_out_ref[layer], ((1,), (0,)))
         for n in range(NF):
             t_ref[n * BATCH : (n + 1) * BATCH] = machine[:, n * WIDTH : (n + 1) * WIDTH]
@@ -112,12 +132,20 @@
         saved.append((summary, nhat, rstd_fm, z, gate))
 
     acc = jnp.zeros((BATCH, WIDTH), f32)
+    fetches[5].wait()
     head = head_ref[...].astype(f32)
     for t in range(FIELDS):
         acc = acc + x_ref[t * BATCH : (t + 1) * BATCH] * head[t : t + 1]
     logit = jnp.sum(acc, axis=1, keepdims=True)
-    labels = labels_ref[...]
-    loss_ref[...] = jnp.maximum(logit, 0.0) + jnp.log1p(jnp.exp(-jnp.abs(logit))) - labels * logit
+    square = (BATCH, BATCH)
+    same = lax.broadcasted_iota(jnp.int32, square, 0) == lax.broadcasted_iota(jnp.int32, square, 1)
+    labels = jnp.sum(
+        jnp.where(same, jnp.broadcast_to(labels_ref[...], square), 0.0), axis=1, keepdims=True
+    )
+    loss = jnp.maximum(logit, 0.0) + jnp.log1p(jnp.exp(-jnp.abs(logit))) - labels * logit
+    loss_ref[...] = jnp.sum(
+        jnp.where(same, jnp.broadcast_to(loss, square), 0.0), axis=0, keepdims=True
+    )
     dlogit = jnp.broadcast_to(jax.nn.sigmoid(logit) - labels, (BATCH, WIDTH))
     for t in range(FIELDS):
         x_ref[t * BATCH : (t + 1) * BATCH] = (dlogit * head[t : t + 1]).astype(bf16).astype(f32)
@@ -172,10 +200,7 @@
             dx = x_ref[cut] + t_ref[cut] + dot(d_ref[cut], summary, ((1,), (0,)))
             x_ref[cut] = dx.astype(bf16).astype(f32)
 
-    for y in range(ys):
-        for z in range(zs):
-            at = (y * zs + z) * block
-            back_ref[z, y] = x_ref[at : at + block].astype(bf16).reshape(tables, BATCH, WIDTH)
+    back_ref[...] = x_ref[...].astype(bf16).reshape(back_ref.shape)
 
 
 def mix_of(proj, compress):
@@ -187,13 +212,13 @@
 def counts_kernel(where_ref, b0_ref, b1_ref, b2_ref, b3_ref, counts_ref, idx_ref):
     tables, local, examples = counts_ref.shape
     column, core = where_ref[0], where_ref[1]
-    for src, bags_ref in enumerate((b0_ref, b1_ref, b2_ref, b3_ref)):
+    for hop, bags_ref in enumerate((b0_ref, b1_ref, b2_ref, b3_ref)):
         coded = bags_ref[...]
         mine = ((coded >> 6) & 3) == column
         side = ((coded >> 5) & 1) ^ core
         spot = (side << 8) | ((coded >> 8) << 5) | (coded & 31)
         spot = jnp.where(mine & (coded < DEAD), spot, -1)
-        at = pl.multiple_of(((column + src) & 3) * 128, 128)
+        at = pl.multiple_of(((column + hop) & 3) * 128, 128)
         idx_ref[:, pl.ds(at, 128)] = spot.astype(jnp.float32)
     steps = local // 32
     ids = [
@@ -234,26 +259,18 @@
             [ref[:, table].reshape(local // 2, width) for ref in (mine_ref, other_ref)], axis=0
         )
         part = dot(counts_ref[table], rows, ((0,), (0,)))
-        pools_ref[:, table] = part.astype(jnp.bfloat16).reshape(examples // 32, 32, width)
+        pools_ref[:, table] = part.astype(jnp.bfloat16).reshape(examples // BATCH, BATCH, width)
         return carry
 
     lax.fori_loop(0, tables, per_table, 0)
 
 
 def merge_kernel(moved_ref, out_ref):
-    columns, ys, tables = moved_ref.shape[:3]
-
-    def per_table(table, carry):
-        for y in range(ys):
-            total = moved_ref[0, y, table].astype(jnp.float32)
-            for column in range(1, columns):
-                total = total + moved_ref[column, y, table].astype(jnp.float32)
-            total = total.astype(jnp.bfloat16)
-            out_ref[0, y, table] = total[:BATCH]
-            out_ref[1, y, table] = total[BATCH:]
-        return carry
-
-    lax.fori_loop(0, tables, per_table, 0)
+    for at in range(out_ref.shape[0]):
+        total = moved_ref[0, at].astype(jnp.float32)
+        for source in range(1, moved_ref.shape[0]):
+            total = total + moved_ref[source, at].astype(jnp.float32)
+        out_ref[at] = total.astype(jnp.bfloat16)
 
 
 def grads_kernel(counts_ref, moved_ref, mine_ref, other_ref):
@@ -271,26 +288,27 @@
 
 
 def add_kernel(left_ref, right_ref, out_ref):
-    for shard in range(out_ref.shape[0]):
-        total = left_ref[shard].astype(jnp.float32) + right_ref[shard].astype(jnp.float32)
-        out_ref[shard] = total.astype(jnp.bfloat16)
+    for at in range(out_ref.shape[0]):
+        total = left_ref[at].astype(jnp.float32) + right_ref[at].astype(jnp.float32)
+        out_ref[at] = total.astype(jnp.bfloat16)
 
 
 def swap(values, axes):
     return lax.all_to_all(values, axes, split_axis=0, concat_axis=0, tiled=True)
 
 
-def call(kernel, out_shape, ins, args, scratch=()):
+def call(kernel, out_shape, ins, args, scratch=(), limit=VMEM_LIMIT):
     vmem = pl.BlockSpec(memory_space=pltpu.VMEM)
     smem = pl.BlockSpec(memory_space=pltpu.SMEM)
+    hbm = pl.BlockSpec(memory_space=pltpu.HBM)
     many = isinstance(out_shape, tuple)
     return pl.pallas_call(
         kernel,
         out_shape=out_shape,
-        in_specs=[smem if kind == "s" else vmem for kind in ins],
+        in_specs=[{"s": smem, "v": vmem, "h": hbm}[kind] for kind in ins],
         out_specs=(vmem,) * len(out_shape) if many else vmem,
         scratch_shapes=list(scratch),
-        compiler_params=pltpu.CompilerParams(vmem_limit_bytes=VMEM_LIMIT),
+        compiler_params=pltpu.CompilerParams(vmem_limit_bytes=limit),
     )(*args)
 
 
@@ -301,15 +319,19 @@
     shape = jax.ShapeDtypeStruct
     tables, rows_dev, width = table_rows.shape
     layers = proj.shape[0]
-    sub = lax.axis_index("sub")
     rep = lax.axis_index(REP)
+    sub = lax.axis_index(SUB)
     column, core = lax.axis_index("x"), lax.axis_index("core")
-    columns, cores, subs, ys, zs = 4, 2, 8, 4, 2
+    columns, cores, shards, groups = 4, 2, 8, 8
     reps = columns * cores
     part_rows = rows_dev // reps
-    examples = columns * ys * zs * BATCH
+    examples = columns * groups * BATCH
     across = [(0, 1), (1, 0)]
 
+    part = lax.dynamic_slice_in_dim(table_rows, rep * part_rows, part_rows, axis=1)
+    gathered = swap(
+        jnp.broadcast_to(part.reshape(1, *part.shape), (shards, tables, part_rows, width)), SUB
+    )
     coded = call(
         pick_kernel,
         shape((tables * 8, 128), jnp.int32),
@@ -320,8 +342,6 @@
         lax.ppermute(coded, "x", [((i + hop) % columns, i) for i in range(columns)])
         for hop in range(1, columns)
     ]
-    part = lax.dynamic_slice_in_dim(table_rows, rep * part_rows, part_rows, axis=1)
-    gathered = swap(jnp.broadcast_to(part, (subs, tables, part_rows, width)), "sub")
     counts = call(
         counts_kernel,
         shape((tables, 2 * rows_dev, examples), bf16),
@@ -329,31 +349,31 @@
         (jnp.stack([column, core]), *bags),
         [pltpu.VMEM((tables * 8, examples), f32)],
     )
+    mix = mix_of(proj, compress)
+    gathered, counts, mix = lax.optimization_barrier((gathered, counts, mix))
     other = lax.ppermute(gathered, "core", across)
     pools = call(
         pool_kernel,
-        shape((columns * ys, tables, zs * BATCH, width), bf16),
+        shape((columns * groups, tables, BATCH, width), bf16),
         "vvv",
         (counts, gathered, other),
     )
-    moved = swap(pools, ("x", "y"))
+    moved = swap(pools, "x")
+    per_group = shape((groups, tables, BATCH, width), bf16)
     merged = call(
-        merge_kernel,
-        shape((zs, ys, tables, BATCH, width), bf16),
-        "v",
-        (moved.reshape(columns, ys, tables, zs * BATCH, width),),
-    )
-    near = swap(merged, "zhi")
+        merge_kernel, per_group, "v", (moved.reshape(columns, groups, tables, BATCH, width),)
+    )
+    near = swap(merged, GRP)
 
     rows = FIELDS * BATCH
     losses, back = call(
         dense_kernel,
-        (shape((BATCH, 1), f32), shape(near.shape, bf16)),
-        "v" * 8,
+        (shape((1, BATCH), f32), shape(near.shape, bf16)),
+        "vv" + "h" * 6,
         (
             near,
-            labels.reshape(BATCH, 1),
-            mix_of(proj, compress),
+            labels.reshape(1, BATCH),
+            mix,
             mlp_in,
             mlp_out,
             gain_fm,
@@ -367,16 +387,24 @@
             pltpu.VMEM((layers, rows, 1), f32),
             pltpu.VMEM((layers + 1, rows, WIDTH), bf16),
             pltpu.VMEM((rows, WIDTH), bf16),
+            pltpu.VMEM((layers, FIELDS, FIELDS), bf16),
+            pltpu.VMEM(mlp_in.shape, bf16),
+            pltpu.VMEM(mlp_out.shape, bf16),
+            pltpu.VMEM(gain_fm.shape, f32),
+            pltpu.VMEM(gain_out.shape, f32),
+            pltpu.VMEM(head.shape, bf16),
+            pltpu.SemaphoreType.DMA((6,)),
         ],
-    )
-
-    back = jnp.transpose(swap(back, "zhi"), (1, 2, 0, 3, 4)).reshape(1, ys, tables, -1, width)
-    back = jnp.broadcast_to(back, (columns, *back.shape[1:]))
-    returned = swap(back.reshape(columns * ys, tables, -1, width), ("x", "y"))
-    piece = shape((subs, tables, part_rows, width), bf16)
+        60 * 1024 * 1024,
+    )
+
+    back = swap(back, GRP)
+    back = jnp.broadcast_to(back, (columns, *back.shape))
+    returned = swap(back.reshape(columns * groups, tables, BATCH, width), "x")
+    piece = shape((shards, tables, part_rows, width), bf16)
     mine, other = call(grads_kernel, (piece, piece), "vv", (counts, returned))
     other = lax.ppermute(other, "core", across)
-    pieces = swap(call(add_kernel, piece, "vv", (mine, other)), "sub")
+    pieces = swap(call(add_kernel, piece, "vv", (mine, other)), SUB)
     own = jnp.sum(pieces.astype(f32), axis=0).astype(bf16)
     spread = swap(jnp.broadcast_to(own, (reps, tables, part_rows, width)), REP)
     row_grads = jnp.transpose(spread, (1, 0, 2, 3)).reshape(tables, rows_dev, width)
@@ -384,15 +412,17 @@
 
 
 def solution(mesh):
-    view = Mesh(mesh.devices.reshape(4, 2, 4, 2, 8), ("x", "core", "y", "zhi", "sub"))
+    view = Mesh(
+        mesh.devices.reshape(4, 2, 4, 2, 8), ("x", "core", "y", "zhi", "sub")
+    )
     return jax.shard_map(
         per_device,
         mesh=view,
         in_specs=(
-            P(GRP, "sub", None),
+            P(GRP, SUB, None),
             P(REP, GRP, None),
             P(REP, GRP),
-            P(REP + GRP + ("sub",)),
+            P(REP + GRP + SUB),
             P(),
             P(),
             P(),
@@ -401,6 +431,6 @@
             P(),
             P(),
         ),
-        out_specs=(P(REP + GRP + ("sub",)), P(GRP, "sub", None)),
+        out_specs=(P(REP + GRP + SUB), P(GRP, SUB, None)),
         check_vma=False,
     )

time: 200 us -> 182 us (0.910)
  waiting for transfers between devices: 25 us -> 2.88 us
  local copies, waits for them, and re-layouts: 10.8 us -> 4.46 us
  blocking collectives: 109 us -> 114 us
  starting transfers between devices: 35 us -> 39.3 us
    all_to_all x2 -> x1, waiting for transfers between devices: 20.5 us -> 0.01 us  [swap(): return lax.all_to_all(values, axes, split_axis=0, concat_axis=0, tiled=True)]
    unnamed x25 -> x7, local copies, waits for them, and re-layouts: 9.61 us -> 3.39 us
    all_to_all x5 -> x6, blocking collectives: 109 us -> 114 us  [swap(): return lax.all_to_all(values, axes, split_axis=0, concat_axis=0, tiled=True)]
    ppermute x3, waiting for transfers between devices: 3.18 us -> 0.01 us  [per_device(): lax.ppermute(coded, 'x', [((i + hop) % columns, i) for i in range(columns)])]
    ppermute x1, starting transfers between devices: 5.23 us -> 7.49 us  [per_device(): other = lax.ppermute(other, 'core', across)]
    all_to_all x2 -> x1, starting transfers between devices: 13.7 us -> 13.1 us  [swap(): return lax.all_to_all(values, axes, split_axis=0, concat_axis=0, tiled=True)]
  transfers between devices with their start and end apart: 7 -> 6, of which waited for: 5 -> 2; matrix products, arithmetic and copies ran while one was open for 1% -> 1% of each run, Pallas kernels for 2% -> 2%
where the time goes in v3:
time: 182 us; the launch traced here: 181 us
  blocking collectives  114 us (63%)
  starting transfers between devices  39.3 us (22%)
  Pallas kernels  17.2 us (9%)
  local copies, waits for them, and re-layouts  4.46 us (2%)
  waiting for transfers between devices  2.88 us (2%)
  other arithmetic  2.47 us (1%)
    all_to_all x6, blocking collectives, swap(): return lax.all_to_all(values, axes, split_axis=0, concat_axis=0, tiled=True)  114 us
    pallas_call x7, Pallas kernels, call(): pl.pallas_call(kernel, out_shape=out_shape, in_specs=[{'s': smem, 'v': vm...  17.2 us
    all_to_all x1, starting transfers between devices, swap(): return lax.all_to_all(values, axes, split_axis=0, concat_axis=0, tiled=True)  13.1 us
    ppermute x3, starting transfers between devices, per_device(): lax.ppermute(coded, 'x', [((i + hop) % columns, i) for i in range(columns)])  10.5 us
    ppermute x1, starting transfers between devices, per_device(): other = lax.ppermute(gathered, 'core', across)  8.16 us
    ppermute x1, starting transfers between devices, per_device(): other = lax.ppermute(other, 'core', across)  7.49 us
  transfers between devices with their start and end apart: 6, of which 2 were waited for; matrix products, arithmetic and copies ran while one was open for 1% of the time, Pallas kernels for 2%

profile of v3, /device:TPU:1, one launch (start us, length us, event | category | flops | bytes accessed | tf_op | source)
XLA Modules:
  0.0 181.1 jit_solution(14166901488103611491)
XLA Ops:
  0.7 1.0 copy-done
  1.6 0.8 broadcast_in_dim.14
  2.4 13.1 %all-to-all-start = ((bf16[8,6,32,128]{3,2,1,0:T(8,128)(2,1)}), bf16[8,6,32,128]{3,2,1,0:T(8,128)(2,1)}, u32[]{:S(2)}, u32[]{:S(2)}) async-start(bf16[8,6,32,128]{3,2,1,0:T(8,128)(2,1)} %broadcast_in_dim.14), calls=%async_computation | async-start | bytes 786432 | tf_op jit(solution)/shard_map/all_to_all | solution.py:297
  15.5 0.9 copy-done.1
  16.5 0.8 copy-done.2
  17.2 0.1 shard_map.122.b0_ref
  17.3 3.1 %collective-permute-start.2 = (s32[48,128]{1,0:T(8,128)S(1)}, s32[48,128]{1,0:T(8,128)S(1)}, u32[]{:S(2)}, u32[]{:S(2)}) collective-permute-start(s32[48,128]{1,0:T(8,128)S(1)} %shard_map.122.b0_ref), channel_id=1, source_target_pairs={{384,0},{0,128},{128,256},{256,384},{385,1},{1,129},{129,257},{257... | collective-permute-start | bytes 73736 | tf_op jit(solution)/shard_map/ppermute | solution.py:342
  20.5 4.4 %collective-permute-start.1 = (s32[48,128]{1,0:T(8,128)S(1)}, s32[48,128]{1,0:T(8,128)S(1)}, u32[]{:S(2)}, u32[]{:S(2)}) collective-permute-start(s32[48,128]{1,0:T(8,128)S(1)} %shard_map.122.b0_ref), channel_id=1, source_target_pairs={{256,0},{384,128},{0,256},{128,384},{257,1},{385,129},{1,257},{129... | collective-permute-start | bytes 73736 | tf_op jit(solution)/shard_map/ppermute | solution.py:342
  24.8 3.1 %collective-permute-start = (s32[48,128]{1,0:T(8,128)S(1)}, s32[48,128]{1,0:T(8,128)S(1)}, u32[]{:S(2)}, u32[]{:S(2)}) collective-permute-start(s32[48,128]{1,0:T(8,128)S(1)} %shard_map.122.b0_ref), channel_id=1, source_target_pairs={{128,0},{256,128},{384,256},{0,384},{129,1},{257,129},{385,257},{1... | collective-permute-start | bytes 73736 | tf_op jit(solution)/shard_map/ppermute | solution.py:342
  27.9 0.7 copy.15
  28.6 0.1 pad.1.clone
  28.7 1.4 pad_maximum_fusion.mix_hbm
  30.1 0.1 pad_add_fusion.where_ref
  30.2 3.3 %shard_map.123.counts_ref = bf16[6,512,512]{2,1,0:T(8,128)(2,1)S(1)} custom-call(s32[2]{0:T(128)S(1)} %pad_add_fusion.where_ref, s32[48,128]{1,0:T(8,128)S(1)} %shard_map.122.b0_ref, s32[48,128]{1,0:T(8,128)S(1)} %collective-permute-done.b1_ref, s32[48,128]{1,0:T(8,128)S(1)} %collective-permute-done.1.b2_ref, s32[48,128]{1,0:T(8,128)S(1)} %collective-permute-done.2.b3_ref), custom_call_target="tpu_custom_call" | custom-call | tf_op jit(solution)/shard_map/pallas_call | solution.py:305
  33.4 8.2 %collective-permute-start.3 = (bf16[8,6,32,128]{3,2,1,0:T(8,128)(2,1)}, bf16[8,6,32,128]{3,2,1,0:T(8,128)(2,1)S(1)}, u32[]{:S(2)}, u32[]{:S(2)}) collective-permute-start(bf16[8,6,32,128]{3,2,1,0:T(8,128)(2,1)} %all-to-all-done.mine_ref), channel_id=1, source_target_pairs={{0,64},{64,0},{1,65},{65,1},{2,66},{66,2},{3,67},{67,3},{4,68},{68... | collective-permute-start | bytes 1179656 | tf_op jit(solution)/shard_map/ppermute | solution.py:354
  41.6 1.5 collective-permute-done.3.other_ref
  43.1 3.1 %shard_map.124 = bf16[32,6,16,128]{3,2,1,0:T(8,128)(2,1)S(1)} custom-call(bf16[6,512,512]{2,1,0:T(8,128)(2,1)S(1)} %shard_map.123.counts_ref, bf16[8,6,32,128]{3,2,1,0:T(8,128)(2,1)} %all-to-all-done.mine_ref, bf16[8,6,32,128]{3,2,1,0:T(8,128)(2,1)S(1)} %collective-permute-done.3.other_ref), custom_call_target="tpu_custom_call" | custom-call | tf_op jit(solution)/shard_map/pallas_call | solution.py:305
  46.2 15.2 %all_to_all.35 = bf16[32,6,16,128]{3,2,1,0:T(8,128)(2,1)S(1)} all-to-all(bf16[32,6,16,128]{3,2,1,0:T(8,128)(2,1)S(1)} %shard_map.124), channel_id=1, replica_groups=mesh['x'=4,'core'=2,'y'=4,'zhi'=2,'sub'=8] {'x'}, dimensions={0} | all-to-all | bytes 1572864 | tf_op jit(solution)/shard_map/all_to_all | solution.py:297
  61.5 0.1 shard_map.125
  61.6 24.4 %all_to_all.36.near_ref = bf16[8,6,16,128]{3,2,1,0:T(8,128)(2,1)} all-to-all(bf16[8,6,16,128]{3,2,1,0:T(8,128)(2,1)S(1)} %shard_map.125), channel_id=1, replica_groups=mesh['x'=4,'core'=2,'y'=4,'zhi'=2,'sub'=8] {'y','zhi'}, dimensions={0} | all-to-all | bytes 393216 | tf_op jit(solution)/shard_map/all_to_all | solution.py:297
  86.0 8.7 %shard_map.126 = (f32[1,16]{1,0:T(1,128)}, bf16[8,6,16,128]{3,2,1,0:T(8,128)(2,1)}) custom-call(bf16[8,6,16,128]{3,2,1,0:T(8,128)(2,1)} %all_to_all.36.near_ref, f32[1,16]{1,0:T(1,128)} %bitcast.19, bf16[2,48,48]{2,1,0:T(8,128)(2,1)} %pad_maximum_fusion.mix_hbm, bf16[2,384,384]{2,1,0:T(8,128)(2,1)} %mlp_in_hbm.1, bf16[2,384,1536]{2,1,0:T(8,128)(2,1)} %mlp_out_hbm.1, ...), custom_call_target="tpu_custom_call" | custom-call | tf_op jit(solution)/shard_map/pallas_call | solution.py:305
  94.8 17.9 %all_to_all.37 = bf16[8,6,16,128]{3,2,1,0:T(8,128)(2,1)S(1)} all-to-all(bf16[8,6,16,128]{3,2,1,0:T(8,128)(2,1)} %get-tuple-element.13), channel_id=1, replica_groups=mesh['x'=4,'core'=2,'y'=4,'zhi'=2,'sub'=8] {'y','zhi'}, dimensions={0} | all-to-all | bytes 393216 | tf_op jit(solution)/shard_map/all_to_all | solution.py:297
  112.7 0.1 broadcast_in_dim.16
  112.8 10.7 %all_to_all.38.moved_ref = bf16[32,6,16,128]{3,2,1,0:T(8,128)(2,1)S(1)} all-to-all(bf16[32,6,16,128]{3,2,1,0:T(8,128)(2,1)S(1)} %bitcast.16), channel_id=1, replica_groups=mesh['x'=4,'core'=2,'y'=4,'zhi'=2,'sub'=8] {'x'}, dimensions={0} | all-to-all | bytes 1572864 | tf_op jit(solution)/shard_map/all_to_all | solution.py:297
  123.6 1.8 shard_map.127
  125.4 7.5 %collective-permute-start.4 = (bf16[8,6,32,128]{3,2,1,0:T(8,128)(2,1)S(1)}, bf16[8,6,32,128]{3,2,1,0:T(8,128)(2,1)S(1)}, u32[]{:S(2)}, u32[]{:S(2)}) collective-permute-start(bf16[8,6,32,128]{3,2,1,0:T(8,128)(2,1)S(1)} %get-tuple-element.15), channel_id=1, source_target_pairs={{0,64},{64,0},{1,65},{65,1},{2,66},{66,2},{3,67},{67,3},{4,68},{68... | collective-permute-start | bytes 1179656 | tf_op jit(solution)/shard_map/ppermute | solution.py:406
  132.8 1.3 collective-permute-done.4.right_ref
  134.2 0.1 shard_map.128
  134.3 32.3 %all_to_all.39 = bf16[8,6,32,128]{3,2,1,0:T(8,128)(2,1)S(1)} all-to-all(bf16[8,6,32,128]{3,2,1,0:T(8,128)(2,1)S(1)} %shard_map.128), channel_id=1, replica_groups=mesh['x'=4,'core'=2,'y'=4,'zhi'=2,'sub'=8] {'sub'}, dimensions={0} | all-to-all | bytes 786432 | tf_op jit(solution)/shard_map/all_to_all | solution.py:297
  166.6 0.1 broadcast_in_dim.17
  166.7 13.5 %all_to_all.40 = bf16[8,6,32,128]{3,2,1,0:T(8,128)(2,1)S(1)} all-to-all(bf16[8,6,32,128]{3,2,1,0:T(8,128)(2,1)S(1)} %broadcast_in_dim.17), channel_id=1, replica_groups=mesh['x'=4,'core'=2,'y'=4,'zhi'=2,'sub'=8] {'x','core'}, dimensions={0} | all-to-all | bytes 786432 | tf_op jit(solution)/shard_map/all_to_all | solution.py:297
  180.2 1.0 copy_convert_fusion
  (10 shorter events, 0.1 us)
Async XLA Ops:
  0.6 1.0 copy-start
  2.4 31.0 %all-to-all-start = ((bf16[8,6,32,128]{3,2,1,0:T(8,128)(2,1)}), bf16[8,6,32,128]{3,2,1,0:T(8,128)(2,1)}, u32[]{:S(2)}, u32[]{:S(2)}) async-start(bf16[8,6,32,128]{3,2,1,0:T(8,128)(2,1)} %broadcast_in_dim.14), calls=%async_computation | async-start | bytes 786432 | tf_op jit(solution)/shard_map/all_to_all | solution.py:297
  15.5 0.9 copy-start.1
  16.5 0.8 copy-start.2
  17.3 12.8 %collective-permute-start.2 = (s32[48,128]{1,0:T(8,128)S(1)}, s32[48,128]{1,0:T(8,128)S(1)}, u32[]{:S(2)}, u32[]{:S(2)}) collective-permute-start(s32[48,128]{1,0:T(8,128)S(1)} %shard_map.122.b0_ref), channel_id=1, source_target_pairs={{384,0},{0,128},{128,256},{256,384},{385,1},{1,129},{129,257},{257... | collective-permute-start | bytes 73736 | tf_op jit(solution)/shard_map/ppermute | solution.py:342
  20.5 9.7 %collective-permute-start.1 = (s32[48,128]{1,0:T(8,128)S(1)}, s32[48,128]{1,0:T(8,128)S(1)}, u32[]{:S(2)}, u32[]{:S(2)}) collective-permute-start(s32[48,128]{1,0:T(8,128)S(1)} %shard_map.122.b0_ref), channel_id=1, source_target_pairs={{256,0},{384,128},{0,256},{128,384},{257,1},{385,129},{1,257},{129... | collective-permute-start | bytes 73736 | tf_op jit(solution)/shard_map/ppermute | solution.py:342
  24.8 5.3 %collective-permute-start = (s32[48,128]{1,0:T(8,128)S(1)}, s32[48,128]{1,0:T(8,128)S(1)}, u32[]{:S(2)}, u32[]{:S(2)}) collective-permute-start(s32[48,128]{1,0:T(8,128)S(1)} %shard_map.122.b0_ref), channel_id=1, source_target_pairs={{128,0},{256,128},{384,256},{0,384},{129,1},{257,129},{385,257},{1... | collective-permute-start | bytes 73736 | tf_op jit(solution)/shard_map/ppermute | solution.py:342
  33.4 9.7 %collective-permute-start.3 = (bf16[8,6,32,128]{3,2,1,0:T(8,128)(2,1)}, bf16[8,6,32,128]{3,2,1,0:T(8,128)(2,1)S(1)}, u32[]{:S(2)}, u32[]{:S(2)}) collective-permute-start(bf16[8,6,32,128]{3,2,1,0:T(8,128)(2,1)} %all-to-all-done.mine_ref), channel_id=1, source_target_pairs={{0,64},{64,0},{1,65},{65,1},{2,66},{66,2},{3,67},{67,3},{4,68},{68... | collective-permute-start | bytes 1179656 | tf_op jit(solution)/shard_map/ppermute | solution.py:354
  125.4 8.8 %collective-permute-start.4 = (bf16[8,6,32,128]{3,2,1,0:T(8,128)(2,1)S(1)}, bf16[8,6,32,128]{3,2,1,0:T(8,128)(2,1)S(1)}, u32[]{:S(2)}, u32[]{:S(2)}) collective-permute-start(bf16[8,6,32,128]{3,2,1,0:T(8,128)(2,1)S(1)} %get-tuple-element.15), channel_id=1, source_target_pairs={{0,64},{64,0},{1,65},{65,1},{2,66},{66,2},{3,67},{67,3},{4,68},{68... | collective-permute-start | bytes 1179656 | tf_op jit(solution)/shard_map/ppermute | solution.py:406

commit v4 on v3

--- a/solution.py
+++ b/solution.py
@@ -1,3 +1,5 @@
+import functools
+
 import jax
 import jax.numpy as jnp
 from jax import lax
@@ -10,16 +12,27 @@
 GRP = ("y", "zhi")
 SUB = ("sub",)
 DEAD = 4095
+COLUMNS = 4
 FIELDS, BATCH, WIDTH, RANK, NF = 48, 16, 128, 8, 12
-VMEM_LIMIT = 48 * 1024 * 1024
-
-
-def pick_kernel(sub_ref, rows_ref, lens_ref, out_ref):
-    tables, bag, _ = rows_ref.shape
+VMEM_LIMIT = 24 * 1024 * 1024
+DENSE_LIMIT = 56 * 1024 * 1024
+
+
+def pick_kernel(where_ref, rows_hbm, lens_hbm, *refs):
+    outs, (rows_ref, lens_ref, kept_ref, sems) = refs[:COLUMNS], refs[COLUMNS:]
+    fetches = [
+        pltpu.make_async_copy(rows_hbm, rows_ref, sems.at[0]),
+        pltpu.make_async_copy(lens_hbm, lens_ref, sems.at[1]),
+    ]
+    for fetch in fetches:
+        fetch.start()
+    for fetch in fetches:
+        fetch.wait()
+    bag = rows_ref.shape[1]
     slots = lax.broadcasted_iota(jnp.int32, (bag, 128), 0)
     lanes = lax.broadcasted_iota(jnp.int32, (bag, 128), 1)
-    sub = sub_ref[0]
-    for table in range(tables):
+    sub, column = where_ref[0], where_ref[1]
+    for table in range(rows_ref.shape[0]):
         kept = jnp.zeros((bag, 128), jnp.int32)
         for run in range(8):
             cut = slice(run * 128, run * 128 + 128)
@@ -28,7 +41,11 @@
             )
             moved = pltpu.roll(coded, (run * 16 - sub * 16) & 127, 1)
             kept = jnp.where(lanes // 16 == run, moved, kept)
-        out_ref[pl.ds(table * bag, bag), :] = kept
+        kept_ref[table] = kept
+    for hop in range(COLUMNS):
+        target = (column - hop) & (COLUMNS - 1)
+        outs[hop][:bag] = kept_ref[target]
+        outs[hop][bag:] = kept_ref[COLUMNS + (target >> 1)]
 
 
 def dot(a, b, dims):
@@ -47,33 +64,43 @@
 
 
 def dense_kernel(
-    near_ref, labels_ref, mix_hbm, mlp_in_hbm, mlp_out_hbm, gain_fm_hbm, gain_out_hbm, head_hbm,
+    labels_hbm, near_hbm, mix_hbm, gain_fm_hbm, mlp_in_hbm, mlp_out_hbm, gain_out_hbm, head_hbm,
     loss_ref, back_ref,
     x_ref, t_ref, xhat_ref, rstd_ref, xb_ref, d_ref,
-    mix_ref, mlp_in_ref, mlp_out_ref, gain_fm_ref, gain_out_ref, head_ref, fetch_sems,
+    near_ref, mix_ref, gain_fm_ref, mlp_in_ref, mlp_out_ref, gain_out_ref, head_ref, labels_ref, sems,
 ):
     f32, bf16 = jnp.float32, jnp.bfloat16
     layers = mix_ref.shape[0]
     rows = FIELDS * BATCH
     chunk = 128
     lane = lax.broadcasted_iota(jnp.int32, (BATCH, WIDTH), 1) // RANK
-    fetches = [
-        pltpu.make_async_copy(source, target, fetch_sems.at[i])
-        for i, (source, target) in enumerate(
-            (
-                (mix_hbm, mix_ref),
-                (gain_fm_hbm, gain_fm_ref),
-                (mlp_in_hbm, mlp_in_ref),
-                (mlp_out_hbm, mlp_out_ref),
-                (gain_out_hbm, gain_out_ref),
-                (head_hbm, head_ref),
-            )
-        )
-    ]
+    pairs = (
+        (near_hbm, near_ref),
+        (mix_hbm, mix_ref),
+        (gain_fm_hbm, gain_fm_ref),
+        (mlp_in_hbm, mlp_in_ref),
+        (mlp_out_hbm.at[0], mlp_out_ref.at[0]),
+        (gain_out_hbm, gain_out_ref),
+        (mlp_out_hbm.at[1], mlp_out_ref.at[1]),
+        (head_hbm, head_ref),
+        (labels_hbm, labels_ref),
+    )
+    fetches = [pltpu.make_async_copy(*pair, sems.at[i]) for i, pair in enumerate(pairs)]
     for fetch in fetches:
         fetch.start()
 
-    xb_ref[0] = near_ref[...].reshape(rows, WIDTH)
+    fetches[0].wait()
+    groups = near_ref.shape[1]
+    tables = FIELDS // groups
+    for group in range(groups):
+        for table in range(tables):
+            if table < COLUMNS:
+                whole = near_ref[table, group, 0]
+            else:
+                first = 2 * (table - COLUMNS)
+                whole = near_ref[first, group, 1].astype(f32) + near_ref[first + 1, group, 1].astype(f32)
+            at = (group * tables + table) * BATCH
+            xb_ref[0, at : at + BATCH] = whole.astype(bf16)
     x_ref[...] = xb_ref[0].astype(f32)
 
     def example(ref, e):
@@ -83,7 +110,7 @@
     for layer in range(layers):
         across = jnp.concatenate([example(x_ref, e).astype(bf16) for e in range(BATCH)], axis=1)
         if layer == 0:
-            fetches[0].wait()
+            fetches[1].wait()
         mixed = dot(mix_ref[layer], across, ((1,), (0,)))
         for e in range(BATCH):
             t_ref[pl.ds(e, FIELDS, stride=BATCH), :] = mixed[:, e * WIDTH : (e + 1) * WIDTH]
@@ -105,15 +132,17 @@
         rstd_fm = lax.rsqrt(jnp.mean(flat * flat, axis=1, keepdims=True) + 1e-05)
         nhat = flat * rstd_fm
         if layer == 0:
-            fetches[1].wait()
             fetches[2].wait()
+            fetches[3].wait()
         normed = (nhat * gain_fm_ref[layer : layer + 1]).astype(bf16)
         z = dot(normed, mlp_in_ref[layer], ((1,), (0,)))
         gate = jax.nn.sigmoid(z)
         hidden = (z * gate).astype(bf16)
         if layer == 0:
-            fetches[3].wait()
             fetches[4].wait()
+            fetches[5].wait()
+        if layer == 1:
+            fetches[6].wait()
         machine = dot(hidden, mlp_out_ref[layer], ((1,), (0,)))
         for n in range(NF):
             t_ref[n * BATCH : (n + 1) * BATCH] = machine[:, n * WIDTH : (n + 1) * WIDTH]
@@ -132,7 +161,8 @@
         saved.append((summary, nhat, rstd_fm, z, gate))
 
     acc = jnp.zeros((BATCH, WIDTH), f32)
-    fetches[5].wait()
+    fetches[7].wait()
+    fetches[8].wait()
     head = head_ref[...].astype(f32)
     for t in range(FIELDS):
         acc = acc + x_ref[t * BATCH : (t + 1) * BATCH] * head[t : t + 1]
@@ -200,7 +230,11 @@
             dx = x_ref[cut] + t_ref[cut] + dot(d_ref[cut], summary, ((1,), (0,)))
             x_ref[cut] = dx.astype(bf16).astype(f32)
 
-    back_ref[...] = x_ref[...].astype(bf16).reshape(back_ref.shape)
+    for group in range(groups):
+        for column in range(COLUMNS):
+            for half, table in enumerate((column, COLUMNS + column // 2)):
+                at = (group * tables + table) * BATCH
+                back_ref[column, group, half] = x_ref[at : at + BATCH].astype(bf16)
 
 
 def mix_of(proj, compress):
@@ -210,17 +244,20 @@
 
 
 def counts_kernel(where_ref, b0_ref, b1_ref, b2_ref, b3_ref, counts_ref, idx_ref):
-    tables, local, examples = counts_ref.shape
+    rows, examples = counts_ref.shape
     column, core = where_ref[0], where_ref[1]
     for hop, bags_ref in enumerate((b0_ref, b1_ref, b2_ref, b3_ref)):
-        coded = bags_ref[...]
-        mine = ((coded >> 6) & 3) == column
-        side = ((coded >> 5) & 1) ^ core
-        spot = (side << 8) | ((coded >> 8) << 5) | (coded & 31)
+        at = pl.multiple_of(((column + hop) & (COLUMNS - 1)) * 128, 128)
+        coded = bags_ref[:8]
+        side = ((coded >> 7) & 1) ^ core
+        spot = (side << 10) | ((coded >> 8) << 7) | (coded & 127)
+        idx_ref[:8, pl.ds(at, 128)] = jnp.where(coded < DEAD, spot, -1).astype(jnp.float32)
+        coded = bags_ref[8:]
+        side = ((coded >> 6) & 1) ^ core
+        spot = (side << 9) | ((coded >> 8) << 6) | (coded & 63)
+        mine = ((coded >> 7) & 1) == (column & 1)
         spot = jnp.where(mine & (coded < DEAD), spot, -1)
-        at = pl.multiple_of(((column + hop) & 3) * 128, 128)
-        idx_ref[:, pl.ds(at, 128)] = spot.astype(jnp.float32)
-    steps = local // 32
+        idx_ref[8:, pl.ds(at, 128)] = spot.astype(jnp.float32)
     ids = [
         (lax.broadcasted_iota(jnp.int32, (16, 128), 0) + 16 * i)
         .astype(jnp.float32)
@@ -230,61 +267,59 @@
     one = jnp.ones((16, 128), jnp.bfloat16)
     zero = jnp.zeros((16, 128), jnp.bfloat16)
 
-    def per_table(table, carry):
+    def per_window(window, carry):
+        half = window // 8
+        first = ((window - 8 * half) * 256).astype(jnp.float32)
         for run in range(examples // 128):
             cut = slice(run * 128, run * 128 + 128)
-            slots = idx_ref[pl.ds(pl.multiple_of(table * 8, 8), 8), cut]
-            for half in range(2):
-                keys = [
-                    jnp.broadcast_to(slots[b : b + 1] - 256.0 * half, (16, 128)).astype(jnp.bfloat16)
-                    for b in range(8)
-                ]
-                for i in range(steps):
-                    hits = [jnp.where(keys[b] == ids[i], one, zero) for b in range(8)]
-                    while len(hits) > 1:
-                        hits = [hits[k] + hits[k + 1] for k in range(0, len(hits), 2)]
-                    at = half * 256 + i * 16
-                    counts_ref[table, at : at + 16, cut] = hits[0]
+            slots = idx_ref[pl.ds(pl.multiple_of(half * 8, 8), 8), cut] - first
+            keys = [
+                jnp.broadcast_to(slots[b : b + 1], (16, 128)).astype(jnp.bfloat16) for b in range(8)
+            ]
+            for i in range(len(ids)):
+                hits = [jnp.where(keys[b] == ids[i], one, zero) for b in range(8)]
+                while len(hits) > 1:
+                    hits = [hits[k] + hits[k + 1] for k in range(0, len(hits), 2)]
+                at = pl.multiple_of(window * 256 + i * 16, 16)
+                counts_ref[pl.ds(at, 16), cut] = hits[0]
         return carry
 
-    lax.fori_loop(0, tables, per_table, 0)
+    lax.fori_loop(0, rows // 256, per_window, 0)
+
+
+def spans(rows):
+    share = rows // 6
+    return ((0, 2 * share), (4 * share, share))
 
 
 def pool_kernel(counts_ref, mine_ref, other_ref, pools_ref):
-    tables, local, examples = counts_ref.shape
-    width = mine_ref.shape[-1]
-
-    def per_table(table, carry):
-        rows = jnp.concatenate(
-            [ref[:, table].reshape(local // 2, width) for ref in (mine_ref, other_ref)], axis=0
-        )
-        part = dot(counts_ref[table], rows, ((0,), (0,)))
-        pools_ref[:, table] = part.astype(jnp.bfloat16).reshape(examples // BATCH, BATCH, width)
-        return carry
-
-    lax.fori_loop(0, tables, per_table, 0)
-
-
-def merge_kernel(moved_ref, out_ref):
-    for at in range(out_ref.shape[0]):
-        total = moved_ref[0, at].astype(jnp.float32)
-        for source in range(1, moved_ref.shape[0]):
-            total = total + moved_ref[source, at].astype(jnp.float32)
-        out_ref[at] = total.astype(jnp.bfloat16)
-
-
-def grads_kernel(counts_ref, moved_ref, mine_ref, other_ref):
-    tables, local, examples = counts_ref.shape
-    shards, _, rows, width = mine_ref.shape
-
-    def per_table(table, carry):
-        grads = moved_ref[:, table].reshape(examples, width)
-        acc = dot(counts_ref[table], grads, ((1,), (0,))).astype(jnp.bfloat16)
-        mine_ref[:, table] = acc[: local // 2].reshape(shards, rows, width)
-        other_ref[:, table] = acc[local // 2 :].reshape(shards, rows, width)
-        return carry
-
-    lax.fori_loop(0, tables, per_table, 0)
+    rows, examples = counts_ref.shape
+    shards = mine_ref.shape[0]
+    for half, (first, share) in enumerate(spans(rows)):
+        deep = share // shards
+        start = half * 2 * deep
+        total = None
+        for side, ref in enumerate((mine_ref, other_ref)):
+            at = first + side * share
+            part = dot(
+                counts_ref[at : at + share],
+                ref[:, start : start + deep].reshape(share, WIDTH),
+                ((0,), (0,)),
+            )
+            total = part if total is None else total + part
+        pools_ref[:, half] = total.astype(jnp.bfloat16).reshape(examples // BATCH, BATCH, WIDTH)
+
+
+def grads_kernel(side, counts_ref, moved_ref, out_ref):
+    rows, examples = counts_ref.shape
+    shards = out_ref.shape[0]
+    for half, (first, share) in enumerate(spans(rows)):
+        deep = share // shards
+        start = half * 2 * deep
+        at = first + side * share
+        grads = moved_ref[:, half].reshape(examples, WIDTH)
+        acc = dot(counts_ref[at : at + share], grads, ((1,), (0,))).astype(jnp.bfloat16)
+        out_ref[:, start : start + deep] = acc.reshape(shards, deep, WIDTH)
 
 
 def add_kernel(left_ref, right_ref, out_ref):
@@ -322,61 +357,66 @@
     rep = lax.axis_index(REP)
     sub = lax.axis_index(SUB)
     column, core = lax.axis_index("x"), lax.axis_index("core")
-    columns, cores, shards, groups = 4, 2, 8, 8
-    reps = columns * cores
-    part_rows = rows_dev // reps
-    examples = columns * groups * BATCH
-    across = [(0, 1), (1, 0)]
-
-    part = lax.dynamic_slice_in_dim(table_rows, rep * part_rows, part_rows, axis=1)
-    gathered = swap(
-        jnp.broadcast_to(part.reshape(1, *part.shape), (shards, tables, part_rows, width)), SUB
-    )
+    shards, groups, reps, across = 8, 8, 8, [(0, 1), (1, 0)]
+    share = rows_dev // 2
+    examples = COLUMNS * groups * BATCH
+    piece = shape((shards, share + share // 2, width), bf16)
+    per_owner = shape((COLUMNS * groups, 2, BATCH, width), bf16)
+
+    def of_table(table, first, count):
+        return lax.dynamic_slice(table_rows, (table, first, 0), (1, count, width))[0]
+
+    part = jnp.concatenate(
+        [
+            of_table(column, core * share, share),
+            of_table(
+                COLUMNS + column // 2, (column & 1) * share + core * (share // 2), share // 2
+            ),
+        ]
+    )
+    gathered = swap(jnp.broadcast_to(part, piece.shape), SUB)
     coded = call(
         pick_kernel,
-        shape((tables * 8, 128), jnp.int32),
-        "svv",
-        (sub.reshape(1), jnp.transpose(bag_rows, (1, 2, 0)), jnp.transpose(bag_lens)),
-    )
-    bags = [coded] + [
-        lax.ppermute(coded, "x", [((i + hop) % columns, i) for i in range(columns)])
-        for hop in range(1, columns)
+        (shape((16, 128), jnp.int32),) * COLUMNS,
+        "shh",
+        (jnp.stack([sub, column]), jnp.transpose(bag_rows, (1, 2, 0)), jnp.transpose(bag_lens)),
+        [
+            pltpu.VMEM((tables, 8, bag_rows.shape[0]), jnp.int32),
+            pltpu.VMEM((tables, bag_rows.shape[0]), jnp.int32),
+            pltpu.VMEM((tables, 8, 128), jnp.int32),
+            pltpu.SemaphoreType.DMA((2,)),
+        ],
+        DENSE_LIMIT,
+    )
+    bags = [coded[0]] + [
+        lax.ppermute(coded[hop], "x", [((i + hop) % COLUMNS, i) for i in range(COLUMNS)])
+        for hop in range(1, COLUMNS)
     ]
     counts = call(
         counts_kernel,
-        shape((tables, 2 * rows_dev, examples), bf16),
+        shape((2 * 6 * rows_dev, examples), bf16),
         "svvvv",
         (jnp.stack([column, core]), *bags),
-        [pltpu.VMEM((tables * 8, examples), f32)],
-    )
-    mix = mix_of(proj, compress)
-    gathered, counts, mix = lax.optimization_barrier((gathered, counts, mix))
+        [pltpu.VMEM((16, examples), f32)],
+    )
+    gathered, counts = lax.optimization_barrier((gathered, counts))
     other = lax.ppermute(gathered, "core", across)
-    pools = call(
-        pool_kernel,
-        shape((columns * groups, tables, BATCH, width), bf16),
-        "vvv",
-        (counts, gathered, other),
-    )
-    moved = swap(pools, "x")
-    per_group = shape((groups, tables, BATCH, width), bf16)
-    merged = call(
-        merge_kernel, per_group, "v", (moved.reshape(columns, groups, tables, BATCH, width),)
-    )
-    near = swap(merged, GRP)
+    other, mix = lax.optimization_barrier((other, mix_of(proj, compress)))
+    pools = call(pool_kernel, per_owner, "vvv", (counts, gathered, other))
+    near = swap(pools, ("x",) + GRP).reshape(COLUMNS, groups, 2, BATCH, width)
 
     rows = FIELDS * BATCH
     losses, back = call(
         dense_kernel,
         (shape((1, BATCH), f32), shape(near.shape, bf16)),
-        "vv" + "h" * 6,
+        "h" * 8,
         (
+            labels.reshape(1, BATCH),
             near,
-            labels.reshape(1, BATCH),
             mix,
+            gain_fm,
             mlp_in,
             mlp_out,
-            gain_fm,
             gain_out,
             head,
         ),
@@ -387,27 +427,32 @@
             pltpu.VMEM((layers, rows, 1), f32),
             pltpu.VMEM((layers + 1, rows, WIDTH), bf16),
             pltpu.VMEM((rows, WIDTH), bf16),
-            pltpu.VMEM((layers, FIELDS, FIELDS), bf16),
+            pltpu.VMEM(near.shape, bf16),
+            pltpu.VMEM(mix.shape, bf16),
+            pltpu.VMEM(gain_fm.shape, f32),
             pltpu.VMEM(mlp_in.shape, bf16),
             pltpu.VMEM(mlp_out.shape, bf16),
-            pltpu.VMEM(gain_fm.shape, f32),
             pltpu.VMEM(gain_out.shape, f32),
             pltpu.VMEM(head.shape, bf16),
-            pltpu.SemaphoreType.DMA((6,)),
+            pltpu.VMEM((1, BATCH), f32),
+            pltpu.SemaphoreType.DMA((9,)),
         ],
-        60 * 1024 * 1024,
-    )
-
-    back = swap(back, GRP)
-    back = jnp.broadcast_to(back, (columns, *back.shape))
-    returned = swap(back.reshape(columns * groups, tables, BATCH, width), "x")
-    piece = shape((shards, tables, part_rows, width), bf16)
-    mine, other = call(grads_kernel, (piece, piece), "vv", (counts, returned))
+        DENSE_LIMIT,
+    )
+
+    returned = swap(back.reshape(per_owner.shape), ("x",) + GRP)
+    other = call(functools.partial(grads_kernel, 1), piece, "vv", (counts, returned))
     other = lax.ppermute(other, "core", across)
+    mine = call(functools.partial(grads_kernel, 0), piece, "vv", (counts, returned))
     pieces = swap(call(add_kernel, piece, "vv", (mine, other)), SUB)
     own = jnp.sum(pieces.astype(f32), axis=0).astype(bf16)
-    spread = swap(jnp.broadcast_to(own, (reps, tables, part_rows, width)), REP)
-    row_grads = jnp.transpose(spread, (1, 0, 2, 3)).reshape(tables, rows_dev, width)
+    spread = swap(jnp.broadcast_to(own, (reps, *own.shape)), REP)
+    row_grads = jnp.concatenate(
+        [
+            spread[:, :share].reshape(COLUMNS, rows_dev, width),
+            spread[:, share:].reshape(COLUMNS // 2, rows_dev, width),
+        ]
+    )
     return (losses.reshape(BATCH), row_grads.astype(f32))
 
 

time: 182 us -> 163 us (0.90)
  blocking collectives: 114 us -> 101 us
  starting transfers between devices: 39.3 us -> 33 us
    all_to_all x6 -> x4, blocking collectives: 114 us -> 101 us  [swap(): return lax.all_to_all(values, axes, split_axis=0, concat_axis=0, tiled=True)]
    ppermute x3, waiting for transfers between devices: 0.01 us -> 3.62 us  [per_device(): lax.ppermute(coded[hop], 'x', [((i + hop) % COLUMNS, i) for i in range(CO...]
    ppermute x1, starting transfers between devices: 7.49 us -> 4.62 us  [per_device(): other = lax.ppermute(other, 'core', across)]
    ppermute x1, starting transfers between devices: 8.16 us -> 5.97 us  [per_device(): other = lax.ppermute(gathered, 'core', across)]
  transfers between devices with their start and end apart: 6 -> 6, of which waited for: 2 -> 3; matrix products, arithmetic and copies ran while one was open for 1% -> 1% of each run, Pallas kernels for 2% -> 4%
where the time goes in v4:
time: 163 us; the launch traced here: 162 us
  blocking collectives  101 us (62%)
  starting transfers between devices  33 us (20%)
  Pallas kernels  17.1 us (10%)
  waiting for transfers between devices  4.41 us (3%)
  local copies, waits for them, and re-layouts  3.36 us (2%)
  other arithmetic  2.33 us (1%)
    all_to_all x4, blocking collectives, swap(): return lax.all_to_all(values, axes, split_axis=0, concat_axis=0, tiled=True)  101 us
    pallas_call x7, Pallas kernels, call(): pl.pallas_call(kernel, out_shape=out_shape, in_specs=[{'s': smem, 'v': vm...  17.1 us
    all_to_all x1, starting transfers between devices, swap(): return lax.all_to_all(values, axes, split_axis=0, concat_axis=0, tiled=True)  13.1 us
    ppermute x3, starting transfers between devices, per_device(): lax.ppermute(coded[hop], 'x', [((i + hop) % COLUMNS, i) for i in range(CO...  9.33 us
    ppermute x1, starting transfers between devices, per_device(): other = lax.ppermute(gathered, 'core', across)  5.97 us
    ppermute x1, starting transfers between devices, per_device(): other = lax.ppermute(other, 'core', across)  4.62 us
    ppermute x3, waiting for transfers between devices, per_device(): lax.ppermute(coded[hop], 'x', [((i + hop) % COLUMNS, i) for i in range(CO...  3.62 us
  transfers between devices with their start and end apart: 6, of which 3 were waited for; matrix products, arithmetic and copies ran while one was open for 1% of the time, Pallas kernels for 4%

profile of v4, /device:TPU:1, one launch (start us, length us, event | category | flops | bytes accessed | tf_op | source)
XLA Modules:
  0.0 162.1 jit_solution(16690660696884472045)
XLA Ops:
  0.7 1.0 copy-done
  1.6 0.8 broadcast_in_dim.9
  2.4 13.1 %all-to-all-start = ((bf16[8,192,128]{2,1,0:T(8,128)(2,1)}), bf16[8,192,128]{2,1,0:T(8,128)(2,1)}, u32[]{:S(2)}, u32[]{:S(2)}) async-start(bf16[8,192,128]{2,1,0:T(8,128)(2,1)} %broadcast_in_dim.9), calls=%async_computation | async-start | bytes 786432 | tf_op jit(solution)/shard_map/all_to_all | solution.py:332
  15.5 0.6 pad_add_fusion.1.where_ref
  16.1 2.3 %shard_map.122 = (s32[16,128]{1,0:T(8,128)}, s32[16,128]{1,0:T(8,128)}, s32[16,128]{1,0:T(8,128)}, s32[16,128]{1,0:T(8,128)}) custom-call(s32[2]{0:T(128)} %pad_add_fusion.1.where_ref, s32[6,8,1024]{2,1,0:T(8,128)} %bitcast.20, s32[6,1024]{1,0:T(8,128)} %bitcast.21), custom_call_target="tpu_custom_call" | custom-call | tf_op jit(solution)/shard_map/pallas_call | solution.py:340
  18.5 4.4 %collective-permute-start = (s32[16,128]{1,0:T(8,128)}, s32[16,128]{1,0:T(8,128)S(1)}, u32[]{:S(2)}, u32[]{:S(2)}) collective-permute-start(s32[16,128]{1,0:T(8,128)} %get-tuple-element.13), channel_id=1, source_target_pairs={{128,0},{256,128},{384,256},{0,384},{129,1},{257,129},{385,257},{1... | collective-permute-start | bytes 24584 | tf_op jit(solution)/shard_map/ppermute | solution.py:392
  22.8 2.4 %collective-permute-start.1 = (s32[16,128]{1,0:T(8,128)}, s32[16,128]{1,0:T(8,128)S(1)}, u32[]{:S(2)}, u32[]{:S(2)}) collective-permute-start(s32[16,128]{1,0:T(8,128)} %get-tuple-element.14), channel_id=1, source_target_pairs={{256,0},{384,128},{0,256},{128,384},{257,1},{385,129},{1,257},{129... | collective-permute-start | bytes 24584 | tf_op jit(solution)/shard_map/ppermute | solution.py:392
  25.3 2.5 %collective-permute-start.2 = (s32[16,128]{1,0:T(8,128)}, s32[16,128]{1,0:T(8,128)S(1)}, u32[]{:S(2)}, u32[]{:S(2)}) collective-permute-start(s32[16,128]{1,0:T(8,128)} %get-tuple-element.15), channel_id=1, source_target_pairs={{384,0},{0,128},{128,256},{256,384},{385,1},{1,129},{129,257},{257... | collective-permute-start | bytes 24584 | tf_op jit(solution)/shard_map/ppermute | solution.py:392
  27.8 0.1 pad_add_fusion.where_ref
  27.9 1.1 collective-permute-done.1.b2_ref
  29.0 2.5 %collective-permute-done.2.b3_ref = s32[16,128]{1,0:T(8,128)S(1)} collective-permute-done((s32[16,128]{1,0:T(8,128)}, s32[16,128]{1,0:T(8,128)S(1)}, u32[]{:S(2)}, u32[]{:S(2)}) %collective-permute-start.2) | collective-permute-done | bytes 8224 | tf_op jit(solution)/shard_map/ppermute | solution.py:392
  31.5 0.7 copy-done.1
  32.2 3.4 %shard_map.123.counts_ref = bf16[3072,512]{1,0:T(8,128)(2,1)S(1)} custom-call(s32[2]{0:T(128)S(1)} %pad_add_fusion.where_ref, s32[16,128]{1,0:T(8,128)S(1)} %copy-done.1, s32[16,128]{1,0:T(8,128)S(1)} %collective-permute-done.b1_ref, s32[16,128]{1,0:T(8,128)S(1)} %collective-permute-done.1.b2_ref, s32[16,128]{1,0:T(8,128)S(1)} %collective-permute-done.2.b3_ref), custom_call_target="tpu_custom_call" | custom-call | tf_op jit(solution)/shard_map/pallas_call | solution.py:340
  35.6 6.0 %collective-permute-start.3 = (bf16[8,192,128]{2,1,0:T(8,128)(2,1)}, bf16[8,192,128]{2,1,0:T(8,128)(2,1)S(1)}, u32[]{:S(2)}, u32[]{:S(2)}) collective-permute-start(bf16[8,192,128]{2,1,0:T(8,128)(2,1)} %all-to-all-done.mine_ref), channel_id=1, source_target_pairs={{0,64},{64,0},{1,65},{65,1},{2,66},{66,2},{3,67},{67,3},{4,68},{68... | collective-permute-start | bytes 1179656 | tf_op jit(solution)/shard_map/ppermute | solution.py:403
  41.6 0.7 copy.13
  42.3 0.1 pad.3.clone
  42.4 0.7 pad_maximum_fusion.1.mix_hbm
  43.1 0.0 collective-permute-done.3.other_ref
  43.1 2.0 %shard_map.124 = bf16[32,2,16,128]{3,2,1,0:T(8,128)(2,1)S(1)} custom-call(bf16[3072,512]{1,0:T(8,128)(2,1)S(1)} %shard_map.123.counts_ref, bf16[8,192,128]{2,1,0:T(8,128)(2,1)} %all-to-all-done.mine_ref, bf16[8,192,128]{2,1,0:T(8,128)(2,1)S(1)} %collective-permute-done.3.other_ref), custom_call_target="tpu_custom_call" | custom-call | tf_op jit(solution)/shard_map/pallas_call | solution.py:340
  45.1 30.7 %all_to_all.25 = bf16[32,2,16,128]{3,2,1,0:T(8,128)(2,1)} all-to-all(bf16[32,2,16,128]{3,2,1,0:T(8,128)(2,1)S(1)} %shard_map.124), channel_id=1, replica_groups=mesh['x'=4,'core'=2,'y'=4,'zhi'=2,'sub'=8] {'x','y','zhi'}, dimensions={0} | all-to-all | bytes 524288 | tf_op jit(solution)/shard_map/all_to_all | solution.py:332
  75.9 8.1 %shard_map.125 = (f32[1,16]{1,0:T(1,128)}, bf16[4,8,2,16,128]{4,3,2,1,0:T(8,128)(2,1)}) custom-call(f32[1,16]{1,0:T(1,128)} %bitcast.23, bf16[4,8,2,16,128]{4,3,2,1,0:T(8,128)(2,1)} %bitcast.17, bf16[2,48,48]{2,1,0:T(8,128)(2,1)} %pad_maximum_fusion.1.mix_hbm, f32[2,384]{1,0:T(2,128)} %gain_fm_hbm.1, bf16[2,384,384]{2,1,0:T(8,128)(2,1)} %mlp_in_hbm.1, ...), custom_call_target="tpu_custom_call" | custom-call | tf_op jit(solution)/shard_map/pallas_call | solution.py:340
  84.0 20.9 %all_to_all.26.moved_ref = bf16[32,2,16,128]{3,2,1,0:T(8,128)(2,1)S(1)} all-to-all(bf16[32,2,16,128]{3,2,1,0:T(8,128)(2,1)} %bitcast.19), channel_id=1, replica_groups=mesh['x'=4,'core'=2,'y'=4,'zhi'=2,'sub'=8] {'x','y','zhi'}, dimensions={0} | all-to-all | bytes 524288 | tf_op jit(solution)/shard_map/all_to_all | solution.py:332
  104.9 0.6 shard_map.127
  105.5 4.6 %collective-permute-start.4 = (bf16[8,192,128]{2,1,0:T(8,128)(2,1)S(1)}, bf16[8,192,128]{2,1,0:T(8,128)(2,1)S(1)}, u32[]{:S(2)}, u32[]{:S(2)}) collective-permute-start(bf16[8,192,128]{2,1,0:T(8,128)(2,1)S(1)} %shard_map.127), channel_id=1, source_target_pairs={{0,64},{64,0},{1,65},{65,1},{2,66},{66,2},{3,67},{67,3},{4,68},{68... | collective-permute-start | bytes 1179656 | tf_op jit(solution)/shard_map/ppermute | solution.py:445
  110.1 0.6 shard_map.126.left_ref
  110.7 0.7 collective-permute-done.4.right_ref
  111.4 0.1 shard_map.128
  111.5 36.0 %all_to_all.27 = bf16[8,192,128]{2,1,0:T(8,128)(2,1)S(1)} all-to-all(bf16[8,192,128]{2,1,0:T(8,128)(2,1)S(1)} %shard_map.128), channel_id=1, replica_groups=mesh['x'=4,'core'=2,'y'=4,'zhi'=2,'sub'=8] {'sub'}, dimensions={0} | all-to-all | bytes 786432 | tf_op jit(solution)/shard_map/all_to_all | solution.py:332
  147.5 0.1 reduce_sum.12
  147.5 0.1 broadcast_in_dim.11
  147.6 13.5 %all_to_all.28 = bf16[8,192,128]{2,1,0:T(8,128)(2,1)S(1)} all-to-all(bf16[8,192,128]{2,1,0:T(8,128)(2,1)S(1)} %broadcast_in_dim.11), channel_id=1, replica_groups=mesh['x'=4,'core'=2,'y'=4,'zhi'=2,'sub'=8] {'x','core'}, dimensions={0} | all-to-all | bytes 786432 | tf_op jit(solution)/shard_map/all_to_all | solution.py:332
  161.1 0.9 maximum_convert_fusion
  (12 shorter events, 0.1 us)
Async XLA Ops:
  0.6 1.0 copy-start
  0.6 41.8 %copy-start.2 = (bf16[2,48,8]{1,2,0:T(8,128)(2,1)S(1)}, bf16[2,48,8]{1,2,0:T(8,128)(2,1)}, u32[]{:S(2)}) copy-start(bf16[2,48,8]{1,2,0:T(8,128)(2,1)} %param.15) | copy-start | bytes 4612
  2.4 33.2 %all-to-all-start = ((bf16[8,192,128]{2,1,0:T(8,128)(2,1)}), bf16[8,192,128]{2,1,0:T(8,128)(2,1)}, u32[]{:S(2)}, u32[]{:S(2)}) async-start(bf16[8,192,128]{2,1,0:T(8,128)(2,1)} %broadcast_in_dim.9), calls=%async_computation | async-start | bytes 786432 | tf_op jit(solution)/shard_map/all_to_all | solution.py:332
  18.5 9.4 %collective-permute-start = (s32[16,128]{1,0:T(8,128)}, s32[16,128]{1,0:T(8,128)S(1)}, u32[]{:S(2)}, u32[]{:S(2)}) collective-permute-start(s32[16,128]{1,0:T(8,128)} %get-tuple-element.13), channel_id=1, source_target_pairs={{128,0},{256,128},{384,256},{0,384},{129,1},{257,129},{385,257},{1... | collective-permute-start | bytes 24584 | tf_op jit(solution)/shard_map/ppermute | solution.py:392
  22.8 6.1 %collective-permute-start.1 = (s32[16,128]{1,0:T(8,128)}, s32[16,128]{1,0:T(8,128)S(1)}, u32[]{:S(2)}, u32[]{:S(2)}) collective-permute-start(s32[16,128]{1,0:T(8,128)} %get-tuple-element.14), channel_id=1, source_target_pairs={{256,0},{384,128},{0,256},{128,384},{257,1},{385,129},{1,257},{129... | collective-permute-start | bytes 24584 | tf_op jit(solution)/shard_map/ppermute | solution.py:392
  25.3 6.2 %collective-permute-start.2 = (s32[16,128]{1,0:T(8,128)}, s32[16,128]{1,0:T(8,128)S(1)}, u32[]{:S(2)}, u32[]{:S(2)}) collective-permute-start(s32[16,128]{1,0:T(8,128)} %get-tuple-element.15), channel_id=1, source_target_pairs={{384,0},{0,128},{128,256},{256,384},{385,1},{1,129},{129,257},{257... | collective-permute-start | bytes 24584 | tf_op jit(solution)/shard_map/ppermute | solution.py:392
  31.5 0.7 copy-start.1
  35.6 7.5 %collective-permute-start.3 = (bf16[8,192,128]{2,1,0:T(8,128)(2,1)}, bf16[8,192,128]{2,1,0:T(8,128)(2,1)S(1)}, u32[]{:S(2)}, u32[]{:S(2)}) collective-permute-start(bf16[8,192,128]{2,1,0:T(8,128)(2,1)} %all-to-all-done.mine_ref), channel_id=1, source_target_pairs={{0,64},{64,0},{1,65},{65,1},{2,66},{66,2},{3,67},{67,3},{4,68},{68... | collective-permute-start | bytes 1179656 | tf_op jit(solution)/shard_map/ppermute | solution.py:403
  105.5 6.0 %collective-permute-start.4 = (bf16[8,192,128]{2,1,0:T(8,128)(2,1)S(1)}, bf16[8,192,128]{2,1,0:T(8,128)(2,1)S(1)}, u32[]{:S(2)}, u32[]{:S(2)}) collective-permute-start(bf16[8,192,128]{2,1,0:T(8,128)(2,1)S(1)} %shard_map.127), channel_id=1, source_target_pairs={{0,64},{64,0},{1,65},{65,1},{2,66},{66,2},{3,67},{67,3},{4,68},{68... | collective-permute-start | bytes 1179656 | tf_op jit(solution)/shard_map/ppermute | solution.py:445

commit v5 on v4

--- a/solution.py
+++ b/solution.py
@@ -10,7 +10,7 @@
 
 REP = ("x", "core")
 GRP = ("y", "zhi")
-SUB = ("sub",)
+SUB = ("quad", "pair")
 DEAD = 4095
 COLUMNS = 4
 FIELDS, BATCH, WIDTH, RANK, NF = 48, 16, 128, 8, 12
@@ -31,21 +31,22 @@
     bag = rows_ref.shape[1]
     slots = lax.broadcasted_iota(jnp.int32, (bag, 128), 0)
     lanes = lax.broadcasted_iota(jnp.int32, (bag, 128), 1)
-    sub, column = where_ref[0], where_ref[1]
+    column, quad, pair = where_ref[0], where_ref[2], where_ref[3]
     for table in range(rows_ref.shape[0]):
-        kept = jnp.zeros((bag, 128), jnp.int32)
-        for run in range(8):
-            cut = slice(run * 128, run * 128 + 128)
-            coded = jnp.where(
-                slots < lens_ref[table : table + 1, cut], rows_ref[table, :, cut], DEAD
-            )
-            moved = pltpu.roll(coded, (run * 16 - sub * 16) & 127, 1)
-            kept = jnp.where(lanes // 16 == run, moved, kept)
-        kept_ref[table] = kept
+        for group in range(2):
+            kept = jnp.zeros((bag, 128), jnp.int32)
+            for run in range(4):
+                at = (group * 4 + run) * 128
+                cut = slice(at, at + 128)
+                coded = jnp.where(
+                    slots < lens_ref[table : table + 1, cut], rows_ref[table, :, cut], DEAD
+                )
+                moved = pltpu.roll(coded, (run * 32 - quad * 32) & 127, 1)
+                kept = jnp.where(lanes // 32 == run, moved, kept)
+            kept_ref[table, :, group * 128 : group * 128 + 128] = kept
     for hop in range(COLUMNS):
         target = (column - hop) & (COLUMNS - 1)
-        outs[hop][:bag] = kept_ref[target]
-        outs[hop][bag:] = kept_ref[COLUMNS + (target >> 1)]
+        outs[hop][...] = kept_ref[jnp.where(pair == 0, target, COLUMNS + (target >> 1))]
 
 
 def dot(a, b, dims):
@@ -243,21 +244,16 @@
     return jnp.concatenate([jnp.transpose(proj, (0, 2, 1)), gap, compress], axis=1)
 
 
-def counts_kernel(where_ref, b0_ref, b1_ref, b2_ref, b3_ref, counts_ref, idx_ref):
+def counts_kernel(where_ref, bags_ref, counts_ref, idx_ref):
     rows, examples = counts_ref.shape
-    column, core = where_ref[0], where_ref[1]
-    for hop, bags_ref in enumerate((b0_ref, b1_ref, b2_ref, b3_ref)):
-        at = pl.multiple_of(((column + hop) & (COLUMNS - 1)) * 128, 128)
-        coded = bags_ref[:8]
-        side = ((coded >> 7) & 1) ^ core
-        spot = (side << 10) | ((coded >> 8) << 7) | (coded & 127)
-        idx_ref[:8, pl.ds(at, 128)] = jnp.where(coded < DEAD, spot, -1).astype(jnp.float32)
-        coded = bags_ref[8:]
-        side = ((coded >> 6) & 1) ^ core
-        spot = (side << 9) | ((coded >> 8) << 6) | (coded & 63)
-        mine = ((coded >> 7) & 1) == (column & 1)
-        spot = jnp.where(mine & (coded < DEAD), spot, -1)
-        idx_ref[8:, pl.ds(at, 128)] = spot.astype(jnp.float32)
+    column, core, pair = where_ref[0], where_ref[1], where_ref[3]
+    coded = bags_ref[...]
+    top, low = (coded >> 7) & 1, (coded >> 6) & 1
+    shard = (coded >> 8) << 7
+    whole = ((top ^ core) << 10) | shard | (coded & 127)
+    partial = jnp.where(top == (column & 1), ((low ^ core) << 10) | shard | (coded & 63), -1)
+    spot = jnp.where(coded < DEAD, jnp.where(pair == 0, whole, partial), -1)
+    idx_ref[...] = spot.astype(jnp.float32)
     ids = [
         (lax.broadcasted_iota(jnp.int32, (16, 128), 0) + 16 * i)
         .astype(jnp.float32)
@@ -268,11 +264,10 @@
     zero = jnp.zeros((16, 128), jnp.bfloat16)
 
     def per_window(window, carry):
-        half = window // 8
-        first = ((window - 8 * half) * 256).astype(jnp.float32)
+        first = (window * 256).astype(jnp.float32)
         for run in range(examples // 128):
             cut = slice(run * 128, run * 128 + 128)
-            slots = idx_ref[pl.ds(pl.multiple_of(half * 8, 8), 8), cut] - first
+            slots = idx_ref[:, cut] - first
             keys = [
                 jnp.broadcast_to(slots[b : b + 1], (16, 128)).astype(jnp.bfloat16) for b in range(8)
             ]
@@ -287,39 +282,30 @@
     lax.fori_loop(0, rows // 256, per_window, 0)
 
 
-def spans(rows):
-    share = rows // 6
-    return ((0, 2 * share), (4 * share, share))
-
-
-def pool_kernel(counts_ref, mine_ref, other_ref, pools_ref):
-    rows, examples = counts_ref.shape
-    shards = mine_ref.shape[0]
-    for half, (first, share) in enumerate(spans(rows)):
-        deep = share // shards
-        start = half * 2 * deep
-        total = None
-        for side, ref in enumerate((mine_ref, other_ref)):
-            at = first + side * share
-            part = dot(
-                counts_ref[at : at + share],
-                ref[:, start : start + deep].reshape(share, WIDTH),
-                ((0,), (0,)),
-            )
-            total = part if total is None else total + part
-        pools_ref[:, half] = total.astype(jnp.bfloat16).reshape(examples // BATCH, BATCH, WIDTH)
-
-
-def grads_kernel(side, counts_ref, moved_ref, out_ref):
-    rows, examples = counts_ref.shape
-    shards = out_ref.shape[0]
-    for half, (first, share) in enumerate(spans(rows)):
-        deep = share // shards
-        start = half * 2 * deep
-        at = first + side * share
-        grads = moved_ref[:, half].reshape(examples, WIDTH)
-        acc = dot(counts_ref[at : at + share], grads, ((1,), (0,))).astype(jnp.bfloat16)
-        out_ref[:, start : start + deep] = acc.reshape(shards, deep, WIDTH)
+def pool_kernel(where_ref, c0_ref, c1_ref, c2_ref, c3_ref, mine_ref, other_ref, pools_ref):
+    column = where_ref[0]
+    for hop, counts_ref in enumerate((c0_ref, c1_ref, c2_ref, c3_ref)):
+        rows, examples = counts_ref.shape
+        share = rows // 2
+        total = dot(counts_ref[:share], mine_ref[...].reshape(share, WIDTH), ((0,), (0,)))
+        total += dot(counts_ref[share:], other_ref[...].reshape(share, WIDTH), ((0,), (0,)))
+        owners = examples // BATCH
+        at = ((column + hop) & (COLUMNS - 1)) * owners
+        pools_ref[pl.ds(at, owners)] = total.astype(jnp.bfloat16).reshape(owners, BATCH, WIDTH)
+
+
+def grads_kernel(side, where_ref, c0_ref, c1_ref, c2_ref, c3_ref, moved_ref, out_ref):
+    column = where_ref[0]
+    total = None
+    for hop, counts_ref in enumerate((c0_ref, c1_ref, c2_ref, c3_ref)):
+        rows, examples = counts_ref.shape
+        share = rows // 2
+        owners = examples // BATCH
+        at = ((column + hop) & (COLUMNS - 1)) * owners
+        grads = moved_ref[pl.ds(at, owners)].reshape(examples, WIDTH)
+        part = dot(counts_ref[side * share : side * share + share], grads, ((1,), (0,)))
+        total = part if total is None else total + part
+    out_ref[...] = total.astype(jnp.bfloat16).reshape(out_ref.shape)
 
 
 def add_kernel(left_ref, right_ref, out_ref):
@@ -354,36 +340,35 @@
     shape = jax.ShapeDtypeStruct
     tables, rows_dev, width = table_rows.shape
     layers = proj.shape[0]
-    rep = lax.axis_index(REP)
-    sub = lax.axis_index(SUB)
-    column, core = lax.axis_index("x"), lax.axis_index("core")
-    shards, groups, reps, across = 8, 8, 8, [(0, 1), (1, 0)]
+    column, core, quad, pair = (lax.axis_index(name) for name in ("x", "core") + SUB)
+    where = jnp.stack([column, core, quad, pair])
+    quads, pairs, groups, reps, across = 4, 2, 8, 8, [(0, 1), (1, 0)]
     share = rows_dev // 2
-    examples = COLUMNS * groups * BATCH
-    piece = shape((shards, share + share // 2, width), bf16)
-    per_owner = shape((COLUMNS * groups, 2, BATCH, width), bf16)
+    owners = groups * pairs
+    piece = shape((quads * pairs, share, width), bf16)
+    per_owner = shape((COLUMNS * owners, BATCH, width), bf16)
+    exchange = ("x",) + GRP + ("pair",)
 
     def of_table(table, first, count):
-        return lax.dynamic_slice(table_rows, (table, first, 0), (1, count, width))[0]
-
-    part = jnp.concatenate(
-        [
-            of_table(column, core * share, share),
-            of_table(
-                COLUMNS + column // 2, (column & 1) * share + core * (share // 2), share // 2
-            ),
-        ]
-    )
-    gathered = swap(jnp.broadcast_to(part, piece.shape), SUB)
+        return lax.dynamic_slice(table_rows, (table, first, 0), (1, count, width))
+
+    whole = of_table(column, core * share, share)
+    half = of_table(
+        COLUMNS + column // 2, (column & 1) * share + core * (share // 2), share // 2
+    )
+    both = jnp.concatenate([whole, jnp.pad(half, ((0, 0), (0, share // 2), (0, 0)))])
+    gathered = swap(
+        jnp.broadcast_to(both, (quads, *both.shape)).reshape(piece.shape), SUB
+    )
     coded = call(
         pick_kernel,
-        (shape((16, 128), jnp.int32),) * COLUMNS,
+        (shape((8, owners * BATCH), jnp.int32),) * COLUMNS,
         "shh",
-        (jnp.stack([sub, column]), jnp.transpose(bag_rows, (1, 2, 0)), jnp.transpose(bag_lens)),
+        (where, jnp.transpose(bag_rows, (1, 2, 0)), jnp.transpose(bag_lens)),
         [
             pltpu.VMEM((tables, 8, bag_rows.shape[0]), jnp.int32),
             pltpu.VMEM((tables, bag_rows.shape[0]), jnp.int32),
-            pltpu.VMEM((tables, 8, 128), jnp.int32),
+            pltpu.VMEM((tables, 8, owners * BATCH), jnp.int32),
             pltpu.SemaphoreType.DMA((2,)),
         ],
         DENSE_LIMIT,
@@ -392,18 +377,21 @@
         lax.ppermute(coded[hop], "x", [((i + hop) % COLUMNS, i) for i in range(COLUMNS)])
         for hop in range(1, COLUMNS)
     ]
-    counts = call(
-        counts_kernel,
-        shape((2 * 6 * rows_dev, examples), bf16),
-        "svvvv",
-        (jnp.stack([column, core]), *bags),
-        [pltpu.VMEM((16, examples), f32)],
-    )
-    gathered, counts = lax.optimization_barrier((gathered, counts))
+    counts = [
+        call(
+            counts_kernel,
+            shape((8 * rows_dev, owners * BATCH), bf16),
+            "sv",
+            (where, bag),
+            [pltpu.VMEM((8, owners * BATCH), f32)],
+        )
+        for bag in bags
+    ]
+    gathered, *counts = lax.optimization_barrier((gathered, *counts))
     other = lax.ppermute(gathered, "core", across)
     other, mix = lax.optimization_barrier((other, mix_of(proj, compress)))
-    pools = call(pool_kernel, per_owner, "vvv", (counts, gathered, other))
-    near = swap(pools, ("x",) + GRP).reshape(COLUMNS, groups, 2, BATCH, width)
+    pools = call(pool_kernel, per_owner, "svvvvvv", (where, *counts, gathered, other))
+    near = swap(pools, exchange).reshape(COLUMNS, groups, pairs, BATCH, width)
 
     rows = FIELDS * BATCH
     losses, back = call(
@@ -440,12 +428,16 @@
         DENSE_LIMIT,
     )
 
-    returned = swap(back.reshape(per_owner.shape), ("x",) + GRP)
-    other = call(functools.partial(grads_kernel, 1), piece, "vv", (counts, returned))
+    returned = swap(back.reshape(per_owner.shape), exchange)
+    operands = (where, *counts, returned)
+    other = call(functools.partial(grads_kernel, 1), piece, "svvvvv", operands)
     other = lax.ppermute(other, "core", across)
-    mine = call(functools.partial(grads_kernel, 0), piece, "vv", (counts, returned))
+    mine = call(functools.partial(grads_kernel, 0), piece, "svvvvv", operands)
     pieces = swap(call(add_kernel, piece, "vv", (mine, other)), SUB)
-    own = jnp.sum(pieces.astype(f32), axis=0).astype(bf16)
+    whole, half = jnp.sum(
+        pieces.reshape(quads, pairs, share, width).astype(f32), axis=0
+    ).astype(bf16)
+    own = jnp.concatenate([whole, half[: share // 2]])
     spread = swap(jnp.broadcast_to(own, (reps, *own.shape)), REP)
     row_grads = jnp.concatenate(
         [
@@ -458,7 +450,7 @@
 
 def solution(mesh):
     view = Mesh(
-        mesh.devices.reshape(4, 2, 4, 2, 8), ("x", "core", "y", "zhi", "sub")
+        mesh.devices.reshape(4, 2, 4, 2, 4, 2), ("x", "core", "y", "zhi", "quad", "pair")
     )
     return jax.shard_map(
         per_device,

time: 163 us -> 161 us (0.988)
  blocking collectives: 101 us -> 95.9 us
  waiting for transfers between devices: 4.41 us -> 0.02 us
  Pallas kernels: 17.1 us -> 21.4 us
  local copies, waits for them, and re-layouts: 3.36 us -> 6.19 us
    all_to_all x4, blocking collectives: 101 us -> 95.9 us  [swap(): return lax.all_to_all(values, axes, split_axis=0, concat_axis=0, tiled=True)]
    pallas_call x7 -> x10, Pallas kernels: 17.1 us -> 21.4 us  [call(): pl.pallas_call(kernel, out_shape=out_shape, in_specs=[{'s': smem, 'v': vm...]
    ppermute x3, waiting for transfers between devices: 3.62 us -> 0.01 us  [per_device(): lax.ppermute(coded[hop], 'x', [((i + hop) % COLUMNS, i) for i in range(CO...]
    unnamed x7 -> x17, local copies, waits for them, and re-layouts: 2.39 us -> 5.27 us
    ppermute x1, starting transfers between devices: 5.97 us -> 3.69 us  [per_device(): other = lax.ppermute(gathered, 'core', across)]
    ppermute x1, starting transfers between devices: 4.62 us -> 6.35 us  [per_device(): other = lax.ppermute(other, 'core', across)]
  transfers between devices with their start and end apart: 6 -> 6, of which waited for: 3 -> 0; matrix products, arithmetic and copies ran while one was open for 1% -> 1% of each run, Pallas kernels for 4% -> 6%
where the time goes in v5:
time: 161 us; the launch traced here: 160 us
  blocking collectives  95.9 us (60%)
  starting transfers between devices  33.7 us (21%)
  Pallas kernels  21.4 us (13%)
  local copies, waits for them, and re-layouts  6.19 us (4%)
  other arithmetic  2.32 us (1%)
    all_to_all x4, blocking collectives, swap(): return lax.all_to_all(values, axes, split_axis=0, concat_axis=0, tiled=True)  95.9 us
    pallas_call x10, Pallas kernels, call(): pl.pallas_call(kernel, out_shape=out_shape, in_specs=[{'s': smem, 'v': vm...  21.4 us
    all_to_all x1, starting transfers between devices, swap(): return lax.all_to_all(values, axes, split_axis=0, concat_axis=0, tiled=True)  13.1 us
    ppermute x3, starting transfers between devices, per_device(): lax.ppermute(coded[hop], 'x', [((i + hop) % COLUMNS, i) for i in range(CO...  10.5 us
    ppermute x1, starting transfers between devices, per_device(): other = lax.ppermute(other, 'core', across)  6.35 us
    unnamed x17, local copies, waits for them, and re-layouts  5.27 us
    ppermute x1, starting transfers between devices, per_device(): other = lax.ppermute(gathered, 'core', across)  3.69 us
  transfers between devices with their start and end apart: 6, of which 0 were waited for; matrix products, arithmetic and copies ran while one was open for 1% of the time, Pallas kernels for 6%

profile of v5, /device:TPU:1, one launch (start us, length us, event | category | flops | bytes accessed | tf_op | source)
XLA Modules:
  0.0 160.4 jit_solution(16081129492146286986)
XLA Ops:
  0.7 1.0 copy-done
  1.6 0.7 broadcast_in_dim.9
  2.4 13.1 %all-to-all-start = ((bf16[8,128,128]{2,1,0:T(8,128)(2,1)}), bf16[8,128,128]{2,1,0:T(8,128)(2,1)}, u32[]{:S(2)}, u32[]{:S(2)}) async-start(bf16[8,128,128]{2,1,0:T(8,128)(2,1)} %bitcast.5), calls=%async_computation | async-start | bytes 524288 | tf_op jit(solution)/shard_map/all_to_all | solution.py:318
  15.5 0.7 pad_add_fusion.where_ref
  16.1 2.4 %shard_map.122 = (s32[8,256]{1,0:T(8,128)}, s32[8,256]{1,0:T(8,128)}, s32[8,256]{1,0:T(8,128)}, s32[8,256]{1,0:T(8,128)}) custom-call(s32[4]{0:T(128)} %pad_add_fusion.where_ref, s32[6,8,1024]{2,1,0:T(8,128)} %bitcast.24, s32[6,1024]{1,0:T(8,128)} %bitcast.25), custom_call_target="tpu_custom_call" | custom-call | tf_op jit(solution)/shard_map/pallas_call | solution.py:326
  18.6 3.1 %collective-permute-start.2 = (s32[8,256]{1,0:T(8,128)}, s32[8,256]{1,0:T(8,128)S(1)}, u32[]{:S(2)}, u32[]{:S(2)}) collective-permute-start(s32[8,256]{1,0:T(8,128)} %get-tuple-element.18), channel_id=1, source_target_pairs={{384,0},{0,128},{128,256},{256,384},{385,1},{1,129},{129,257},{257... | collective-permute-start | bytes 24584 | tf_op jit(solution)/shard_map/ppermute | solution.py:377
  21.7 4.4 %collective-permute-start.1 = (s32[8,256]{1,0:T(8,128)}, s32[8,256]{1,0:T(8,128)S(1)}, u32[]{:S(2)}, u32[]{:S(2)}) collective-permute-start(s32[8,256]{1,0:T(8,128)} %get-tuple-element.17), channel_id=1, source_target_pairs={{256,0},{384,128},{0,256},{128,384},{257,1},{385,129},{1,257},{129... | collective-permute-start | bytes 24584 | tf_op jit(solution)/shard_map/ppermute | solution.py:377
  26.0 3.1 %collective-permute-start = (s32[8,256]{1,0:T(8,128)}, s32[8,256]{1,0:T(8,128)S(1)}, u32[]{:S(2)}, u32[]{:S(2)}) collective-permute-start(s32[8,256]{1,0:T(8,128)} %get-tuple-element.16), channel_id=1, source_target_pairs={{128,0},{256,128},{384,256},{0,384},{129,1},{257,129},{385,257},{1... | collective-permute-start | bytes 24584 | tf_op jit(solution)/shard_map/ppermute | solution.py:377
  29.1 0.7 copy-done.4
  29.8 0.7 copy-done.6
  30.5 1.5 shard_map.123.c0_ref
  32.0 1.5 shard_map.126.c3_ref
  33.5 1.5 shard_map.125.c2_ref
  35.1 1.5 shard_map.124.c1_ref
  36.6 1.0 copy-done.1
  37.6 3.7 %collective-permute-start.3 = (bf16[8,128,128]{2,1,0:T(8,128)(2,1)}, bf16[8,128,128]{2,1,0:T(8,128)(2,1)S(1)}, u32[]{:S(2)}, u32[]{:S(2)}) collective-permute-start(bf16[8,128,128]{2,1,0:T(8,128)(2,1)} %all-to-all-done.mine_ref), channel_id=1, source_target_pairs={{0,64},{64,0},{1,65},{65,1},{2,66},{66,2},{3,67},{67,3},{4,68},{68... | collective-permute-start | bytes 786440 | tf_op jit(solution)/shard_map/ppermute | solution.py:391
  41.3 0.7 copy.13
  42.0 0.1 pad.10.clone
  42.1 0.7 pad_maximum_fusion.1.mix_hbm
  42.8 1.2 copy-done.2
  44.0 2.3 %shard_map.127 = bf16[64,16,128]{2,1,0:T(8,128)(2,1)S(1)} custom-call(s32[4]{0:T(128)S(1)} %copy-done.5, bf16[2048,256]{1,0:T(8,128)(2,1)S(1)} %shard_map.123.c0_ref, bf16[2048,256]{1,0:T(8,128)(2,1)S(1)} %copy-done.2, bf16[2048,256]{1,0:T(8,128)(2,1)S(1)} %shard_map.125.c2_ref, bf16[2048,256]{1,0:T(8,128)(2,1)S(1)} %shard_map.126.c3_ref, ...), custom_call_target="tpu_custom_call" | custom-call | tf_op jit(solution)/shard_map/pallas_call | solution.py:326
  46.3 29.7 %all_to_all.25 = bf16[64,16,128]{2,1,0:T(8,128)(2,1)} all-to-all(bf16[64,16,128]{2,1,0:T(8,128)(2,1)S(1)} %shard_map.127), channel_id=1, replica_groups=mesh['x'=4,'core'=2,'y'=4,'zhi'=2,'quad'=4,'pair'=2] {'x','y','zhi','pair'}, dimensions={0} | all-to-all | bytes 524288 | tf_op jit(solution)/shard_map/all_to_all | solution.py:318
  76.0 8.1 %shard_map.128 = (f32[1,16]{1,0:T(1,128)}, bf16[4,8,2,16,128]{4,3,2,1,0:T(8,128)(2,1)}) custom-call(f32[1,16]{1,0:T(1,128)} %bitcast.27, bf16[4,8,2,16,128]{4,3,2,1,0:T(8,128)(2,1)} %bitcast.21, bf16[2,48,48]{2,1,0:T(8,128)(2,1)} %pad_maximum_fusion.1.mix_hbm, f32[2,384]{1,0:T(2,128)} %gain_fm_hbm.1, bf16[2,384,384]{2,1,0:T(8,128)(2,1)} %mlp_in_hbm.1, ...), custom_call_target="tpu_custom_call" | custom-call | tf_op jit(solution)/shard_map/pallas_call | solution.py:326
  84.1 26.1 %all_to_all.26.moved_ref = bf16[64,16,128]{2,1,0:T(8,128)(2,1)S(1)} all-to-all(bf16[64,16,128]{2,1,0:T(8,128)(2,1)} %bitcast.23), channel_id=1, replica_groups=mesh['x'=4,'core'=2,'y'=4,'zhi'=2,'quad'=4,'pair'=2] {'x','y','zhi','pair'}, dimensions={0} | all-to-all | bytes 524288 | tf_op jit(solution)/shard_map/all_to_all | solution.py:318
  110.2 1.2 shard_map.130
  111.4 6.3 %collective-permute-start.4 = (bf16[8,128,128]{2,1,0:T(8,128)(2,1)S(1)}, bf16[8,128,128]{2,1,0:T(8,128)(2,1)S(1)}, u32[]{:S(2)}, u32[]{:S(2)}) collective-permute-start(bf16[8,128,128]{2,1,0:T(8,128)(2,1)S(1)} %shard_map.130), channel_id=1, source_target_pairs={{0,64},{64,0},{1,65},{65,1},{2,66},{66,2},{3,67},{67,3},{4,68},{68... | collective-permute-start | bytes 786440 | tf_op jit(solution)/shard_map/ppermute | solution.py:434
  117.8 1.3 shard_map.129.left_ref
  119.1 0.1 shard_map.131
  119.1 26.5 %all_to_all.27 = bf16[8,128,128]{2,1,0:T(8,128)(2,1)S(1)} all-to-all(bf16[8,128,128]{2,1,0:T(8,128)(2,1)S(1)} %shard_map.131), channel_id=1, replica_groups=mesh['x'=4,'core'=2,'y'=4,'zhi'=2,'quad'=4,'pair'=2] {'quad','pair'}, dimensions={0} | all-to-all | bytes 524288 | tf_op jit(solution)/shard_map/all_to_all | solution.py:318
  145.7 0.1 broadcast_in_dim.11
  145.8 13.6 %all_to_all.28 = bf16[8,192,128]{2,1,0:T(8,128)(2,1)S(1)} all-to-all(bf16[8,192,128]{2,1,0:T(8,128)(2,1)S(1)} %broadcast_in_dim.11), channel_id=1, replica_groups=mesh['x'=4,'core'=2,'y'=4,'zhi'=2,'quad'=4,'pair'=2] {'x','core'}, dimensions={0} | all-to-all | bytes 786432 | tf_op jit(solution)/shard_map/all_to_all | solution.py:318
  159.4 0.9 maximum_convert_fusion
  (27 shorter events, 0.1 us)
Async XLA Ops:
  0.6 1.0 copy-start
  2.4 35.2 %all-to-all-start = ((bf16[8,128,128]{2,1,0:T(8,128)(2,1)}), bf16[8,128,128]{2,1,0:T(8,128)(2,1)}, u32[]{:S(2)}, u32[]{:S(2)}) async-start(bf16[8,128,128]{2,1,0:T(8,128)(2,1)} %bitcast.5), calls=%async_computation | async-start | bytes 524288 | tf_op jit(solution)/shard_map/all_to_all | solution.py:318
  15.5 26.6 %copy-start.7 = (bf16[2,48,8]{1,2,0:T(8,128)(2,1)S(1)}, bf16[2,48,8]{1,2,0:T(8,128)(2,1)}, u32[]{:S(2)}) copy-start(bf16[2,48,8]{1,2,0:T(8,128)(2,1)} %param.15) | copy-start | bytes 4612
  16.1 26.6 %copy-start.5 = (s32[4]{0:T(128)S(1)}, s32[4]{0:T(128)}, u32[]{:S(2)}) copy-start(s32[4]{0:T(128)} %pad_add_fusion.where_ref) | copy-start | bytes 52
  18.6 13.4 %collective-permute-start.2 = (s32[8,256]{1,0:T(8,128)}, s32[8,256]{1,0:T(8,128)S(1)}, u32[]{:S(2)}, u32[]{:S(2)}) collective-permute-start(s32[8,256]{1,0:T(8,128)} %get-tuple-element.18), channel_id=1, source_target_pairs={{384,0},{0,128},{128,256},{256,384},{385,1},{1,129},{129,257},{257... | collective-permute-start | bytes 24584 | tf_op jit(solution)/shard_map/ppermute | solution.py:377
  21.7 11.8 %collective-permute-start.1 = (s32[8,256]{1,0:T(8,128)}, s32[8,256]{1,0:T(8,128)S(1)}, u32[]{:S(2)}, u32[]{:S(2)}) collective-permute-start(s32[8,256]{1,0:T(8,128)} %get-tuple-element.17), channel_id=1, source_target_pairs={{256,0},{384,128},{0,256},{128,384},{257,1},{385,129},{1,257},{129... | collective-permute-start | bytes 24584 | tf_op jit(solution)/shard_map/ppermute | solution.py:377
  26.0 9.0 %collective-permute-start = (s32[8,256]{1,0:T(8,128)}, s32[8,256]{1,0:T(8,128)S(1)}, u32[]{:S(2)}, u32[]{:S(2)}) collective-permute-start(s32[8,256]{1,0:T(8,128)} %get-tuple-element.16), channel_id=1, source_target_pairs={{128,0},{256,128},{384,256},{0,384},{129,1},{257,129},{385,257},{1... | collective-permute-start | bytes 24584 | tf_op jit(solution)/shard_map/ppermute | solution.py:377
  29.1 0.7 copy-start.4
  29.8 0.7 copy-start.6
  36.6 1.0 copy-start.1
  37.6 5.2 %collective-permute-start.3 = (bf16[8,128,128]{2,1,0:T(8,128)(2,1)}, bf16[8,128,128]{2,1,0:T(8,128)(2,1)S(1)}, u32[]{:S(2)}, u32[]{:S(2)}) collective-permute-start(bf16[8,128,128]{2,1,0:T(8,128)(2,1)} %all-to-all-done.mine_ref), channel_id=1, source_target_pairs={{0,64},{64,0},{1,65},{65,1},{2,66},{66,2},{3,67},{67,3},{4,68},{68... | collective-permute-start | bytes 786440 | tf_op jit(solution)/shard_map/ppermute | solution.py:391
  42.8 1.2 copy-start.2
  46.3 63.9 %copy-start.3 = (bf16[2048,256]{1,0:T(8,128)(2,1)S(1)}, bf16[2048,256]{1,0:T(8,128)(2,1)}, u32[]{:S(2)}) copy-start(bf16[2048,256]{1,0:T(8,128)(2,1)} %copy-done.1) | copy-start | bytes 3145732
  111.4 7.6 %collective-permute-start.4 = (bf16[8,128,128]{2,1,0:T(8,128)(2,1)S(1)}, bf16[8,128,128]{2,1,0:T(8,128)(2,1)S(1)}, u32[]{:S(2)}, u32[]{:S(2)}) collective-permute-start(bf16[8,128,128]{2,1,0:T(8,128)(2,1)S(1)} %shard_map.130), channel_id=1, source_target_pairs={{0,64},{64,0},{1,65},{65,1},{2,66},{66,2},{3,67},{67,3},{4,68},{68... | collective-permute-start | bytes 786440 | tf_op jit(solution)/shard_map/ppermute | solution.py:434

commit v6 on v5

--- a/solution.py
+++ b/solution.py
@@ -14,11 +14,11 @@
 DEAD = 4095
 COLUMNS = 4
 FIELDS, BATCH, WIDTH, RANK, NF = 48, 16, 128, 8, 12
-VMEM_LIMIT = 24 * 1024 * 1024
-DENSE_LIMIT = 56 * 1024 * 1024
-
-
-def pick_kernel(where_ref, rows_hbm, lens_hbm, *refs):
+VMEM_LIMIT = 20 * 1024 * 1024
+DENSE_LIMIT = 24 * 1024 * 1024
+
+
+def pick_kernel(rows_hbm, lens_hbm, *refs):
     outs, (rows_ref, lens_ref, kept_ref, sems) = refs[:COLUMNS], refs[COLUMNS:]
     fetches = [
         pltpu.make_async_copy(rows_hbm, rows_ref, sems.at[0]),
@@ -31,7 +31,7 @@
     bag = rows_ref.shape[1]
     slots = lax.broadcasted_iota(jnp.int32, (bag, 128), 0)
     lanes = lax.broadcasted_iota(jnp.int32, (bag, 128), 1)
-    column, quad, pair = where_ref[0], where_ref[2], where_ref[3]
+    column, quad, pair = (lax.axis_index(name) for name in ("x",) + SUB)
     for table in range(rows_ref.shape[0]):
         for group in range(2):
             kept = jnp.zeros((bag, 128), jnp.int32)
@@ -244,16 +244,19 @@
     return jnp.concatenate([jnp.transpose(proj, (0, 2, 1)), gap, compress], axis=1)
 
 
-def counts_kernel(where_ref, bags_ref, counts_ref, idx_ref):
+def counts_kernel(*refs):
+    bags_refs, (counts_ref, idx_ref) = refs[:-2], refs[-2:]
     rows, examples = counts_ref.shape
-    column, core, pair = where_ref[0], where_ref[1], where_ref[3]
-    coded = bags_ref[...]
-    top, low = (coded >> 7) & 1, (coded >> 6) & 1
-    shard = (coded >> 8) << 7
-    whole = ((top ^ core) << 10) | shard | (coded & 127)
-    partial = jnp.where(top == (column & 1), ((low ^ core) << 10) | shard | (coded & 63), -1)
-    spot = jnp.where(coded < DEAD, jnp.where(pair == 0, whole, partial), -1)
-    idx_ref[...] = spot.astype(jnp.float32)
+    column, core, pair = (lax.axis_index(name) for name in ("x", "core", "pair"))
+    for hop, bags_ref in enumerate(bags_refs):
+        coded = bags_ref[...]
+        top, low = (coded >> 7) & 1, (coded >> 6) & 1
+        shard = (coded >> 8) << 7
+        whole = ((top ^ core) << 10) | shard | (coded & 127)
+        partial = jnp.where(top == (column & 1), ((low ^ core) << 10) | shard | (coded & 63), -1)
+        spot = jnp.where(coded < DEAD, jnp.where(pair == 0, whole, partial), -1)
+        each = coded.shape[1]
+        idx_ref[:, hop * each : hop * each + each] = spot.astype(jnp.float32)
     ids = [
         (lax.broadcasted_iota(jnp.int32, (16, 128), 0) + 16 * i)
         .astype(jnp.float32)
@@ -282,29 +285,30 @@
     lax.fori_loop(0, rows // 256, per_window, 0)
 
 
-def pool_kernel(where_ref, c0_ref, c1_ref, c2_ref, c3_ref, mine_ref, other_ref, pools_ref):
-    column = where_ref[0]
-    for hop, counts_ref in enumerate((c0_ref, c1_ref, c2_ref, c3_ref)):
-        rows, examples = counts_ref.shape
-        share = rows // 2
-        total = dot(counts_ref[:share], mine_ref[...].reshape(share, WIDTH), ((0,), (0,)))
-        total += dot(counts_ref[share:], other_ref[...].reshape(share, WIDTH), ((0,), (0,)))
-        owners = examples // BATCH
-        at = ((column + hop) & (COLUMNS - 1)) * owners
-        pools_ref[pl.ds(at, owners)] = total.astype(jnp.bfloat16).reshape(owners, BATCH, WIDTH)
-
-
-def grads_kernel(side, where_ref, c0_ref, c1_ref, c2_ref, c3_ref, moved_ref, out_ref):
-    column = where_ref[0]
-    total = None
-    for hop, counts_ref in enumerate((c0_ref, c1_ref, c2_ref, c3_ref)):
-        rows, examples = counts_ref.shape
-        share = rows // 2
-        owners = examples // BATCH
-        at = ((column + hop) & (COLUMNS - 1)) * owners
-        grads = moved_ref[pl.ds(at, owners)].reshape(examples, WIDTH)
-        part = dot(counts_ref[side * share : side * share + share], grads, ((1,), (0,)))
-        total = part if total is None else total + part
+def by_column(first_ref, last_ref, owned):
+    each = last_ref.shape[1]
+    column = lax.axis_index("x")
+    for hop in range(COLUMNS):
+        ref, at = (first_ref, hop * each) if hop < COLUMNS - 1 else (last_ref, 0)
+        yield ref, slice(at, at + each), pl.ds(((column + hop) & (COLUMNS - 1)) * owned, owned)
+
+
+def pool_kernel(first_ref, last_ref, mine_ref, other_ref, pools_ref):
+    share = first_ref.shape[0] // 2
+    owned = pools_ref.shape[0] // COLUMNS
+    for ref, cut, owners in by_column(first_ref, last_ref, owned):
+        total = dot(ref[:share, cut], mine_ref[...].reshape(share, WIDTH), ((0,), (0,)))
+        total += dot(ref[share:, cut], other_ref[...].reshape(share, WIDTH), ((0,), (0,)))
+        pools_ref[owners] = total.astype(jnp.bfloat16).reshape(owned, BATCH, WIDTH)
+
+
+def grads_kernel(side, first_ref, last_ref, moved_ref, out_ref):
+    share = first_ref.shape[0] // 2
+    owned = moved_ref.shape[0] // COLUMNS
+    total = jnp.zeros((share, WIDTH), jnp.float32)
+    for ref, cut, owners in by_column(first_ref, last_ref, owned):
+        grads = moved_ref[owners].reshape(owned * BATCH, WIDTH)
+        total += dot(ref[side * share : side * share + share, cut], grads, ((1,), (0,)))
     out_ref[...] = total.astype(jnp.bfloat16).reshape(out_ref.shape)
 
 
@@ -340,8 +344,7 @@
     shape = jax.ShapeDtypeStruct
     tables, rows_dev, width = table_rows.shape
     layers = proj.shape[0]
-    column, core, quad, pair = (lax.axis_index(name) for name in ("x", "core") + SUB)
-    where = jnp.stack([column, core, quad, pair])
+    column, core = lax.axis_index("x"), lax.axis_index("core")
     quads, pairs, groups, reps, across = 4, 2, 8, 8, [(0, 1), (1, 0)]
     share = rows_dev // 2
     owners = groups * pairs
@@ -363,8 +366,8 @@
     coded = call(
         pick_kernel,
         (shape((8, owners * BATCH), jnp.int32),) * COLUMNS,
-        "shh",
-        (where, jnp.transpose(bag_rows, (1, 2, 0)), jnp.transpose(bag_lens)),
+        "hh",
+        (jnp.transpose(bag_rows, (1, 2, 0)), jnp.transpose(bag_lens)),
         [
             pltpu.VMEM((tables, 8, bag_rows.shape[0]), jnp.int32),
             pltpu.VMEM((tables, bag_rows.shape[0]), jnp.int32),
@@ -377,20 +380,24 @@
         lax.ppermute(coded[hop], "x", [((i + hop) % COLUMNS, i) for i in range(COLUMNS)])
         for hop in range(1, COLUMNS)
     ]
-    counts = [
-        call(
+    each = owners * BATCH
+
+    def count(bags):
+        examples = len(bags) * each
+        return call(
             counts_kernel,
-            shape((8 * rows_dev, owners * BATCH), bf16),
-            "sv",
-            (where, bag),
-            [pltpu.VMEM((8, owners * BATCH), f32)],
+            shape((8 * rows_dev, examples), bf16),
+            "v" * len(bags),
+            bags,
+            [pltpu.VMEM((8, examples), f32)],
         )
-        for bag in bags
-    ]
-    gathered, *counts = lax.optimization_barrier((gathered, *counts))
+
+    first = count(bags[:-1])
+    gathered, first, late = lax.optimization_barrier((gathered, first, bags[-1]))
     other = lax.ppermute(gathered, "core", across)
-    other, mix = lax.optimization_barrier((other, mix_of(proj, compress)))
-    pools = call(pool_kernel, per_owner, "svvvvvv", (where, *counts, gathered, other))
+    last = count([late])
+    other, last, mix = lax.optimization_barrier((other, last, mix_of(proj, compress)))
+    pools = call(pool_kernel, per_owner, "vvvv", (first, last, gathered, other))
     near = swap(pools, exchange).reshape(COLUMNS, groups, pairs, BATCH, width)
 
     rows = FIELDS * BATCH
@@ -429,10 +436,10 @@
     )
 
     returned = swap(back.reshape(per_owner.shape), exchange)
-    operands = (where, *counts, returned)
-    other = call(functools.partial(grads_kernel, 1), piece, "svvvvv", operands)
+    operands = (first, last, returned)
+    other = call(functools.partial(grads_kernel, 1), piece, "vvv", operands)
     other = lax.ppermute(other, "core", across)
-    mine = call(functools.partial(grads_kernel, 0), piece, "svvvvv", operands)
+    mine = call(functools.partial(grads_kernel, 0), piece, "vvv", operands)
     pieces = swap(call(add_kernel, piece, "vv", (mine, other)), SUB)
     whole, half = jnp.sum(
         pieces.reshape(quads, pairs, share, width).astype(f32), axis=0

time: 161 us -> 153 us (0.950)
  Pallas kernels: 21.4 us -> 15 us
  starting transfers between devices: 33.7 us -> 30.9 us
  blocking collectives: 95.9 us -> 98.5 us
  local copies, waits for them, and re-layouts: 6.19 us -> 4.32 us
  waiting for transfers between devices: 0.02 us -> 1.76 us
    pallas_call x10 -> x8, Pallas kernels: 21.4 us -> 15 us  [call(): pl.pallas_call(kernel, out_shape=out_shape, in_specs=[{'s': smem, 'v': vm...]
    all_to_all x4, blocking collectives: 95.9 us -> 98.5 us  [swap(): return lax.all_to_all(values, axes, split_axis=0, concat_axis=0, tiled=True)]
    ppermute x1, starting transfers between devices: 6.35 us -> 4.48 us  [per_device(): other = lax.ppermute(other, 'core', across)]
    unnamed x17 -> x21, local copies, waits for them, and re-layouts: 5.27 us -> 3.41 us
  transfers between devices with their start and end apart: 6 -> 6, of which waited for: 0 -> 2; matrix products, arithmetic and copies ran while one was open for 1% -> 1% of each run, Pallas kernels for 6% -> 3%
where the time goes in v6:
time: 153 us; the launch traced here: 152 us
  blocking collectives  98.5 us (64%)
  starting transfers between devices  30.9 us (20%)
  Pallas kernels  15 us (10%)
  local copies, waits for them, and re-layouts  4.32 us (3%)
  waiting for transfers between devices  1.76 us (1%)
    all_to_all x4, blocking collectives, swap(): return lax.all_to_all(values, axes, split_axis=0, concat_axis=0, tiled=True)  98.5 us
    pallas_call x8, Pallas kernels, call(): pl.pallas_call(kernel, out_shape=out_shape, in_specs=[{'s': smem, 'v': vm...  15 us
    all_to_all x1, starting transfers between devices, swap(): return lax.all_to_all(values, axes, split_axis=0, concat_axis=0, tiled=True)  13.1 us
    ppermute x3, starting transfers between devices, per_device(): lax.ppermute(coded[hop], 'x', [((i + hop) % COLUMNS, i) for i in range(CO...  9.33 us
    ppermute x1, starting transfers between devices, per_device(): other = lax.ppermute(other, 'core', across)  4.48 us
    ppermute x1, starting transfers between devices, per_device(): other = lax.ppermute(gathered, 'core', across)  4.05 us
    unnamed x21, local copies, waits for them, and re-layouts  3.41 us
  transfers between devices with their start and end apart: 6, of which 2 were waited for; matrix products, arithmetic and copies ran while one was open for 1% of the time, Pallas kernels for 3%

profile of v6, /device:TPU:1, one launch (start us, length us, event | category | flops | bytes accessed | tf_op | source)
XLA Modules:
  0.0 152.5 jit_solution(7977046647081481523)
XLA Ops:
  0.6 0.0 copy-start
  0.7 1.0 copy-done
  1.6 0.7 broadcast_in_dim.9
  2.4 13.1 %all-to-all-start = ((bf16[8,128,128]{2,1,0:T(8,128)(2,1)}), bf16[8,128,128]{2,1,0:T(8,128)(2,1)}, u32[]{:S(2)}, u32[]{:S(2)}) async-start(bf16[8,128,128]{2,1,0:T(8,128)(2,1)} %bitcast.1), calls=%async_computation | async-start | bytes 524288 | tf_op jit(solution)/shard_map/all_to_all | solution.py:322
  15.5 0.9 copy-done.3
  16.4 0.8 copy-done.4
  17.1 0.4 shard_map.122
  17.6 4.4 %collective-permute-start = (s32[8,256]{1,0:T(8,128)S(1)}, s32[8,256]{1,0:T(8,128)S(1)}, u32[]{:S(2)}, u32[]{:S(2)}) collective-permute-start(s32[8,256]{1,0:T(8,128)S(1)} %get-tuple-element.15), channel_id=1, source_target_pairs={{128,0},{256,128},{384,256},{0,384},{129,1},{257,129},{385,257},{1... | collective-permute-start | bytes 24584 | tf_op jit(solution)/shard_map/ppermute | solution.py:380
  22.0 2.4 %collective-permute-start.1 = (s32[8,256]{1,0:T(8,128)S(1)}, s32[8,256]{1,0:T(8,128)S(1)}, u32[]{:S(2)}, u32[]{:S(2)}) collective-permute-start(s32[8,256]{1,0:T(8,128)S(1)} %get-tuple-element.16), channel_id=1, source_target_pairs={{256,0},{384,128},{0,256},{128,384},{257,1},{385,129},{1,257},{129... | collective-permute-start | bytes 24584 | tf_op jit(solution)/shard_map/ppermute | solution.py:380
  24.4 2.5 %collective-permute-start.2 = (s32[8,256]{1,0:T(8,128)S(1)}, s32[8,256]{1,0:T(8,128)S(1)}, u32[]{:S(2)}, u32[]{:S(2)}) collective-permute-start(s32[8,256]{1,0:T(8,128)S(1)} %get-tuple-element.17), channel_id=1, source_target_pairs={{384,0},{0,128},{128,256},{256,384},{385,1},{1,129},{129,257},{257... | collective-permute-start | bytes 24584 | tf_op jit(solution)/shard_map/ppermute | solution.py:380
  26.9 1.3 collective-permute-done.1.refs_2_
  28.3 2.8 %shard_map.123.first_ref = bf16[2048,768]{1,0:T(8,128)(2,1)S(1)} custom-call(s32[8,256]{1,0:T(8,128)S(1)} %get-tuple-element.14.refs_0_, s32[8,256]{1,0:T(8,128)S(1)} %collective-permute-done.refs_1_, s32[8,256]{1,0:T(8,128)S(1)} %collective-permute-done.1.refs_2_), custom_call_target="tpu_custom_call" | custom-call | tf_op jit(solution)/shard_map/pallas_call | solution.py:330
  31.1 4.0 %collective-permute-start.3 = (bf16[8,128,128]{2,1,0:T(8,128)(2,1)}, bf16[8,128,128]{2,1,0:T(8,128)(2,1)S(1)}, u32[]{:S(2)}, u32[]{:S(2)}) collective-permute-start(bf16[8,128,128]{2,1,0:T(8,128)(2,1)} %all-to-all-done.mine_ref), channel_id=1, source_target_pairs={{0,64},{64,0},{1,65},{65,1},{2,66},{66,2},{3,67},{67,3},{4,68},{68... | collective-permute-start | bytes 786440 | tf_op jit(solution)/shard_map/ppermute | solution.py:397
  35.1 0.7 copy.13
  35.8 0.1 pad.10.clone
  35.9 0.1 pad_maximum_fusion.1.mix_hbm
  36.0 0.0 copy-start.5
  36.0 0.0 copy-start.6
  36.1 1.0 shard_map.124.last_ref
  37.1 2.2 %shard_map.125 = bf16[64,16,128]{2,1,0:T(8,128)(2,1)S(1)} custom-call(bf16[2048,768]{1,0:T(8,128)(2,1)S(1)} %shard_map.123.first_ref, bf16[2048,256]{1,0:T(8,128)(2,1)S(1)} %shard_map.124.last_ref, bf16[8,128,128]{2,1,0:T(8,128)(2,1)} %all-to-all-done.mine_ref, bf16[8,128,128]{2,1,0:T(8,128)(2,1)S(1)} %collective-permute-done.3.other_ref), custom_call_target="tpu_custom_call" | custom-call | tf_op jit(solution)/shard_map/pallas_call | solution.py:330
  39.3 31.8 %all_to_all.25 = bf16[64,16,128]{2,1,0:T(8,128)(2,1)S(1)} all-to-all(bf16[64,16,128]{2,1,0:T(8,128)(2,1)S(1)} %shard_map.125), channel_id=1, replica_groups=mesh['x'=4,'core'=2,'y'=4,'zhi'=2,'quad'=4,'pair'=2] {'x','y','zhi','pair'}, dimensions={0} | all-to-all | bytes 524288 | tf_op jit(solution)/shard_map/all_to_all | solution.py:322
  71.1 7.1 %shard_map.126 = (f32[1,16]{1,0:T(1,128)}, bf16[4,8,2,16,128]{4,3,2,1,0:T(8,128)(2,1)S(1)}) custom-call(f32[1,16]{1,0:T(1,128)S(1)} %bitcast.19, bf16[4,8,2,16,128]{4,3,2,1,0:T(8,128)(2,1)S(1)} %bitcast.15, bf16[2,48,48]{2,1,0:T(8,128)(2,1)S(1)} %pad_maximum_fusion.1.mix_hbm, f32[2,384]{1,0:T(2,128)S(1)} %copy-done.6, bf16[2,384,384]{2,1,0:T(8,128)(2,1)S(1)} %copy-done.2, ...), custom_call_target="tpu_custom_call" | custom-call | tf_op jit(solution)/shard_map/pallas_call | solution.py:330
  78.3 29.3 %all_to_all.26.moved_ref = bf16[64,16,128]{2,1,0:T(8,128)(2,1)S(1)} all-to-all(bf16[64,16,128]{2,1,0:T(8,128)(2,1)S(1)} %bitcast.16), channel_id=1, replica_groups=mesh['x'=4,'core'=2,'y'=4,'zhi'=2,'quad'=4,'pair'=2] {'x','y','zhi','pair'}, dimensions={0} | all-to-all | bytes 524288 | tf_op jit(solution)/shard_map/all_to_all | solution.py:322
  107.5 0.7 shard_map.128
  108.3 4.5 %collective-permute-start.4 = (bf16[8,128,128]{2,1,0:T(8,128)(2,1)S(1)}, bf16[8,128,128]{2,1,0:T(8,128)(2,1)S(1)}, u32[]{:S(2)}, u32[]{:S(2)}) collective-permute-start(bf16[8,128,128]{2,1,0:T(8,128)(2,1)S(1)} %shard_map.128), channel_id=1, source_target_pairs={{0,64},{64,0},{1,65},{65,1},{2,66},{66,2},{3,67},{67,3},{4,68},{68... | collective-permute-start | bytes 786440 | tf_op jit(solution)/shard_map/ppermute | solution.py:441
  112.7 0.7 shard_map.127.left_ref
  113.5 0.4 collective-permute-done.4.right_ref
  113.9 0.1 shard_map.129
  114.0 23.6 %all_to_all.27 = bf16[8,128,128]{2,1,0:T(8,128)(2,1)S(1)} all-to-all(bf16[8,128,128]{2,1,0:T(8,128)(2,1)S(1)} %shard_map.129), channel_id=1, replica_groups=mesh['x'=4,'core'=2,'y'=4,'zhi'=2,'quad'=4,'pair'=2] {'quad','pair'}, dimensions={0} | all-to-all | bytes 524288 | tf_op jit(solution)/shard_map/all_to_all | solution.py:322
  137.6 0.1 broadcast_in_dim.11
  137.7 13.8 %all_to_all.28 = bf16[8,192,128]{2,1,0:T(8,128)(2,1)S(1)} all-to-all(bf16[8,192,128]{2,1,0:T(8,128)(2,1)S(1)} %broadcast_in_dim.11), channel_id=1, replica_groups=mesh['x'=4,'core'=2,'y'=4,'zhi'=2,'quad'=4,'pair'=2] {'x','core'}, dimensions={0} | all-to-all | bytes 786432 | tf_op jit(solution)/shard_map/all_to_all | solution.py:322
  151.6 0.9 maximum_convert_fusion
  (28 shorter events, 0.1 us)
Async XLA Ops:
  0.6 1.0 copy-start
  0.6 35.3 %copy-start.9 = (bf16[2,48,8]{1,2,0:T(8,128)(2,1)S(1)}, bf16[2,48,8]{1,2,0:T(8,128)(2,1)}, u32[]{:S(2)}) copy-start(bf16[2,48,8]{1,2,0:T(8,128)(2,1)} %param.15) | copy-start | bytes 4612
  2.4 28.7 %all-to-all-start = ((bf16[8,128,128]{2,1,0:T(8,128)(2,1)}), bf16[8,128,128]{2,1,0:T(8,128)(2,1)}, u32[]{:S(2)}, u32[]{:S(2)}) async-start(bf16[8,128,128]{2,1,0:T(8,128)(2,1)} %bitcast.1), calls=%async_computation | async-start | bytes 524288 | tf_op jit(solution)/shard_map/all_to_all | solution.py:322
  15.5 0.9 copy-start.3
  16.4 0.8 copy-start.4
  17.6 9.4 %collective-permute-start = (s32[8,256]{1,0:T(8,128)S(1)}, s32[8,256]{1,0:T(8,128)S(1)}, u32[]{:S(2)}, u32[]{:S(2)}) collective-permute-start(s32[8,256]{1,0:T(8,128)S(1)} %get-tuple-element.15), channel_id=1, source_target_pairs={{128,0},{256,128},{384,256},{0,384},{129,1},{257,129},{385,257},{1... | collective-permute-start | bytes 24584 | tf_op jit(solution)/shard_map/ppermute | solution.py:380
  22.0 6.3 %collective-permute-start.1 = (s32[8,256]{1,0:T(8,128)S(1)}, s32[8,256]{1,0:T(8,128)S(1)}, u32[]{:S(2)}, u32[]{:S(2)}) collective-permute-start(s32[8,256]{1,0:T(8,128)S(1)} %get-tuple-element.16), channel_id=1, source_target_pairs={{256,0},{384,128},{0,256},{128,384},{257,1},{385,129},{1,257},{129... | collective-permute-start | bytes 24584 | tf_op jit(solution)/shard_map/ppermute | solution.py:380
  24.4 6.6 %collective-permute-start.2 = (s32[8,256]{1,0:T(8,128)S(1)}, s32[8,256]{1,0:T(8,128)S(1)}, u32[]{:S(2)}, u32[]{:S(2)}) collective-permute-start(s32[8,256]{1,0:T(8,128)S(1)} %get-tuple-element.17), channel_id=1, source_target_pairs={{384,0},{0,128},{128,256},{256,384},{385,1},{1,129},{129,257},{257... | collective-permute-start | bytes 24584 | tf_op jit(solution)/shard_map/ppermute | solution.py:380
  31.1 6.0 %collective-permute-start.3 = (bf16[8,128,128]{2,1,0:T(8,128)(2,1)}, bf16[8,128,128]{2,1,0:T(8,128)(2,1)S(1)}, u32[]{:S(2)}, u32[]{:S(2)}) collective-permute-start(bf16[8,128,128]{2,1,0:T(8,128)(2,1)} %all-to-all-done.mine_ref), channel_id=1, source_target_pairs={{0,64},{64,0},{1,65},{65,1},{2,66},{66,2},{3,67},{67,3},{4,68},{68... | collective-permute-start | bytes 786440 | tf_op jit(solution)/shard_map/ppermute | solution.py:397
  36.0 35.1 %copy-start.1 = (bf16[2,384,1536]{2,1,0:T(8,128)(2,1)S(1)}, bf16[2,384,1536]{2,1,0:T(8,128)(2,1)}, u32[]{:S(2)}) copy-start(bf16[2,384,1536]{2,1,0:T(8,128)(2,1)} %mlp_out_hbm.1) | copy-start | bytes 7077892
  36.0 35.1 %copy-start.2 = (bf16[2,384,384]{2,1,0:T(8,128)(2,1)S(1)}, bf16[2,384,384]{2,1,0:T(8,128)(2,1)}, u32[]{:S(2)}) copy-start(bf16[2,384,384]{2,1,0:T(8,128)(2,1)} %mlp_in_hbm.1) | copy-start | bytes 1769476
  36.0 35.1 %copy-start.5 = (bf16[48,128]{1,0:T(8,128)(2,1)S(1)}, bf16[48,128]{1,0:T(8,128)(2,1)}, u32[]{:S(2)}) copy-start(bf16[48,128]{1,0:T(8,128)(2,1)} %head_hbm.1) | copy-start | bytes 36868
  36.0 35.1 %copy-start.6 = (f32[2,384]{1,0:T(2,128)S(1)}, f32[2,384]{1,0:T(2,128)}, u32[]{:S(2)}) copy-start(f32[2,384]{1,0:T(2,128)} %gain_fm_hbm.1) | copy-start | bytes 9220
  36.0 35.1 %copy-start.7 = (f32[2,128]{1,0:T(2,128)S(1)}, f32[2,128]{1,0:T(2,128)}, u32[]{:S(2)}) copy-start(f32[2,128]{1,0:T(2,128)} %gain_out_hbm.1) | copy-start | bytes 3076
  36.0 35.1 %copy-start.8 = (f32[16]{0:T(128)S(1)}, f32[16]{0:T(128)}, u32[]{:S(2)}) copy-start(f32[16]{0:T(128)} %param.14) | copy-start | bytes 196
  108.3 5.6 %collective-permute-start.4 = (bf16[8,128,128]{2,1,0:T(8,128)(2,1)S(1)}, bf16[8,128,128]{2,1,0:T(8,128)(2,1)S(1)}, u32[]{:S(2)}, u32[]{:S(2)}) collective-permute-start(bf16[8,128,128]{2,1,0:T(8,128)(2,1)S(1)} %shard_map.128), channel_id=1, source_target_pairs={{0,64},{64,0},{1,65},{65,1},{2,66},{66,2},{3,67},{67,3},{4,68},{68... | collective-permute-start | bytes 786440 | tf_op jit(solution)/shard_map/ppermute | solution.py:441

commit v7 on v6

--- a/solution.py
+++ b/solution.py
@@ -15,7 +15,6 @@
 COLUMNS = 4
 FIELDS, BATCH, WIDTH, RANK, NF = 48, 16, 128, 8, 12
 VMEM_LIMIT = 20 * 1024 * 1024
-DENSE_LIMIT = 24 * 1024 * 1024
 
 
 def pick_kernel(rows_hbm, lens_hbm, *refs):
@@ -65,41 +64,26 @@
 
 
 def dense_kernel(
-    labels_hbm, near_hbm, mix_hbm, gain_fm_hbm, mlp_in_hbm, mlp_out_hbm, gain_out_hbm, head_hbm,
+    labels_ref, near_ref, mix_ref, gain_fm_ref, mlp_in_ref, mlp_out_ref, gain_out_ref, head_ref,
     loss_ref, back_ref,
     x_ref, t_ref, xhat_ref, rstd_ref, xb_ref, d_ref,
-    near_ref, mix_ref, gain_fm_ref, mlp_in_ref, mlp_out_ref, gain_out_ref, head_ref, labels_ref, sems,
 ):
     f32, bf16 = jnp.float32, jnp.bfloat16
     layers = mix_ref.shape[0]
     rows = FIELDS * BATCH
     chunk = 128
     lane = lax.broadcasted_iota(jnp.int32, (BATCH, WIDTH), 1) // RANK
-    pairs = (
-        (near_hbm, near_ref),
-        (mix_hbm, mix_ref),
-        (gain_fm_hbm, gain_fm_ref),
-        (mlp_in_hbm, mlp_in_ref),
-        (mlp_out_hbm.at[0], mlp_out_ref.at[0]),
-        (gain_out_hbm, gain_out_ref),
-        (mlp_out_hbm.at[1], mlp_out_ref.at[1]),
-        (head_hbm, head_ref),
-        (labels_hbm, labels_ref),
-    )
-    fetches = [pltpu.make_async_copy(*pair, sems.at[i]) for i, pair in enumerate(pairs)]
-    for fetch in fetches:
-        fetch.start()
-
-    fetches[0].wait()
-    groups = near_ref.shape[1]
+    zs, ys = near_ref.shape[:2]
+    groups = ys * zs
     tables = FIELDS // groups
     for group in range(groups):
         for table in range(tables):
             if table < COLUMNS:
-                whole = near_ref[table, group, 0]
+                whole = near_ref[group % zs, group // zs, table, 0]
             else:
                 first = 2 * (table - COLUMNS)
-                whole = near_ref[first, group, 1].astype(f32) + near_ref[first + 1, group, 1].astype(f32)
+                halves = near_ref.at[group % zs, group // zs]
+                whole = halves[first, 1].astype(f32) + halves[first + 1, 1].astype(f32)
             at = (group * tables + table) * BATCH
             xb_ref[0, at : at + BATCH] = whole.astype(bf16)
     x_ref[...] = xb_ref[0].astype(f32)
@@ -110,8 +94,6 @@
     saved = []
     for layer in range(layers):
         across = jnp.concatenate([example(x_ref, e).astype(bf16) for e in range(BATCH)], axis=1)
-        if layer == 0:
-            fetches[1].wait()
         mixed = dot(mix_ref[layer], across, ((1,), (0,)))
         for e in range(BATCH):
             t_ref[pl.ds(e, FIELDS, stride=BATCH), :] = mixed[:, e * WIDTH : (e + 1) * WIDTH]
@@ -132,18 +114,10 @@
         flat = flat - center
         rstd_fm = lax.rsqrt(jnp.mean(flat * flat, axis=1, keepdims=True) + 1e-05)
         nhat = flat * rstd_fm
-        if layer == 0:
-            fetches[2].wait()
-            fetches[3].wait()
         normed = (nhat * gain_fm_ref[layer : layer + 1]).astype(bf16)
         z = dot(normed, mlp_in_ref[layer], ((1,), (0,)))
         gate = jax.nn.sigmoid(z)
         hidden = (z * gate).astype(bf16)
-        if layer == 0:
-            fetches[4].wait()
-            fetches[5].wait()
-        if layer == 1:
-            fetches[6].wait()
         machine = dot(hidden, mlp_out_ref[layer], ((1,), (0,)))
         for n in range(NF):
             t_ref[n * BATCH : (n + 1) * BATCH] = machine[:, n * WIDTH : (n + 1) * WIDTH]
@@ -162,8 +136,6 @@
         saved.append((summary, nhat, rstd_fm, z, gate))
 
     acc = jnp.zeros((BATCH, WIDTH), f32)
-    fetches[7].wait()
-    fetches[8].wait()
     head = head_ref[...].astype(f32)
     for t in range(FIELDS):
         acc = acc + x_ref[t * BATCH : (t + 1) * BATCH] * head[t : t + 1]
@@ -235,7 +207,7 @@
         for column in range(COLUMNS):
             for half, table in enumerate((column, COLUMNS + column // 2)):
                 at = (group * tables + table) * BATCH
-                back_ref[column, group, half] = x_ref[at : at + BATCH].astype(bf16)
+                back_ref[group % zs, group // zs, column, half] = x_ref[at : at + BATCH].astype(bf16)
 
 
 def mix_of(proj, compress):
@@ -285,29 +257,37 @@
     lax.fori_loop(0, rows // 256, per_window, 0)
 
 
-def by_column(first_ref, last_ref, owned):
+def by_column(first_ref, last_ref):
     each = last_ref.shape[1]
     column = lax.axis_index("x")
     for hop in range(COLUMNS):
         ref, at = (first_ref, hop * each) if hop < COLUMNS - 1 else (last_ref, 0)
-        yield ref, slice(at, at + each), pl.ds(((column + hop) & (COLUMNS - 1)) * owned, owned)
+        yield ref, slice(at, at + each), (column + hop) & (COLUMNS - 1)
 
 
 def pool_kernel(first_ref, last_ref, mine_ref, other_ref, pools_ref):
     share = first_ref.shape[0] // 2
-    owned = pools_ref.shape[0] // COLUMNS
-    for ref, cut, owners in by_column(first_ref, last_ref, owned):
+    zs, ys, _, pairs = pools_ref.shape[:4]
+    for ref, cut, column in by_column(first_ref, last_ref):
         total = dot(ref[:share, cut], mine_ref[...].reshape(share, WIDTH), ((0,), (0,)))
         total += dot(ref[share:, cut], other_ref[...].reshape(share, WIDTH), ((0,), (0,)))
-        pools_ref[owners] = total.astype(jnp.bfloat16).reshape(owned, BATCH, WIDTH)
+        total = total.astype(jnp.bfloat16).reshape(ys, zs, pairs, BATCH, WIDTH)
+        for y in range(ys):
+            for z in range(zs):
+                pools_ref[z, y, column] = total[y, z]
 
 
 def grads_kernel(side, first_ref, last_ref, moved_ref, out_ref):
     share = first_ref.shape[0] // 2
-    owned = moved_ref.shape[0] // COLUMNS
+    zs, ys, _, pairs = moved_ref.shape[:4]
     total = jnp.zeros((share, WIDTH), jnp.float32)
-    for ref, cut, owners in by_column(first_ref, last_ref, owned):
-        grads = moved_ref[owners].reshape(owned * BATCH, WIDTH)
+    for ref, cut, column in by_column(first_ref, last_ref):
+        parts = [
+            moved_ref[z, y, column].reshape(pairs * BATCH, WIDTH)
+            for y in range(ys)
+            for z in range(zs)
+        ]
+        grads = jnp.concatenate(parts, axis=0)
         total += dot(ref[side * share : side * share + share, cut], grads, ((1,), (0,)))
     out_ref[...] = total.astype(jnp.bfloat16).reshape(out_ref.shape)
 
@@ -349,8 +329,12 @@
     share = rows_dev // 2
     owners = groups * pairs
     piece = shape((quads * pairs, share, width), bf16)
-    per_owner = shape((COLUMNS * owners, BATCH, width), bf16)
-    exchange = ("x",) + GRP + ("pair",)
+    per_owner = shape((2, 4, COLUMNS, pairs, BATCH, width), bf16)
+    exchange = ("zhi", "y", "x", "pair")
+
+    def swap_owners(values):
+        flat = values.reshape(COLUMNS * owners, BATCH, width)
+        return swap(flat, exchange).reshape(per_owner.shape)
 
     def of_table(table, first, count):
         return lax.dynamic_slice(table_rows, (table, first, 0), (1, count, width))
@@ -374,7 +358,6 @@
             pltpu.VMEM((tables, 8, owners * BATCH), jnp.int32),
             pltpu.SemaphoreType.DMA((2,)),
         ],
-        DENSE_LIMIT,
     )
     bags = [coded[0]] + [
         lax.ppermute(coded[hop], "x", [((i + hop) % COLUMNS, i) for i in range(COLUMNS)])
@@ -398,13 +381,13 @@
     last = count([late])
     other, last, mix = lax.optimization_barrier((other, last, mix_of(proj, compress)))
     pools = call(pool_kernel, per_owner, "vvvv", (first, last, gathered, other))
-    near = swap(pools, exchange).reshape(COLUMNS, groups, pairs, BATCH, width)
+    near = swap_owners(pools)
 
     rows = FIELDS * BATCH
     losses, back = call(
         dense_kernel,
         (shape((1, BATCH), f32), shape(near.shape, bf16)),
-        "h" * 8,
+        "v" * 8,
         (
             labels.reshape(1, BATCH),
             near,
@@ -422,20 +405,10 @@
             pltpu.VMEM((layers, rows, 1), f32),
             pltpu.VMEM((layers + 1, rows, WIDTH), bf16),
             pltpu.VMEM((rows, WIDTH), bf16),
-            pltpu.VMEM(near.shape, bf16),
-            pltpu.VMEM(mix.shape, bf16),
-            pltpu.VMEM(gain_fm.shape, f32),
-            pltpu.VMEM(mlp_in.shape, bf16),
-            pltpu.VMEM(mlp_out.shape, bf16),
-            pltpu.VMEM(gain_out.shape, f32),
-            pltpu.VMEM(head.shape, bf16),
-            pltpu.VMEM((1, BATCH), f32),
-            pltpu.SemaphoreType.DMA((9,)),
         ],
-        DENSE_LIMIT,
-    )
-
-    returned = swap(back.reshape(per_owner.shape), exchange)
+    )
+
+    returned = swap_owners(back)
     operands = (first, last, returned)
     other = call(functools.partial(grads_kernel, 1), piece, "vvv", operands)
     other = lax.ppermute(other, "core", across)

time: 153 us -> 151 us (0.987)
  blocking collectives: 98.5 us -> 96.3 us
    all_to_all x4, blocking collectives: 98.5 us -> 96.3 us  [swap(): return lax.all_to_all(values, axes, split_axis=0, concat_axis=0, tiled=True)]
where the time goes in v7:
time: 151 us
  blocking collectives  96.3 us (64%)
  starting transfers between devices  32.3 us (21%)
  Pallas kernels  14.1 us (9%)
  local copies, waits for them, and re-layouts  4.32 us (3%)
  waiting for transfers between devices  1.76 us (1%)
    all_to_all x4, blocking collectives, swap(): return lax.all_to_all(values, axes, split_axis=0, concat_axis=0, tiled=True)  96.3 us
    pallas_call x8, Pallas kernels, call(): pl.pallas_call(kernel, out_shape=out_shape, in_specs=[{'s': smem, 'v': vm...  14.1 us
    all_to_all x1, starting transfers between devices, swap(): return lax.all_to_all(values, axes, split_axis=0, concat_axis=0, tiled=True)  13.1 us
    ppermute x3, starting transfers between devices, per_device(): lax.ppermute(coded[hop], 'x', [((i + hop) % COLUMNS, i) for i in range(CO...  9.33 us
    ppermute x1, starting transfers between devices, per_device(): other = lax.ppermute(other, 'core', across)  5.82 us
    ppermute x1, starting transfers between devices, per_device(): other = lax.ppermute(gathered, 'core', across)  4.05 us
    unnamed x21, local copies, waits for them, and re-layouts  3.41 us
  transfers between devices with their start and end apart: 6, of which 2 were waited for; matrix products, arithmetic and copies ran while one was open for 1% of the time, Pallas kernels for 3%

profile of v7, /device:TPU:1, one launch (start us, length us, event | category | flops | bytes accessed | tf_op | source)
XLA Modules:
  0.0 150.7 jit_solution(10858413750976918866)
XLA Ops:
  0.6 0.0 copy-start
  0.7 1.0 copy-done
  1.6 0.7 broadcast_in_dim.9
  2.4 13.1 %all-to-all-start = ((bf16[8,128,128]{2,1,0:T(8,128)(2,1)}), bf16[8,128,128]{2,1,0:T(8,128)(2,1)}, u32[]{:S(2)}, u32[]{:S(2)}) async-start(bf16[8,128,128]{2,1,0:T(8,128)(2,1)} %bitcast.1), calls=%async_computation | async-start | bytes 524288 | tf_op jit(solution)/shard_map/all_to_all | solution.py:302
  15.5 0.9 copy-done.3
  16.4 0.8 copy-done.4
  17.1 0.4 shard_map.122
  17.6 4.4 %collective-permute-start = (s32[8,256]{1,0:T(8,128)S(1)}, s32[8,256]{1,0:T(8,128)S(1)}, u32[]{:S(2)}, u32[]{:S(2)}) collective-permute-start(s32[8,256]{1,0:T(8,128)S(1)} %get-tuple-element.15), channel_id=1, source_target_pairs={{128,0},{256,128},{384,256},{0,384},{129,1},{257,129},{385,257},{1... | collective-permute-start | bytes 24584 | tf_op jit(solution)/shard_map/ppermute | solution.py:363
  22.0 2.4 %collective-permute-start.1 = (s32[8,256]{1,0:T(8,128)S(1)}, s32[8,256]{1,0:T(8,128)S(1)}, u32[]{:S(2)}, u32[]{:S(2)}) collective-permute-start(s32[8,256]{1,0:T(8,128)S(1)} %get-tuple-element.16), channel_id=1, source_target_pairs={{256,0},{384,128},{0,256},{128,384},{257,1},{385,129},{1,257},{129... | collective-permute-start | bytes 24584 | tf_op jit(solution)/shard_map/ppermute | solution.py:363
  24.4 2.5 %collective-permute-start.2 = (s32[8,256]{1,0:T(8,128)S(1)}, s32[8,256]{1,0:T(8,128)S(1)}, u32[]{:S(2)}, u32[]{:S(2)}) collective-permute-start(s32[8,256]{1,0:T(8,128)S(1)} %get-tuple-element.17), channel_id=1, source_target_pairs={{384,0},{0,128},{128,256},{256,384},{385,1},{1,129},{129,257},{257... | collective-permute-start | bytes 24584 | tf_op jit(solution)/shard_map/ppermute | solution.py:363
  26.9 1.3 collective-permute-done.1.refs_2_
  28.3 2.8 %shard_map.123.first_ref = bf16[2048,768]{1,0:T(8,128)(2,1)S(1)} custom-call(s32[8,256]{1,0:T(8,128)S(1)} %get-tuple-element.14.refs_0_, s32[8,256]{1,0:T(8,128)S(1)} %collective-permute-done.refs_1_, s32[8,256]{1,0:T(8,128)S(1)} %collective-permute-done.1.refs_2_), custom_call_target="tpu_custom_call" | custom-call | tf_op jit(solution)/shard_map/pallas_call | solution.py:310
  31.1 4.0 %collective-permute-start.3 = (bf16[8,128,128]{2,1,0:T(8,128)(2,1)}, bf16[8,128,128]{2,1,0:T(8,128)(2,1)S(1)}, u32[]{:S(2)}, u32[]{:S(2)}) collective-permute-start(bf16[8,128,128]{2,1,0:T(8,128)(2,1)} %all-to-all-done.mine_ref), channel_id=1, source_target_pairs={{0,64},{64,0},{1,65},{65,1},{2,66},{66,2},{3,67},{67,3},{4,68},{68... | collective-permute-start | bytes 786440 | tf_op jit(solution)/shard_map/ppermute | solution.py:380
  35.1 0.7 copy.13
  35.8 0.1 pad.10.clone
  35.9 0.1 pad_maximum_fusion.1.mix_ref
  36.0 0.0 copy-start.6
  36.0 0.0 copy-start.7
  36.1 1.0 shard_map.124.last_ref
  37.1 2.2 %shard_map.125 = bf16[2,4,4,2,16,128]{5,4,3,2,1,0:T(8,128)(2,1)S(1)} custom-call(bf16[2048,768]{1,0:T(8,128)(2,1)S(1)} %shard_map.123.first_ref, bf16[2048,256]{1,0:T(8,128)(2,1)S(1)} %shard_map.124.last_ref, bf16[8,128,128]{2,1,0:T(8,128)(2,1)} %all-to-all-done.mine_ref, bf16[8,128,128]{2,1,0:T(8,128)(2,1)S(1)} %collective-permute-done.3.other_ref), custom_call_target="tpu_custom_call" | custom-call | tf_op jit(solution)/shard_map/pallas_call | solution.py:310
  39.3 30.9 %all_to_all.25 = bf16[64,16,128]{2,1,0:T(8,128)(2,1)S(1)} all-to-all(bf16[64,16,128]{2,1,0:T(8,128)(2,1)S(1)} %bitcast.19), channel_id=1, replica_groups=mesh['x'=4,'core'=2,'y'=4,'zhi'=2,'quad'=4,'pair'=2] {'zhi','y','x','pair'}, dimensions={0} | all-to-all | bytes 524288 | tf_op jit(solution)/shard_map/all_to_all | solution.py:302
  70.2 6.2 %shard_map.126 = (f32[1,16]{1,0:T(1,128)}, bf16[2,4,4,2,16,128]{5,4,3,2,1,0:T(8,128)(2,1)S(1)}) custom-call(f32[1,16]{1,0:T(1,128)S(1)} %bitcast.24, bf16[2,4,4,2,16,128]{5,4,3,2,1,0:T(8,128)(2,1)S(1)} %bitcast.20, bf16[2,48,48]{2,1,0:T(8,128)(2,1)S(1)} %pad_maximum_fusion.1.mix_ref, f32[2,384]{1,0:T(2,128)S(1)} %copy-done.6, ...), custom_call_target="tpu_custom_call" | custom-call | tf_op jit(solution)/shard_map/pallas_call | solution.py:310
  76.5 28.4 %all_to_all.26 = bf16[64,16,128]{2,1,0:T(8,128)(2,1)S(1)} all-to-all(bf16[64,16,128]{2,1,0:T(8,128)(2,1)S(1)} %bitcast.21), channel_id=1, replica_groups=mesh['x'=4,'core'=2,'y'=4,'zhi'=2,'quad'=4,'pair'=2] {'zhi','y','x','pair'}, dimensions={0} | all-to-all | bytes 524288 | tf_op jit(solution)/shard_map/all_to_all | solution.py:302
  104.9 0.7 shard_map.128
  105.6 5.8 %collective-permute-start.4 = (bf16[8,128,128]{2,1,0:T(8,128)(2,1)S(1)}, bf16[8,128,128]{2,1,0:T(8,128)(2,1)S(1)}, u32[]{:S(2)}, u32[]{:S(2)}) collective-permute-start(bf16[8,128,128]{2,1,0:T(8,128)(2,1)S(1)} %shard_map.128), channel_id=1, source_target_pairs={{0,64},{64,0},{1,65},{65,1},{2,66},{66,2},{3,67},{67,3},{4,68},{68... | collective-permute-start | bytes 786440 | tf_op jit(solution)/shard_map/ppermute | solution.py:414
  111.4 0.7 shard_map.127.left_ref
  112.1 0.4 collective-permute-done.4.right_ref
  112.6 0.1 shard_map.129
  112.6 23.0 %all_to_all.27 = bf16[8,128,128]{2,1,0:T(8,128)(2,1)S(1)} all-to-all(bf16[8,128,128]{2,1,0:T(8,128)(2,1)S(1)} %shard_map.129), channel_id=1, replica_groups=mesh['x'=4,'core'=2,'y'=4,'zhi'=2,'quad'=4,'pair'=2] {'quad','pair'}, dimensions={0} | all-to-all | bytes 524288 | tf_op jit(solution)/shard_map/all_to_all | solution.py:302
  135.7 0.1 broadcast_in_dim.11
  135.7 14.0 %all_to_all.28 = bf16[8,192,128]{2,1,0:T(8,128)(2,1)S(1)} all-to-all(bf16[8,192,128]{2,1,0:T(8,128)(2,1)S(1)} %broadcast_in_dim.11), channel_id=1, replica_groups=mesh['x'=4,'core'=2,'y'=4,'zhi'=2,'quad'=4,'pair'=2] {'x','core'}, dimensions={0} | all-to-all | bytes 786432 | tf_op jit(solution)/shard_map/all_to_all | solution.py:302
  149.8 0.9 maximum_convert_fusion
  (28 shorter events, 0.1 us)
Async XLA Ops:
  0.6 1.0 copy-start
  0.6 35.3 %copy-start.9 = (bf16[2,48,8]{1,2,0:T(8,128)(2,1)S(1)}, bf16[2,48,8]{1,2,0:T(8,128)(2,1)}, u32[]{:S(2)}) copy-start(bf16[2,48,8]{1,2,0:T(8,128)(2,1)} %param.15) | copy-start | bytes 4612
  2.4 28.7 %all-to-all-start = ((bf16[8,128,128]{2,1,0:T(8,128)(2,1)}), bf16[8,128,128]{2,1,0:T(8,128)(2,1)}, u32[]{:S(2)}, u32[]{:S(2)}) async-start(bf16[8,128,128]{2,1,0:T(8,128)(2,1)} %bitcast.1), calls=%async_computation | async-start | bytes 524288 | tf_op jit(solution)/shard_map/all_to_all | solution.py:302
  15.5 0.9 copy-start.3
  16.4 0.8 copy-start.4
  17.6 9.4 %collective-permute-start = (s32[8,256]{1,0:T(8,128)S(1)}, s32[8,256]{1,0:T(8,128)S(1)}, u32[]{:S(2)}, u32[]{:S(2)}) collective-permute-start(s32[8,256]{1,0:T(8,128)S(1)} %get-tuple-element.15), channel_id=1, source_target_pairs={{128,0},{256,128},{384,256},{0,384},{129,1},{257,129},{385,257},{1... | collective-permute-start | bytes 24584 | tf_op jit(solution)/shard_map/ppermute | solution.py:363
  22.0 6.3 %collective-permute-start.1 = (s32[8,256]{1,0:T(8,128)S(1)}, s32[8,256]{1,0:T(8,128)S(1)}, u32[]{:S(2)}, u32[]{:S(2)}) collective-permute-start(s32[8,256]{1,0:T(8,128)S(1)} %get-tuple-element.16), channel_id=1, source_target_pairs={{256,0},{384,128},{0,256},{128,384},{257,1},{385,129},{1,257},{129... | collective-permute-start | bytes 24584 | tf_op jit(solution)/shard_map/ppermute | solution.py:363
  24.4 6.6 %collective-permute-start.2 = (s32[8,256]{1,0:T(8,128)S(1)}, s32[8,256]{1,0:T(8,128)S(1)}, u32[]{:S(2)}, u32[]{:S(2)}) collective-permute-start(s32[8,256]{1,0:T(8,128)S(1)} %get-tuple-element.17), channel_id=1, source_target_pairs={{384,0},{0,128},{128,256},{256,384},{385,1},{1,129},{129,257},{257... | collective-permute-start | bytes 24584 | tf_op jit(solution)/shard_map/ppermute | solution.py:363
  31.1 6.0 %collective-permute-start.3 = (bf16[8,128,128]{2,1,0:T(8,128)(2,1)}, bf16[8,128,128]{2,1,0:T(8,128)(2,1)S(1)}, u32[]{:S(2)}, u32[]{:S(2)}) collective-permute-start(bf16[8,128,128]{2,1,0:T(8,128)(2,1)} %all-to-all-done.mine_ref), channel_id=1, source_target_pairs={{0,64},{64,0},{1,65},{65,1},{2,66},{66,2},{3,67},{67,3},{4,68},{68... | collective-permute-start | bytes 786440 | tf_op jit(solution)/shard_map/ppermute | solution.py:380
  36.0 34.2 %copy-start.1 = (bf16[2,384,1536]{2,1,0:T(8,128)(2,1)S(1)}, bf16[2,384,1536]{2,1,0:T(8,128)(2,1)}, u32[]{:S(2)}) copy-start(bf16[2,384,1536]{2,1,0:T(8,128)(2,1)} %mlp_out_ref.1) | copy-start | bytes 7077892
  36.0 34.2 %copy-start.2 = (bf16[2,384,384]{2,1,0:T(8,128)(2,1)S(1)}, bf16[2,384,384]{2,1,0:T(8,128)(2,1)}, u32[]{:S(2)}) copy-start(bf16[2,384,384]{2,1,0:T(8,128)(2,1)} %mlp_in_ref.1) | copy-start | bytes 1769476
  36.0 34.2 %copy-start.5 = (bf16[48,128]{1,0:T(8,128)(2,1)S(1)}, bf16[48,128]{1,0:T(8,128)(2,1)}, u32[]{:S(2)}) copy-start(bf16[48,128]{1,0:T(8,128)(2,1)} %head_ref.1) | copy-start | bytes 36868
  36.0 34.2 %copy-start.6 = (f32[2,384]{1,0:T(2,128)S(1)}, f32[2,384]{1,0:T(2,128)}, u32[]{:S(2)}) copy-start(f32[2,384]{1,0:T(2,128)} %gain_fm_ref.1) | copy-start | bytes 9220
  36.0 34.2 %copy-start.7 = (f32[2,128]{1,0:T(2,128)S(1)}, f32[2,128]{1,0:T(2,128)}, u32[]{:S(2)}) copy-start(f32[2,128]{1,0:T(2,128)} %gain_out_ref.1) | copy-start | bytes 3076
  36.0 34.2 %copy-start.8 = (f32[16]{0:T(128)S(1)}, f32[16]{0:T(128)}, u32[]{:S(2)}) copy-start(f32[16]{0:T(128)} %param.14) | copy-start | bytes 196
  105.6 7.0 %collective-permute-start.4 = (bf16[8,128,128]{2,1,0:T(8,128)(2,1)S(1)}, bf16[8,128,128]{2,1,0:T(8,128)(2,1)S(1)}, u32[]{:S(2)}, u32[]{:S(2)}) collective-permute-start(bf16[8,128,128]{2,1,0:T(8,128)(2,1)S(1)} %shard_map.128), channel_id=1, source_target_pairs={{0,64},{64,0},{1,65},{65,1},{2,66},{66,2},{3,67},{67,3},{4,68},{68... | collective-permute-start | bytes 786440 | tf_op jit(solution)/shard_map/ppermute | solution.py:414

commit v8 on v7

--- a/solution.py
+++ b/solution.py
@@ -13,6 +13,7 @@
 SUB = ("quad", "pair")
 DEAD = 4095
 COLUMNS = 4
+HOPS = (0, 1, 3, 2)
 FIELDS, BATCH, WIDTH, RANK, NF = 48, 16, 128, 8, 12
 VMEM_LIMIT = 20 * 1024 * 1024
 
@@ -43,9 +44,9 @@
                 moved = pltpu.roll(coded, (run * 32 - quad * 32) & 127, 1)
                 kept = jnp.where(lanes // 32 == run, moved, kept)
             kept_ref[table, :, group * 128 : group * 128 + 128] = kept
-    for hop in range(COLUMNS):
+    for at, hop in enumerate(HOPS):
         target = (column - hop) & (COLUMNS - 1)
-        outs[hop][...] = kept_ref[jnp.where(pair == 0, target, COLUMNS + (target >> 1))]
+        outs[at][...] = kept_ref[jnp.where(pair == 0, target, COLUMNS + (target >> 1))]
 
 
 def dot(a, b, dims):
@@ -260,8 +261,8 @@
 def by_column(first_ref, last_ref):
     each = last_ref.shape[1]
     column = lax.axis_index("x")
-    for hop in range(COLUMNS):
-        ref, at = (first_ref, hop * each) if hop < COLUMNS - 1 else (last_ref, 0)
+    for i, hop in enumerate(HOPS):
+        ref, at = (first_ref, i * each) if i < COLUMNS - 1 else (last_ref, 0)
         yield ref, slice(at, at + each), (column + hop) & (COLUMNS - 1)
 
 
@@ -360,8 +361,8 @@
         ],
     )
     bags = [coded[0]] + [
-        lax.ppermute(coded[hop], "x", [((i + hop) % COLUMNS, i) for i in range(COLUMNS)])
-        for hop in range(1, COLUMNS)
+        lax.ppermute(mine, "x", [((i + hop) % COLUMNS, i) for i in range(COLUMNS)])
+        for mine, hop in zip(coded[1:], HOPS[1:])
     ]
     each = owners * BATCH
 

time: 151 us -> 153 us (1.013)
  starting transfers between devices: 32.3 us -> 35 us
    ppermute x1, starting transfers between devices: 5.82 us -> 7.68 us  [per_device(): other = lax.ppermute(other, 'core', across)]
where the time goes in v8:
time: 153 us
  blocking collectives  96.3 us (63%)
  starting transfers between devices  35 us (23%)
  Pallas kernels  14.1 us (9%)
  local copies, waits for them, and re-layouts  4.32 us (3%)
    all_to_all x4, blocking collectives, swap(): return lax.all_to_all(values, axes, split_axis=0, concat_axis=0, tiled=True)  96.3 us
    pallas_call x8, Pallas kernels, call(): pl.pallas_call(kernel, out_shape=out_shape, in_specs=[{'s': smem, 'v': vm...  14.1 us
    all_to_all x1, starting transfers between devices, swap(): return lax.all_to_all(values, axes, split_axis=0, concat_axis=0, tiled=True)  13.1 us
    ppermute x3, starting transfers between devices, per_device(): lax.ppermute(mine, 'x', [((i + hop) % COLUMNS, i) for i in range(COLUMNS)])  9.93 us
    ppermute x1, starting transfers between devices, per_device(): other = lax.ppermute(other, 'core', across)  7.68 us
    ppermute x1, starting transfers between devices, per_device(): other = lax.ppermute(gathered, 'core', across)  4.34 us
    unnamed x21, local copies, waits for them, and re-layouts  3.41 us
  transfers between devices with their start and end apart: 6, of which 2 were waited for; matrix products, arithmetic and copies ran while one was open for 1% of the time, Pallas kernels for 3%

profile of v8, /device:TPU:1, one launch (start us, length us, event | category | flops | bytes accessed | tf_op | source)
XLA Modules:
  0.0 152.6 jit_solution(8544512456701548087)
XLA Ops:
  0.6 0.0 copy-start
  0.7 1.0 copy-done
  1.6 0.7 broadcast_in_dim.9
  2.4 13.1 %all-to-all-start = ((bf16[8,128,128]{2,1,0:T(8,128)(2,1)}), bf16[8,128,128]{2,1,0:T(8,128)(2,1)}, u32[]{:S(2)}, u32[]{:S(2)}) async-start(bf16[8,128,128]{2,1,0:T(8,128)(2,1)} %bitcast.1), calls=%async_computation | async-start | bytes 524288 | tf_op jit(solution)/shard_map/all_to_all | solution.py:303
  15.5 0.9 copy-done.3
  16.4 0.8 copy-done.4
  17.1 0.4 shard_map.122
  17.6 4.4 %collective-permute-start = (s32[8,256]{1,0:T(8,128)S(1)}, s32[8,256]{1,0:T(8,128)S(1)}, u32[]{:S(2)}, u32[]{:S(2)}) collective-permute-start(s32[8,256]{1,0:T(8,128)S(1)} %get-tuple-element.15), channel_id=1, source_target_pairs={{128,0},{256,128},{384,256},{0,384},{129,1},{257,129},{385,257},{1... | collective-permute-start | bytes 24584 | tf_op jit(solution)/shard_map/ppermute | solution.py:364
  22.0 1.9 %collective-permute-start.1 = (s32[8,256]{1,0:T(8,128)S(1)}, s32[8,256]{1,0:T(8,128)S(1)}, u32[]{:S(2)}, u32[]{:S(2)}) collective-permute-start(s32[8,256]{1,0:T(8,128)S(1)} %get-tuple-element.16), channel_id=1, source_target_pairs={{384,0},{0,128},{128,256},{256,384},{385,1},{1,129},{129,257},{257... | collective-permute-start | bytes 24584 | tf_op jit(solution)/shard_map/ppermute | solution.py:364
  23.9 3.6 %collective-permute-start.2 = (s32[8,256]{1,0:T(8,128)S(1)}, s32[8,256]{1,0:T(8,128)S(1)}, u32[]{:S(2)}, u32[]{:S(2)}) collective-permute-start(s32[8,256]{1,0:T(8,128)S(1)} %get-tuple-element.17), channel_id=1, source_target_pairs={{256,0},{384,128},{0,256},{128,384},{257,1},{385,129},{1,257},{129... | collective-permute-start | bytes 24584 | tf_op jit(solution)/shard_map/ppermute | solution.py:364
  27.5 0.4 collective-permute-done.1.refs_2_
  28.0 2.8 %shard_map.123.first_ref = bf16[2048,768]{1,0:T(8,128)(2,1)S(1)} custom-call(s32[8,256]{1,0:T(8,128)S(1)} %get-tuple-element.14.refs_0_, s32[8,256]{1,0:T(8,128)S(1)} %collective-permute-done.refs_1_, s32[8,256]{1,0:T(8,128)S(1)} %collective-permute-done.1.refs_2_), custom_call_target="tpu_custom_call" | custom-call | tf_op jit(solution)/shard_map/pallas_call | solution.py:311
  30.8 4.3 %collective-permute-start.3 = (bf16[8,128,128]{2,1,0:T(8,128)(2,1)}, bf16[8,128,128]{2,1,0:T(8,128)(2,1)S(1)}, u32[]{:S(2)}, u32[]{:S(2)}) collective-permute-start(bf16[8,128,128]{2,1,0:T(8,128)(2,1)} %all-to-all-done.mine_ref), channel_id=1, source_target_pairs={{0,64},{64,0},{1,65},{65,1},{2,66},{66,2},{3,67},{67,3},{4,68},{68... | collective-permute-start | bytes 786440 | tf_op jit(solution)/shard_map/ppermute | solution.py:381
  35.1 0.7 copy.13
  35.8 0.1 pad.10.clone
  35.9 0.1 pad_maximum_fusion.1.mix_ref
  36.0 0.0 copy-start.6
  36.0 0.0 copy-start.7
  36.1 1.0 shard_map.124.last_ref
  37.1 2.2 %shard_map.125 = bf16[2,4,4,2,16,128]{5,4,3,2,1,0:T(8,128)(2,1)S(1)} custom-call(bf16[2048,768]{1,0:T(8,128)(2,1)S(1)} %shard_map.123.first_ref, bf16[2048,256]{1,0:T(8,128)(2,1)S(1)} %shard_map.124.last_ref, bf16[8,128,128]{2,1,0:T(8,128)(2,1)} %all-to-all-done.mine_ref, bf16[8,128,128]{2,1,0:T(8,128)(2,1)S(1)} %collective-permute-done.3.other_ref), custom_call_target="tpu_custom_call" | custom-call | tf_op jit(solution)/shard_map/pallas_call | solution.py:311
  39.3 31.0 %all_to_all.25 = bf16[64,16,128]{2,1,0:T(8,128)(2,1)S(1)} all-to-all(bf16[64,16,128]{2,1,0:T(8,128)(2,1)S(1)} %bitcast.19), channel_id=1, replica_groups=mesh['x'=4,'core'=2,'y'=4,'zhi'=2,'quad'=4,'pair'=2] {'zhi','y','x','pair'}, dimensions={0} | all-to-all | bytes 524288 | tf_op jit(solution)/shard_map/all_to_all | solution.py:303
  70.4 6.2 %shard_map.126 = (f32[1,16]{1,0:T(1,128)}, bf16[2,4,4,2,16,128]{5,4,3,2,1,0:T(8,128)(2,1)S(1)}) custom-call(f32[1,16]{1,0:T(1,128)S(1)} %bitcast.24, bf16[2,4,4,2,16,128]{5,4,3,2,1,0:T(8,128)(2,1)S(1)} %bitcast.20, bf16[2,48,48]{2,1,0:T(8,128)(2,1)S(1)} %pad_maximum_fusion.1.mix_ref, f32[2,384]{1,0:T(2,128)S(1)} %copy-done.6, ...), custom_call_target="tpu_custom_call" | custom-call | tf_op jit(solution)/shard_map/pallas_call | solution.py:311
  76.6 28.0 %all_to_all.26 = bf16[64,16,128]{2,1,0:T(8,128)(2,1)S(1)} all-to-all(bf16[64,16,128]{2,1,0:T(8,128)(2,1)S(1)} %bitcast.21), channel_id=1, replica_groups=mesh['x'=4,'core'=2,'y'=4,'zhi'=2,'quad'=4,'pair'=2] {'zhi','y','x','pair'}, dimensions={0} | all-to-all | bytes 524288 | tf_op jit(solution)/shard_map/all_to_all | solution.py:303
  104.6 0.7 shard_map.128
  105.3 7.7 %collective-permute-start.4 = (bf16[8,128,128]{2,1,0:T(8,128)(2,1)S(1)}, bf16[8,128,128]{2,1,0:T(8,128)(2,1)S(1)}, u32[]{:S(2)}, u32[]{:S(2)}) collective-permute-start(bf16[8,128,128]{2,1,0:T(8,128)(2,1)S(1)} %shard_map.128), channel_id=1, source_target_pairs={{0,64},{64,0},{1,65},{65,1},{2,66},{66,2},{3,67},{67,3},{4,68},{68... | collective-permute-start | bytes 786440 | tf_op jit(solution)/shard_map/ppermute | solution.py:415
  113.0 0.7 shard_map.127.left_ref
  113.7 0.4 collective-permute-done.4.right_ref
  114.2 0.1 shard_map.129
  114.2 23.2 %all_to_all.27 = bf16[8,128,128]{2,1,0:T(8,128)(2,1)S(1)} all-to-all(bf16[8,128,128]{2,1,0:T(8,128)(2,1)S(1)} %shard_map.129), channel_id=1, replica_groups=mesh['x'=4,'core'=2,'y'=4,'zhi'=2,'quad'=4,'pair'=2] {'quad','pair'}, dimensions={0} | all-to-all | bytes 524288 | tf_op jit(solution)/shard_map/all_to_all | solution.py:303
  137.5 0.1 broadcast_in_dim.11
  137.5 14.1 %all_to_all.28 = bf16[8,192,128]{2,1,0:T(8,128)(2,1)S(1)} all-to-all(bf16[8,192,128]{2,1,0:T(8,128)(2,1)S(1)} %broadcast_in_dim.11), channel_id=1, replica_groups=mesh['x'=4,'core'=2,'y'=4,'zhi'=2,'quad'=4,'pair'=2] {'x','core'}, dimensions={0} | all-to-all | bytes 786432 | tf_op jit(solution)/shard_map/all_to_all | solution.py:303
  151.7 0.9 maximum_convert_fusion
  (28 shorter events, 0.1 us)
Async XLA Ops:
  0.6 1.0 copy-start
  0.6 35.3 %copy-start.9 = (bf16[2,48,8]{1,2,0:T(8,128)(2,1)S(1)}, bf16[2,48,8]{1,2,0:T(8,128)(2,1)}, u32[]{:S(2)}) copy-start(bf16[2,48,8]{1,2,0:T(8,128)(2,1)} %param.15) | copy-start | bytes 4612
  2.4 28.4 %all-to-all-start = ((bf16[8,128,128]{2,1,0:T(8,128)(2,1)}), bf16[8,128,128]{2,1,0:T(8,128)(2,1)}, u32[]{:S(2)}, u32[]{:S(2)}) async-start(bf16[8,128,128]{2,1,0:T(8,128)(2,1)} %bitcast.1), calls=%async_computation | async-start | bytes 524288 | tf_op jit(solution)/shard_map/all_to_all | solution.py:303
  15.5 0.9 copy-start.3
  16.4 0.8 copy-start.4
  17.6 10.0 %collective-permute-start = (s32[8,256]{1,0:T(8,128)S(1)}, s32[8,256]{1,0:T(8,128)S(1)}, u32[]{:S(2)}, u32[]{:S(2)}) collective-permute-start(s32[8,256]{1,0:T(8,128)S(1)} %get-tuple-element.15), channel_id=1, source_target_pairs={{128,0},{256,128},{384,256},{0,384},{129,1},{257,129},{385,257},{1... | collective-permute-start | bytes 24584 | tf_op jit(solution)/shard_map/ppermute | solution.py:364
  22.0 6.0 %collective-permute-start.1 = (s32[8,256]{1,0:T(8,128)S(1)}, s32[8,256]{1,0:T(8,128)S(1)}, u32[]{:S(2)}, u32[]{:S(2)}) collective-permute-start(s32[8,256]{1,0:T(8,128)S(1)} %get-tuple-element.16), channel_id=1, source_target_pairs={{384,0},{0,128},{128,256},{256,384},{385,1},{1,129},{129,257},{257... | collective-permute-start | bytes 24584 | tf_op jit(solution)/shard_map/ppermute | solution.py:364
  23.9 6.9 %collective-permute-start.2 = (s32[8,256]{1,0:T(8,128)S(1)}, s32[8,256]{1,0:T(8,128)S(1)}, u32[]{:S(2)}, u32[]{:S(2)}) collective-permute-start(s32[8,256]{1,0:T(8,128)S(1)} %get-tuple-element.17), channel_id=1, source_target_pairs={{256,0},{384,128},{0,256},{128,384},{257,1},{385,129},{1,257},{129... | collective-permute-start | bytes 24584 | tf_op jit(solution)/shard_map/ppermute | solution.py:364
  30.8 6.3 %collective-permute-start.3 = (bf16[8,128,128]{2,1,0:T(8,128)(2,1)}, bf16[8,128,128]{2,1,0:T(8,128)(2,1)S(1)}, u32[]{:S(2)}, u32[]{:S(2)}) collective-permute-start(bf16[8,128,128]{2,1,0:T(8,128)(2,1)} %all-to-all-done.mine_ref), channel_id=1, source_target_pairs={{0,64},{64,0},{1,65},{65,1},{2,66},{66,2},{3,67},{67,3},{4,68},{68... | collective-permute-start | bytes 786440 | tf_op jit(solution)/shard_map/ppermute | solution.py:381
  36.0 34.3 %copy-start.1 = (bf16[2,384,1536]{2,1,0:T(8,128)(2,1)S(1)}, bf16[2,384,1536]{2,1,0:T(8,128)(2,1)}, u32[]{:S(2)}) copy-start(bf16[2,384,1536]{2,1,0:T(8,128)(2,1)} %mlp_out_ref.1) | copy-start | bytes 7077892
  36.0 34.3 %copy-start.2 = (bf16[2,384,384]{2,1,0:T(8,128)(2,1)S(1)}, bf16[2,384,384]{2,1,0:T(8,128)(2,1)}, u32[]{:S(2)}) copy-start(bf16[2,384,384]{2,1,0:T(8,128)(2,1)} %mlp_in_ref.1) | copy-start | bytes 1769476
  36.0 34.3 %copy-start.5 = (bf16[48,128]{1,0:T(8,128)(2,1)S(1)}, bf16[48,128]{1,0:T(8,128)(2,1)}, u32[]{:S(2)}) copy-start(bf16[48,128]{1,0:T(8,128)(2,1)} %head_ref.1) | copy-start | bytes 36868
  36.0 34.3 %copy-start.6 = (f32[2,384]{1,0:T(2,128)S(1)}, f32[2,384]{1,0:T(2,128)}, u32[]{:S(2)}) copy-start(f32[2,384]{1,0:T(2,128)} %gain_fm_ref.1) | copy-start | bytes 9220
  36.0 34.3 %copy-start.7 = (f32[2,128]{1,0:T(2,128)S(1)}, f32[2,128]{1,0:T(2,128)}, u32[]{:S(2)}) copy-start(f32[2,128]{1,0:T(2,128)} %gain_out_ref.1) | copy-start | bytes 3076
  36.0 34.3 %copy-start.8 = (f32[16]{0:T(128)S(1)}, f32[16]{0:T(128)}, u32[]{:S(2)}) copy-start(f32[16]{0:T(128)} %param.14) | copy-start | bytes 196
  105.3 8.8 %collective-permute-start.4 = (bf16[8,128,128]{2,1,0:T(8,128)(2,1)S(1)}, bf16[8,128,128]{2,1,0:T(8,128)(2,1)S(1)}, u32[]{:S(2)}, u32[]{:S(2)}) collective-permute-start(bf16[8,128,128]{2,1,0:T(8,128)(2,1)S(1)} %shard_map.128), channel_id=1, source_target_pairs={{0,64},{64,0},{1,65},{65,1},{2,66},{66,2},{3,67},{67,3},{4,68},{68... | collective-permute-start | bytes 786440 | tf_op jit(solution)/shard_map/ppermute | solution.py:415
